TPU v7x, 32 devices: a whole 2x2x4 slice. The times are simulated.
32 devices in a mesh: grp: 4 (over z), seq: 8 (over y, x, core).
Axes of the slice: x: 2, y: 2, z: 4, core: 2. Of those that a mesh axis runs over, the one named last changes fastest.
Arguments:
- stream: bfloat16 [4096, 2048], P(('grp', 'seq')), may hold values from -64 to 64
- cotangent: bfloat16 [4096, 2048], P(('grp', 'seq')), may hold values from -6 to 6
- norm_gain: float32 [2048], replicated, may hold values from 0.5 to 1.5
- queries: bfloat16 [4096, 2048], P(('grp', 'seq')), may hold values from -6 to 6
- key_vectors: bfloat16 [4096, 2048], P(('grp', 'seq')), may hold values from -6 to 6
- value_vectors: bfloat16 [4096, 2048], P(('grp', 'seq')), may hold values from -6 to 6
- expert_index: int32 [32, 256], replicated, may hold values from 0 to 4095, as said below
- router_gates: float32 [32, 256], P(('grp', 'seq')), may hold values from 0.05 to 1
- gate_proj: bfloat16 [32, 2048, 768], P(('grp', 'seq')), may hold values from -0.125 to 0.125
- up_proj: bfloat16 [32, 2048, 768], P(('grp', 'seq')), may hold values from -0.125 to 0.125
- down_proj: bfloat16 [32, 768, 2048], P(('grp', 'seq')), may hold values from -0.21875 to 0.21875
Outputs:
- grad_stream: bfloat16 [4096, 2048], P(('grp', 'seq'))
- grad_queries: bfloat16 [4096, 2048], P(('grp', 'seq'))
- grad_keys: bfloat16 [4096, 2048], P(('grp', 'seq'))
- grad_values: bfloat16 [4096, 2048], P(('grp', 'seq'))
- grad_gate: bfloat16 [32, 2048, 768], P(('grp', 'seq'))
- grad_up: bfloat16 [32, 2048, 768], P(('grp', 'seq'))
- grad_down: bfloat16 [32, 768, 2048], P(('grp', 'seq'))
- grad_router: float32 [32, 256], P(('grp', 'seq'))
- grad_norm_gain: float32 [2048], replicated
Inputs may be any that keep to these rules, and one draw needn't show every extreme that they name: `expert_index`: row e holds 256 different token numbers. Of the 128 tokens numbered d * 128 to (d + 1) * 128 - 1, one expert chooses at most 16, and in every row some d has exactly 16 chosen.
All inputs are finite; a program needn't handle non-finite values.
Results may differ from a plain program's by a relative error of at most 0.024.
Values may be sent and summed in bfloat16 or wider, within the bound.
No kernel may reach another device: no remote copies, remote signals or barrier semaphores. Data moves between devices by JAX's collectives and lax.ppermute only.
A program may use at most 192 MiB of HBM per device.

v0:
```python
import math

import jax
import jax.numpy as jnp
from jax import lax
from jax.sharding import PartitionSpec as P

HEADS = 16
HEAD = 128
BLOCK = 128


EPS = 1e-06


def prefix(shard, axis, join, neutral, backward):
    count = lax.axis_size(axis)
    place = lax.axis_index(axis)
    ahead = count - 1 - place if backward else place
    gathered = lax.all_gather(shard.astype(jnp.bfloat16), axis)
    state = jnp.zeros_like(shard) + jnp.asarray(neutral, shard.dtype)

    def one(hop, state):
        source = count - 1 - hop if backward else hop
        return join(state, lax.dynamic_index_in_dim(gathered, source, 0, False).astype(shard.dtype))

    return lax.fori_loop(0, ahead, one, state)


def expert_back(rows, dy_rows, gates, w_gate, w_up, w_down):
    gate_pre = jnp.dot(rows, w_gate, preferred_element_type=jnp.float32)
    up_pre = jnp.dot(rows, w_up, preferred_element_type=jnp.float32)
    sigmoid_gate = jax.nn.sigmoid(gate_pre)
    silu_gate = gate_pre * sigmoid_gate
    hidden = (silu_gate * up_pre).astype(jnp.bfloat16)
    expert_out = jnp.dot(hidden, w_down, preferred_element_type=jnp.float32)
    grad_router = jnp.sum(dy_rows.astype(jnp.float32) * expert_out, axis=1)
    grad_out = (gates[:, None] * dy_rows.astype(jnp.float32)).astype(jnp.bfloat16)
    grad_down = jnp.dot(hidden.T, grad_out, preferred_element_type=jnp.float32).astype(jnp.bfloat16)
    grad_hidden = jnp.dot(grad_out, w_down.T, preferred_element_type=jnp.float32)
    slope = sigmoid_gate * (1.0 + gate_pre * (1.0 - sigmoid_gate))
    grad_gate_pre = (grad_hidden * up_pre * slope).astype(jnp.bfloat16)
    grad_up_pre = (grad_hidden * silu_gate).astype(jnp.bfloat16)
    grad_gate = jnp.dot(rows.T, grad_gate_pre, preferred_element_type=jnp.float32).astype(
        jnp.bfloat16
    )
    grad_up = jnp.dot(rows.T, grad_up_pre, preferred_element_type=jnp.float32).astype(jnp.bfloat16)
    grad_rows = (
        jnp.dot(grad_gate_pre, w_gate.T, preferred_element_type=jnp.float32)
        + jnp.dot(grad_up_pre, w_up.T, preferred_element_type=jnp.float32)
    ).astype(jnp.bfloat16)
    return (grad_rows, grad_gate, grad_up, grad_down, grad_router)


def add_states(earlier, later):
    return earlier + later


def body(
    stream,
    cotangent,
    norm_gain,
    queries,
    key_vectors,
    value_vectors,
    expert_index,
    router_gates,
    gate_proj,
    up_proj,
    down_proj,
):
    tok_rows, width = stream.shape
    seq_count = lax.axis_size("seq")
    grp_count = lax.axis_size("grp")
    dev_count = seq_count * grp_count
    capacity = expert_index.shape[1]
    most = 2 * capacity // dev_count
    here = lax.axis_index("grp") * seq_count + lax.axis_index("seq")
    wide_stream = stream.astype(jnp.float32)
    inverse_rms = lax.rsqrt(jnp.mean(wide_stream * wide_stream, axis=1, keepdims=True) + EPS)
    normed = wide_stream * inverse_rms
    inputs = (normed * norm_gain[None, :]).astype(jnp.bfloat16)
    source = expert_index // tok_rows
    mine = (source == here).astype(jnp.int32)
    before_mine = jnp.cumsum(mine, axis=1) - mine
    local_token = expert_index - here * tok_rows
    slot_ids = jnp.arange(most)
    matched = (mine[:, :, None] == 1) & (before_mine[:, :, None] == slot_ids[None, None, :])
    picked = jnp.sum(jnp.where(matched, local_token[:, :, None], 0), axis=1)
    filled = jnp.any(matched, axis=1)
    outgoing = jnp.concatenate([inputs[picked], cotangent[picked]], axis=1)
    incoming = lax.all_to_all(outgoing, ("grp", "seq"), split_axis=0, concat_axis=0, tiled=True)
    own_index = lax.dynamic_index_in_dim(expert_index, here, 0, keepdims=False)
    anchor = own_index // tok_rows
    positions = jnp.arange(capacity)
    earlier = jnp.sum(
        (anchor[None, :] == anchor[:, None]) & (positions[None, :] < positions[:, None]), axis=1
    )
    table = incoming.reshape(dev_count * 2 * most, width)
    flat_slot = anchor * (2 * most) + earlier
    grad_rows, grad_gate, grad_up, grad_down, grad_router = expert_back(
        table[flat_slot],
        table[flat_slot + most],
        router_gates[0],
        gate_proj[0],
        up_proj[0],
        down_proj[0],
    )
    back_rows = (
        jnp.zeros((dev_count * most, width), jnp.bfloat16)
        .at[anchor * most + earlier]
        .set(grad_rows)
    )
    returned = lax.all_to_all(
        back_rows.reshape(dev_count, most, width),
        ("grp", "seq"),
        split_axis=0,
        concat_axis=0,
        tiled=True,
    )
    returned = returned.reshape(dev_count * most, width)
    combine_table = (
        (jnp.arange(tok_rows)[:, None] == picked.reshape(-1)[None, :]) & filled.reshape(-1)[None, :]
    ).astype(jnp.bfloat16)
    grad_inputs = jnp.dot(combine_table, returned, preferred_element_type=jnp.float32)
    grad_norm_gain = lax.psum(jnp.sum(grad_inputs * normed, axis=0), ("grp", "seq"))
    grad_normed = grad_inputs * norm_gain[None, :]
    grad_wide = cotangent.astype(jnp.float32) + inverse_rms * (
        grad_normed - normed * jnp.mean(grad_normed * normed, axis=1, keepdims=True)
    )
    grad_stream = grad_wide.astype(jnp.bfloat16)
    blocks = tok_rows // BLOCK
    scale = 1.0 / math.sqrt(HEAD * tok_rows * seq_count)

    def shaped(values):
        return values.reshape(blocks, BLOCK, HEADS, HEAD)

    qq, kk, vv, gg = (
        shaped(queries),
        shaped(key_vectors),
        shaped(value_vectors),
        shaped(grad_stream),
    )
    lower = jnp.arange(BLOCK)[:, None] >= jnp.arange(BLOCK)[None, :]
    mix_a = jnp.where(
        lower, jnp.einsum("ntha,nsha->nhts", gg, vv, preferred_element_type=jnp.float32), 0.0
    ).astype(jnp.bfloat16)
    mix_b = jnp.where(
        lower, jnp.einsum("ntha,nsha->nhts", qq, kk, preferred_element_type=jnp.float32), 0.0
    ).astype(jnp.bfloat16)
    inc_state = jnp.einsum("nsha,nshb->nhab", kk, vv, preferred_element_type=jnp.float32)
    inc_grad = jnp.einsum("ntha,nthb->nhab", qq, gg, preferred_element_type=jnp.float32)
    dev_state = jnp.sum(inc_state, axis=0)
    dev_grad = jnp.sum(inc_grad, axis=0)
    before_dev = prefix(dev_state, "seq", add_states, jnp.zeros_like(dev_state), False)
    after_dev = prefix(dev_grad, "seq", add_states, jnp.zeros_like(dev_grad), True)
    prior_state = before_dev[None] + jnp.cumsum(inc_state, axis=0) - inc_state
    later_state = after_dev[None] + jnp.cumsum(inc_grad[::-1], axis=0)[::-1] - inc_grad
    high = lax.Precision.HIGHEST
    wide_grad = gg.astype(jnp.float32)
    grad_q = scale * (
        jnp.einsum("nhts,nsha->ntha", mix_a, kk, preferred_element_type=jnp.float32)
        + jnp.einsum("nthb,nhab->ntha", wide_grad, prior_state, precision=high)
    )
    grad_k = scale * (
        jnp.einsum("nhts,ntha->nsha", mix_a, qq, preferred_element_type=jnp.float32)
        + jnp.einsum("nshb,nhab->nsha", vv.astype(jnp.float32), later_state, precision=high)
    )
    grad_v = scale * (
        jnp.einsum("nhts,nthb->nshb", mix_b, gg, preferred_element_type=jnp.float32)
        + jnp.einsum("nsha,nhab->nshb", kk.astype(jnp.float32), later_state, precision=high)
    )
    grad_queries = grad_q.reshape(tok_rows, width).astype(jnp.bfloat16)
    grad_keys = grad_k.reshape(tok_rows, width).astype(jnp.bfloat16)
    grad_values = grad_v.reshape(tok_rows, width).astype(jnp.bfloat16)
    return (
        grad_stream,
        grad_queries,
        grad_keys,
        grad_values,
        grad_gate[None],
        grad_up[None],
        grad_down[None],
        grad_router[None],
        grad_norm_gain,
    )


def solution(mesh):
    in_specs = (
        P(("grp", "seq"), None),
        P(("grp", "seq"), None),
        P(),
        P(("grp", "seq"), None),
        P(("grp", "seq"), None),
        P(("grp", "seq"), None),
        P(),
        P(("grp", "seq"), None),
        P(("grp", "seq"), None, None),
        P(("grp", "seq"), None, None),
        P(("grp", "seq"), None, None),
    )
    out_specs = (
        P(("grp", "seq"), None),
        P(("grp", "seq"), None),
        P(("grp", "seq"), None),
        P(("grp", "seq"), None),
        P(("grp", "seq"), None, None),
        P(("grp", "seq"), None, None),
        P(("grp", "seq"), None, None),
        P(("grp", "seq"), None),
        P(),
    )
    return jax.shard_map(body, mesh=mesh, in_specs=in_specs, out_specs=out_specs, check_vma=False)
```

profile of v0, /device:TPU:0, one launch (start us, length us, event | category | flops | bytes accessed | tf_op | source)
XLA Modules:
  0.0 311.5 jit_solution(16139342788598652834)
XLA Ops:
  12.4 6.3 %gather_fusion.1 = bf16[512,2048]{1,0:T(8,128)(2,1)} fusion(bf16[128,2048]{1,0:T(8,128)(2,1)} %param.16, s32[1024]{0:T(1024)S(1)} %pad_clamp_fusion.2), kind=kCustom, calls=%fused_computation.1 | custom fusion | bytes 4196352 | tf_op jit(solution)/shard_map/gather | solution.py:91
  18.8 2.0 fusion.42
  20.8 6.3 %gather_fusion = bf16[512,2048]{1,0:T(8,128)(2,1)} fusion(bf16[128,2048]{1,0:T(8,128)(2,1)} %fusion.42, s32[1024]{0:T(1024)S(1)} %pad_clamp_fusion.2), kind=kCustom, calls=%fused_computation | custom fusion | bytes 4196352 | tf_op jit(solution)/shard_map/gather | solution.py:91
  27.1 4.8 %pad_maximum_fusion = bf16[32,32,2048]{2,1,0:T(8,128)(2,1)} fusion(bf16[32,16,2048]{2,1,0:T(8,128)(2,1)} %bitcast.196, bf16[32,16,2048]{2,1,0:T(8,128)(2,1)} %bitcast.197), kind=kLoop, calls=%fused_computation.7 | loop fusion | flops 8388608 | bytes 8388608 | tf_op jit(solution)/shard_map/concatenate | solution.py:91
  31.9 7.4 %all-to-all-start = ((bf16[32,32,2048]{2,1,0:T(8,128)(2,1)}), bf16[32,32,2048]{2,1,0:T(8,128)(2,1)}, u32[]{:S(2)}, u32[]{:S(2)}) async-start(bf16[32,32,2048]{2,1,0:T(8,128)(2,1)} %pad_maximum_fusion), calls=%async_computation | async-start | bytes 8388608 | tf_op jit(solution)/shard_map/all_to_all | solution.py:92
  39.6 2.7 fusion.96
  43.8 89.7 %all-to-all-done = bf16[32,32,2048]{2,1,0:T(8,128)(2,1)} async-done(((bf16[32,32,2048]{2,1,0:T(8,128)(2,1)}), bf16[32,32,2048]{2,1,0:T(8,128)(2,1)}, u32[]{:S(2)}, u32[]{:S(2)}) %all-to-all-start) | async-done | bytes 4194336 | tf_op jit(solution)/shard_map/all_to_all | solution.py:92
  133.6 6.1 %gather_fusion.3 = bf16[256,2048]{1,0:T(8,128)(2,1)} fusion(bf16[1024,2048]{1,0:T(8,128)(2,1)} %bitcast.11, s32[1024]{0:T(1024)S(1)} %pad_clamp_fusion), kind=kCustom, calls=%fused_computation.3 | custom fusion | bytes 2098176 | tf_op jit(solution)/shard_map/gather | solution.py:102
  139.6 6.1 %gather_fusion.2 = bf16[256,2048]{1,0:T(8,128)(2,1)} fusion(bf16[1024,2048]{1,0:T(8,128)(2,1)} %bitcast.11, s32[1024]{0:T(1024)S(1)} %pad_clamp_fusion.1), kind=kCustom, calls=%fused_computation.2 | custom fusion | bytes 2098176 | tf_op jit(solution)/shard_map/gather | solution.py:103
  145.7 3.3 %fusion.2 = f32[256,768]{1,0:T(8,128)S(1)} fusion(bf16[256,2048]{1,0:T(8,128)(2,1)} %gather_fusion.3, bf16[1,2048,768]{2,1,0:T(8,128)(2,1)} %param.23), kind=kOutput, calls=%fused_computation.13 | convolution fusion | flops 805306368 | bytes 4980736 | tf_op jit(solution)/shard_map/dot_general | solution.py:31
  155.2 4.4 %scatter_custom_fusion = bf16[512,2048]{1,0:T(8,128)(2,1)} fusion(s32[256]{0:T(256)} %bitcast.209, bf16[256,2048]{1,0:T(8,128)(2,1)} %fusion.21, bf16[]{:T(256)} %constant.104.clone.1), kind=kCustom, calls=%fused_computation.65 | custom fusion | bytes 2097664 | tf_op jit(solution)/shard_map/scatter | solution.py:112
  159.7 3.7 %all-to-all-start.1 = ((bf16[32,16,2048]{2,1,0:T(8,128)(2,1)}), bf16[32,16,2048]{2,1,0:T(8,128)(2,1)S(1)}, u32[]{:S(2)}, u32[]{:S(2)}) async-start(bf16[32,16,2048]{2,1,0:T(8,128)(2,1)} %bitcast.191), calls=%async_computation.1 | async-start | bytes 4194304 | tf_op jit(solution)/shard_map/all_to_all | solution.py:114
  166.0 46.2 %all-to-all-done.1 = bf16[32,16,2048]{2,1,0:T(8,128)(2,1)S(1)} async-done(((bf16[32,16,2048]{2,1,0:T(8,128)(2,1)}), bf16[32,16,2048]{2,1,0:T(8,128)(2,1)S(1)}, u32[]{:S(2)}, u32[]{:S(2)}) %all-to-all-start.1) | async-done | bytes 2097184 | tf_op jit(solution)/shard_map/all_to_all | solution.py:114
  218.1 4.0 %fusion.12 = bf16[1,2048,768]{2,1,0:T(8,128)(2,1)} fusion(bf16[256,2048]{1,0:T(8,128)(2,1)} %gather_fusion.3, bf16[256,768]{1,0:T(8,128)(2,1)S(1)} %copy-done.20), kind=kOutput, calls=%fused_computation.23 | convolution fusion | flops 806879232 | bytes 4587520 | tf_op jit(solution)/shard_map/dot_general | solution.py:44
  222.1 2.7 fusion.13
  224.8 2.8 fusion.14
  232.7 2.0 copy.100
  234.7 45.5 %psum.7 = f32[2048]{0:T(1024)} all-reduce(f32[2048]{0:T(1024)S(1)} %copy-done.25), channel_id=1, replica_groups=mesh['grp'=4,'seq'=8] {'grp','seq'}, use_global_device_ids=true, to_apply=%region_14.15 | all-reduce | flops 2048 | bytes 16384 | tf_op jit(solution)/shard_map/psum | solution.py:126
  280.2 2.7 fusion.41
  283.0 9.4 %while.23 = (s32[]{:T(128)}, f32[16,128,128]{2,1,0:T(8,128)S(1)}, s32[]{:T(128)}, bf16[8,16,128,128]{3,2,1,0:T(8,128)(2,1)}, s32[]{:T(128)}, /*index=5*/s32[]{:T(128)}, s32[]{:T(128)}, s32[]{:T(128)}) while((s32[]{:T(128)}, f32[16,128,128]{2,1,0:T(8,128)S(1)}, s32[]{:T(128)}, bf16[8,16,128,128]{3,2,1,0:T(8,128)(2,1)}, s32[]{:T(128)}, ...), condition=%wide.region_11.12_spmd, body=%wide.region_10.11_spmd.sunk | while | flops 524294 | bytes 2621583 | solution.py:27
  292.7 2.4 fusion.63
  296.4 2.2 copy.101
  298.6 4.0 %fusion.40 = bf16[16,128,128]{2,1,0:T(8,128)(2,1)} fusion(f32[16,128,128]{2,1,0:T(8,128)} %fusion.41, f32[16,128,128]{1,2,0:T(8,128)} %copy-done.3, f32[16,128,128]{1,2,0:T(8,128)} %copy-done.4, bf16[128,2048]{1,0:T(8,128)(2,1)} %param.19), kind=kOutput, calls=%fused_computation.55 | convolution fusion | flops 403963904 | bytes 4194304 | tf_op jit(solution)/shard_map/nsha,nhab->nshb/dot_general | solution.py:171
  302.6 2.0 copy.102
  (122 shorter events, 37.2 us)
Async XLA Ops:
  7.2 143.0 %copy-start = (bf16[1,2048,768]{2,1,0:T(8,128)(2,1)S(1)}, bf16[1,2048,768]{2,1,0:T(8,128)(2,1)}, u32[]{:S(2)}) copy-start(bf16[1,2048,768]{2,1,0:T(8,128)(2,1)} %param.24) | copy-start | bytes 9437188
  8.6 10.2 %copy-start.26 = (f32[128]{0:T(128)}, f32[128]{0:T(128)S(1)}, u32[]{:S(2)}) copy-start(f32[128]{0:T(128)S(1)} %add_rsqrt_fusion) | copy-start | bytes 1540
  9.4 9.4 %copy-start.24 = (pred[32,256]{1,0:T(8,128)(4,1)}, pred[32,256]{1,0:T(8,128)(4,1)S(1)}, u32[]{:S(2)}) copy-start(pred[32,256]{1,0:T(8,128)(4,1)S(1)} %get-tuple-element.154) | copy-start | bytes 24580
  12.4 6.4 %copy-start.22 = (f32[2048]{0:T(1024)S(1)}, f32[2048]{0:T(1024)}, u32[]{:S(2)}) copy-start(f32[2048]{0:T(1024)} %param.17) | copy-start | bytes 24580
  31.9 101.6 %all-to-all-start = ((bf16[32,32,2048]{2,1,0:T(8,128)(2,1)}), bf16[32,32,2048]{2,1,0:T(8,128)(2,1)}, u32[]{:S(2)}, u32[]{:S(2)}) async-start(bf16[32,32,2048]{2,1,0:T(8,128)(2,1)} %pad_maximum_fusion), calls=%async_computation | async-start | bytes 8388608 | tf_op jit(solution)/shard_map/all_to_all | solution.py:92
  39.4 177.6 %all-gather.5.cloned.1.call-start = ((), (), s32[]{:S(2)}) async-start(), calls=%async_computation.2 | async-start | bytes 4718592 | tf_op jit(solution)/shard_map/all_gather | solution.py:20
  145.7 3.4 %copy-start.15 = (bf16[256,2048]{1,0:T(8,128)(2,1)S(1)}, bf16[256,2048]{1,0:T(8,128)(2,1)}, u32[]{:S(2)}) copy-start(bf16[256,2048]{1,0:T(8,128)(2,1)} %gather_fusion.2) | copy-start | bytes 3145732
  145.7 3.5 %copy-start.28 = (bf16[1,768,2048]{2,1,0:T(8,128)(2,1)S(1)}, bf16[1,768,2048]{2,1,0:T(8,128)(2,1)}, u32[]{:S(2)}) copy-start(bf16[1,768,2048]{2,1,0:T(8,128)(2,1)} %param.25) | copy-start | bytes 9437188
  145.7 3.5 %copy-start.30 = (f32[1,256]{1,0:T(1,128)S(1)}, f32[1,256]{1,0:T(1,128)}, u32[]{:S(2)}) copy-start(f32[1,256]{1,0:T(1,128)} %param.22) | copy-start | bytes 3076
  152.2 3.0 copy-start.19
  155.2 57.0 %copy-start.5 = (bf16[128,2048]{1,0:T(8,128)(2,1)S(1)}, bf16[128,2048]{1,0:T(8,128)(2,1)}, u32[]{:S(2)}) copy-start(bf16[128,2048]{1,0:T(8,128)(2,1)} %param.15) | copy-start | bytes 1572868
  159.6 54.6 %copy-start.2 = (bf16[128,2048]{1,0:T(8,128)(2,1)S(1)}, bf16[128,2048]{1,0:T(8,128)(2,1)}, u32[]{:S(2)}) copy-start(bf16[128,2048]{1,0:T(8,128)(2,1)} %param.16) | copy-start | bytes 1572868
  159.7 52.6 %all-to-all-start.1 = ((bf16[32,16,2048]{2,1,0:T(8,128)(2,1)}), bf16[32,16,2048]{2,1,0:T(8,128)(2,1)S(1)}, u32[]{:S(2)}, u32[]{:S(2)}) async-start(bf16[32,16,2048]{2,1,0:T(8,128)(2,1)} %bitcast.191), calls=%async_computation.1 | async-start | bytes 4194304 | tf_op jit(solution)/shard_map/all_to_all | solution.py:114
  163.3 119.5 %all-gather.7.cloned.1.call-start = ((), (), s32[]{:S(2)}) async-start(), calls=%async_computation.3 | async-start | bytes 4718592 | tf_op jit(solution)/shard_map/all_gather | solution.py:20
  164.0 50.2 %copy-start.23 = (f32[2048]{0:T(1024)S(1)}, f32[2048]{0:T(1024)}, u32[]{:S(2)}) copy-start(f32[2048]{0:T(1024)} %param.17) | copy-start | bytes 24580
  164.0 50.2 %copy-start.27 = (f32[128]{0:T(128)S(1)}, f32[128]{0:T(128)}, u32[]{:S(2)}) copy-start(f32[128]{0:T(128)} %copy-done.26) | copy-start | bytes 1540
  215.7 77.0 %copy-start.3 = (f32[16,128,128]{1,2,0:T(8,128)}, f32[16,128,128]{1,2,0:T(8,128)S(1)}, u32[]{:S(2)}) copy-start(f32[16,128,128]{1,2,0:T(8,128)S(1)} %get-tuple-element.167) | copy-start | bytes 3145732
  218.1 4.0 %copy-start.18 = (bf16[256,2048]{1,0:T(8,128)(2,1)S(1)}, bf16[256,2048]{1,0:T(8,128)(2,1)}, u32[]{:S(2)}) copy-start(bf16[256,2048]{1,0:T(8,128)(2,1)} %gather_fusion.3) | copy-start | bytes 3145732
  222.1 2.7 copy-start.31
  222.1 2.7 copy-start.32
  224.8 2.8 copy-start.29
  227.6 3.0 copy-start.6
  231.1 3.6 %copy-start.25 = (f32[2048]{0:T(1024)S(1)}, f32[2048]{0:T(1024)}, u32[]{:S(2)}) copy-start(f32[2048]{0:T(1024)} %get-tuple-element.134) | copy-start | bytes 24580
  296.4 8.3 %copy-start.1 = (bf16[1,2048,768]{2,1,0:T(8,128)(2,1)S(1)}, bf16[1,2048,768]{2,1,0:T(8,128)(2,1)}, u32[]{:S(2)}) copy-start(bf16[1,2048,768]{2,1,0:T(8,128)(2,1)} %param.24) | copy-start | bytes 9437188
  (13 other events, 21.4 us)
Sparse Core Ops, SparseCore 0:
  42.7 62.7 all-gather.4
  217.0 36.6 all-gather.6
where the time goes:
time: 313 us; the launch traced here: 311 us
  waiting for transfers between devices  136 us (43%)
  blocking collectives  45.5 us (15%)
  local copies, waits for them, and re-layouts  42.1 us (13%)
  matrix products  38.3 us (12%)
  other arithmetic  23.4 us (7%)
  between operations  14.5 us (5%)
  starting transfers between devices  11.3 us (4%)
    all_to_all x1, waiting for transfers between devices, body(): lax.all_to_all(outgoing, ('grp', 'seq'), split_axis=0, concat_axis=0, til...  89.7 us
    all_to_all x1, waiting for transfers between devices, body(): lax.all_to_all(back_rows.reshape(dev_count, most, width), ('grp', 'seq'),...  46.2 us
    psum x1, blocking collectives, body(): lax.psum(jnp.sum(grad_inputs * normed, axis=0), ('grp', 'seq'))  45.5 us
    gather x2, local copies, waits for them, and re-layouts, body(): outgoing = jnp.concatenate([inputs[picked], cotangent[picked]], axis=1)  12.7 us
    unnamed x69, local copies, waits for them, and re-layouts  9.44 us
    add x7, other arithmetic, add_states(): return earlier + later  8.98 us
    all_to_all x1, starting transfers between devices, body(): lax.all_to_all(outgoing, ('grp', 'seq'), split_axis=0, concat_axis=0, til...  7.43 us
  transfers between devices with their start and end apart: 4, of which 2 were waited for; matrix products, arithmetic and copies ran while one was open for 18% of the time, Pallas kernels for 0%

commit v1 on v0

v1 whole, which is shorter than its diff:
```python
import functools
import math

import jax
import jax.numpy as jnp
from jax import lax
from jax.experimental import pallas as pl
from jax.experimental.pallas import tpu as pltpu
from jax.sharding import PartitionSpec as P

HEAD = 128
EPS = 1e-06
F32 = jnp.float32
BF16 = jnp.bfloat16
AXES = ("grp", "seq")
VMEM_LIMIT = 63 * 1024 * 1024
CHUNK = 512

NN = (((1,), (0,)), ((), ()))
NT = (((1,), (1,)), ((), ()))
TN = (((0,), (0,)), ((), ()))


def mm(a, b, dims=NN):
    return lax.dot_general(a, b, dims, preferred_element_type=F32)


def params():
    return pltpu.CompilerParams(vmem_limit_bytes=VMEM_LIMIT)


def cost(flops, moved):
    return pl.CostEstimate(flops=flops, bytes_accessed=moved, transcendentals=0)


def pack_kernel(most, here_ref, index_ref, stream_ref, cot_ref, gain_ref, out_ref, pick_ref, inv_ref, member_ref):
    step = pl.program_id(0)
    tok, width = stream_ref.shape
    cap, experts = index_ref.shape
    rows, chunk = out_ref.shape
    x_steps = width // chunk

    @pl.when(step == 0)
    def _():
        wide = stream_ref[...].astype(F32)
        inv_ref[...] = lax.rsqrt(jnp.mean(wide * wide, axis=1, keepdims=True) + EPS)
        token = lax.broadcasted_iota(jnp.int32, (cap, tok), 1) + here_ref[0] * tok
        for e in range(experts):
            same = index_ref[:, e : e + 1] == token
            member_ref[e : e + 1, :] = jnp.sum(same.astype(F32), axis=0, keepdims=True)
        member = member_ref[...]
        before = lax.broadcasted_iota(jnp.int32, (tok, tok), 0) < lax.broadcasted_iota(jnp.int32, (tok, tok), 1)
        rank = mm(member.astype(BF16), before.astype(BF16))
        value = jnp.where(member > 0.0, rank, -1.0).astype(BF16)
        row = lax.broadcasted_iota(jnp.int32, (rows, experts), 0)
        first = lax.broadcasted_iota(jnp.int32, (rows, experts), 1) * most
        owner = (row >= first) & (row < first + most)
        spread = mm(owner.astype(BF16), value)
        place = jnp.sum(jnp.where(owner, row - first, 0), axis=1, keepdims=True)
        pick_ref[...] = (spread == place.astype(F32)).astype(BF16)

    @pl.when(step < x_steps)
    def _():
        at = pl.ds(pl.multiple_of(step * chunk, chunk), chunk)
        normed = stream_ref[:, at].astype(F32) * inv_ref[...]
        inputs = (normed * gain_ref[:, at]).astype(BF16)
        out_ref[...] = mm(pick_ref[...], inputs).astype(BF16)

    @pl.when(step >= x_steps)
    def _():
        at = pl.ds(pl.multiple_of((step - x_steps) * chunk, chunk), chunk)
        out_ref[...] = mm(pick_ref[...], cot_ref[:, at]).astype(BF16)


def pack(most, here, index_t, stream, cotangent, gain):
    tok, width = stream.shape
    cap, experts = index_t.shape
    rows = experts * most
    chunk = math.gcd(width, CHUNK)
    whole = lambda *shape: pl.BlockSpec(shape, lambda j: (0,) * len(shape))
    return pl.pallas_call(
        functools.partial(pack_kernel, most),
        grid=(2 * width // chunk,),
        in_specs=[
            pl.BlockSpec(memory_space=pltpu.SMEM),
            whole(cap, experts),
            whole(tok, width),
            whole(tok, width),
            whole(1, width),
        ],
        out_specs=[pl.BlockSpec((rows, chunk), lambda j: (0, j)), whole(rows, tok)],
        out_shape=[
            jax.ShapeDtypeStruct((rows, 2 * width), BF16),
            jax.ShapeDtypeStruct((rows, tok), BF16),
        ],
        scratch_shapes=[pltpu.VMEM((tok, 1), F32), pltpu.VMEM((experts, tok), F32)],
        compiler_params=params(),
        cost_estimate=cost(4 * rows * tok * width, 4 * rows * width),
        name="pack_rows",
    )(here, index_t, stream, cotangent, gain)


def columns(rows):
    return pl.BlockSpec((rows, CHUNK), lambda j: (0, j))


def states():
    return pl.BlockSpec((CHUNK // HEAD, HEAD, HEAD), lambda j: (j, 0, 0))


def heads_of(ref):
    return [slice(h * HEAD, (h + 1) * HEAD) for h in range(ref.shape[1] // HEAD)]


def early_kernel(q_ref, k_ref, v_ref, state_ref, mix_ref):
    tok = q_ref.shape[0]
    upper = lax.broadcasted_iota(jnp.int32, (tok, tok), 0) <= lax.broadcasted_iota(jnp.int32, (tok, tok), 1)
    for h, at in enumerate(heads_of(q_ref)):
        k = k_ref[:, at]
        state_ref[h] = mm(k, v_ref[:, at], TN).astype(BF16)
        mix_ref[:, at] = jnp.where(upper, mm(k, q_ref[:, at], NT), 0.0).astype(BF16)


def early(queries, keys, values):
    tok, width = queries.shape
    return pl.pallas_call(
        early_kernel,
        grid=(width // CHUNK,),
        in_specs=[columns(tok)] * 3,
        out_specs=[states(), columns(tok)],
        out_shape=[
            jax.ShapeDtypeStruct((width // HEAD, HEAD, HEAD), BF16),
            jax.ShapeDtypeStruct((tok, width), BF16),
        ],
        compiler_params=params(),
        cost_estimate=cost(4 * tok * HEAD * width, 10 * tok * width),
        name="early_states",
    )(queries, keys, values)


def combine_kernel(
    pick_ref, gain_ref, back_hbm, stream_hbm, cot_hbm, q_hbm, grad_ref, state_ref,
    back_ref, stream_ref, cot_ref, q_ref, sems,
):
    pairs = [(stream_hbm, stream_ref), (back_hbm, back_ref), (cot_hbm, cot_ref), (q_hbm, q_ref)]
    copies = [pltpu.make_async_copy(a, b, sems.at[i]) for i, (a, b) in enumerate(pairs)]
    for copy in copies:
        copy.start()
    copies[0].wait()
    wide = stream_ref[...].astype(F32)
    inv = lax.rsqrt(jnp.mean(wide * wide, axis=1, keepdims=True) + EPS)
    normed = wide * inv
    copies[1].wait()
    grad_normed = mm(pick_ref[...], back_ref[...]) * gain_ref[...]
    mean = jnp.mean(grad_normed * normed, axis=1, keepdims=True)
    copies[2].wait()
    grad = cot_ref[...].astype(F32) + inv * (grad_normed - normed * mean)
    grad_ref[...] = grad.astype(BF16)
    copies[3].wait()
    for h, at in enumerate(heads_of(q_ref)):
        state_ref[h] = mm(q_ref[:, at], grad_ref[:, at], TN).astype(BF16)


def combine(pick_t, back, stream, cotangent, gain, queries):
    tok, width = stream.shape
    vmem = pl.BlockSpec(memory_space=pltpu.VMEM)
    hbm = pl.BlockSpec(memory_space=pl.ANY)
    return pl.pallas_call(
        combine_kernel,
        in_specs=[vmem] * 2 + [hbm] * 4,
        out_specs=[vmem] * 2,
        out_shape=[
            jax.ShapeDtypeStruct((tok, width), BF16),
            jax.ShapeDtypeStruct((width // HEAD, HEAD, HEAD), BF16),
        ],
        scratch_shapes=[pltpu.VMEM(back.shape, BF16)]
        + [pltpu.VMEM((tok, width), BF16)] * 3
        + [pltpu.SemaphoreType.DMA((4,))],
        compiler_params=params(),
        cost_estimate=cost(2 * tok * width * (back.shape[0] + HEAD), 2 * width * (back.shape[0] + 6 * tok)),
        name="combine_rows",
    )(pick_t, gain, back, stream, cotangent, queries)


def expert_kernel(
    place_ref, place_t_ref, gates_ref, in_hbm, wg_hbm, wu_hbm, wd_hbm,
    back_hbm, table_hbm, rows_hbm, ggp_hbm, gup_hbm, hid_hbm, router_ref,
    in_ref, wg_ref, wu_ref, wd_ref, back_ref, table_ref, rows_ref, ggp_ref, gup_ref, hid_ref, sems,
):
    width = wg_ref.shape[0]
    steps = width // CHUNK
    count = iter(range(sems.shape[0]))
    pieces = [slice(j * CHUNK, (j + 1) * CHUNK) for j in range(2 * steps)]

    def copy(source, target):
        made = pltpu.make_async_copy(source, target, sems.at[next(count)])
        made.start()
        return made

    arrived = [copy(in_hbm.at[:, at], in_ref.at[:, at]) for at in pieces[:steps]]
    gate_in = copy(wg_hbm, wg_ref)
    up_in = copy(wu_hbm, wu_ref)
    arrived += [copy(in_hbm.at[:, at], in_ref.at[:, at]) for at in pieces[steps:]]
    down_in = copy(wd_hbm, wd_ref)
    place = place_ref[...]
    for at, part in zip(pieces[:steps], arrived):
        part.wait()
        table_ref[:, at] = mm(place, in_ref[:, at]).astype(BF16)
    rows = table_ref[:, :width]
    gate_in.wait()
    gate_pre = mm(rows, wg_ref[...])
    up_in.wait()
    up_pre = mm(rows, wu_ref[...])
    for at, part in zip(pieces[steps:], arrived[steps:]):
        part.wait()
        table_ref[:, at] = mm(place, in_ref[:, at]).astype(BF16)
    out = [copy(table_ref, table_hbm)]
    down_in.wait()
    raw_hidden = mm(table_ref[:, width:], wd_ref[...], NT)
    gates = gates_ref[...]
    sigmoid = 1.0 / (1.0 + jnp.exp(-gate_pre))
    silu = gate_pre * sigmoid
    hidden = silu * up_pre
    grad_hidden = gates * raw_hidden
    slope = sigmoid * (1.0 + gate_pre * (1.0 - sigmoid))
    ggp_ref[...] = (grad_hidden * up_pre * slope).astype(BF16)
    gup_ref[...] = (grad_hidden * silu).astype(BF16)
    out += [copy(ggp_ref, ggp_hbm), copy(gup_ref, gup_hbm)]
    place_t = place_t_ref[...]
    for at in pieces[:steps]:
        grad = mm(ggp_ref[...], wg_ref[at, :], NT) + mm(gup_ref[...], wu_ref[at, :], NT)
        rows_ref[:, at] = grad.astype(BF16)
        back_ref[:, at] = mm(place_t, rows_ref[:, at]).astype(BF16)
        out += [copy(back_ref.at[:, at], back_hbm.at[:, at])]
    hid_ref[...] = (hidden * gates).astype(BF16)
    router_ref[...] = jnp.sum(hidden.astype(BF16).astype(F32) * raw_hidden, axis=1, keepdims=True)
    out += [copy(hid_ref, hid_hbm), copy(rows_ref, rows_hbm)]
    for part in out:
        part.wait()


def expert(place, place_t, gates, incoming, w_gate, w_up, w_down):
    cap, slots = place.shape
    width, inner = w_gate.shape
    steps = width // CHUNK
    vmem = pl.BlockSpec(memory_space=pltpu.VMEM)
    hbm = pl.BlockSpec(memory_space=pl.ANY)
    results = [(slots, width), (cap, 2 * width), (cap, width), (cap, inner), (cap, inner), (cap, inner)]
    held = [incoming.shape, w_gate.shape, w_up.shape, w_down.shape] + results
    return pl.pallas_call(
        expert_kernel,
        in_specs=[vmem] * 3 + [hbm] * 4,
        out_specs=[hbm] * 6 + [vmem],
        out_shape=[jax.ShapeDtypeStruct(shape, BF16) for shape in results] + [jax.ShapeDtypeStruct((cap, 1), F32)],
        scratch_shapes=[pltpu.VMEM(shape, BF16) for shape in held] + [pltpu.SemaphoreType.DMA((3 * steps + 8,))],
        compiler_params=params(),
        cost_estimate=cost(10 * cap * width * inner + 6 * cap * slots * width, 2 * width * (3 * inner + 3 * slots)),
        name="expert_rows",
    )(place, place_t, gates, incoming, w_gate, w_up, w_down)


def total(value):
    count = lax.axis_size("grp") * lax.axis_size("seq")
    if count & (count - 1):
        return lax.psum(value, AXES)
    for b in range(count.bit_length() - 1):
        value = value + lax.ppermute(value, AXES, [(i, i ^ (1 << b)) for i in range(count)])
    return value


def local_kernel(scale, q_ref, k_ref, v_ref, g_ref, mix_ref, prior_ref, gq_ref, pk_ref, pv_ref):
    tok = q_ref.shape[0]
    row = lax.broadcasted_iota(jnp.int32, (tok, tok), 0)
    col = lax.broadcasted_iota(jnp.int32, (tok, tok), 1)
    for h, at in enumerate(heads_of(q_ref)):
        k, v, g = k_ref[:, at], v_ref[:, at], g_ref[:, at]
        mix_a = jnp.where(row >= col, mm(g, v, NT), 0.0).astype(BF16)
        mix_t = jnp.where(row <= col, mm(v, g, NT), 0.0).astype(BF16)
        gq_ref[:, at] = (scale * (mm(mix_a, k) + mm(g, prior_ref[h], NT))).astype(BF16)
        pk_ref[:, at] = mm(mix_t, q_ref[:, at])
        pv_ref[:, at] = mm(mix_ref[:, at], g)


def local_part(scale, queries, keys, values, grad, mix, prior):
    tok, width = queries.shape
    return pl.pallas_call(
        functools.partial(local_kernel, scale),
        grid=(width // CHUNK,),
        in_specs=[columns(tok)] * 5 + [states()],
        out_specs=[columns(tok)] * 3,
        out_shape=[
            jax.ShapeDtypeStruct((tok, width), BF16),
            jax.ShapeDtypeStruct((tok, width), F32),
            jax.ShapeDtypeStruct((tok, width), F32),
        ],
        compiler_params=params(),
        cost_estimate=cost(12 * tok * HEAD * width, 22 * tok * width),
        name="local_attention",
    )(queries, keys, values, grad, mix, prior)


def last_kernel(scale, k_ref, v_ref, pk_ref, pv_ref, later_ref, gk_ref, gv_ref):
    for h, at in enumerate(heads_of(k_ref)):
        later = later_ref[h]
        gk_ref[:, at] = (scale * (pk_ref[:, at] + mm(v_ref[:, at], later, NT))).astype(BF16)
        gv_ref[:, at] = (scale * (pv_ref[:, at] + mm(k_ref[:, at], later))).astype(BF16)


def last_part(scale, keys, values, pk, pv, later):
    tok, width = keys.shape
    return pl.pallas_call(
        functools.partial(last_kernel, scale),
        grid=(width // CHUNK,),
        in_specs=[columns(tok)] * 4 + [states()],
        out_specs=[columns(tok)] * 2,
        out_shape=[jax.ShapeDtypeStruct((tok, width), BF16)] * 2,
        compiler_params=params(),
        cost_estimate=cost(4 * tok * HEAD * width, 18 * tok * width),
        name="last_attention",
    )(keys, values, pk, pv, later)


def later_states(state):
    count = lax.axis_size("seq")
    place = lax.axis_index("seq")

    def swap(value, bit):
        return lax.ppermute(value.astype(BF16), "seq", [(i, i ^ bit) for i in range(count)]).astype(F32)

    if count & (count - 1) or count < 2 or state.shape[0] % 4:
        gathered = lax.all_gather(state, "seq")
        later = (jnp.arange(count) > place)[:, None, None, None]
        return jnp.sum(jnp.where(later, gathered.astype(F32), 0.0), axis=0).astype(BF16)
    bits = [1 << b for b in range(1, count.bit_length() - 1)]
    half = state.shape[0] // 2
    quarter = half // 2
    parity = place & 1
    parts = state.reshape((2, half) + state.shape[1:])
    mine = lax.dynamic_index_in_dim(parts, parity, 0, False)
    partner = swap(lax.dynamic_index_in_dim(parts, 1 - parity, 0, False), 1)
    mine = mine.astype(F32)
    both = mine + partner
    rising_sum, falling_base = both[:quarter], both[quarter:]
    rising = jnp.zeros_like(rising_sum)
    falling = jnp.zeros_like(falling_base)
    for up, down in zip(bits, reversed(bits)):
        got_up = swap(rising_sum, up)
        got_down = swap(falling + jnp.where((place & down) == 0, 0.0, falling_base), down)
        rising = rising + jnp.where((place & up) == 0, got_up, 0.0)
        rising_sum = rising_sum + got_up
        falling = falling + got_down
    beyond = jnp.concatenate([rising, falling])
    other = swap(beyond + jnp.where(parity == 1, mine, 0.0), 1).astype(BF16)
    own = (beyond + jnp.where(parity == 0, partner, 0.0)).astype(BF16)
    return jnp.concatenate([jnp.where(parity == 0, own, other), jnp.where(parity == 0, other, own)])


def body(
    stream,
    cotangent,
    norm_gain,
    queries,
    key_vectors,
    value_vectors,
    expert_index,
    router_gates,
    gate_proj,
    up_proj,
    down_proj,
):
    tok, width = stream.shape
    seq_count = lax.axis_size("seq")
    dev_count = seq_count * lax.axis_size("grp")
    experts, capacity = expert_index.shape
    most = 2 * capacity // dev_count
    here = lax.axis_index("grp") * seq_count + lax.axis_index("seq")
    scale = 1.0 / math.sqrt(HEAD * tok * seq_count)
    gain = norm_gain[None, :]
    w_gate, w_up, w_down = gate_proj[0], up_proj[0], down_proj[0]

    here_array = here.astype(jnp.int32)[None]
    outgoing, pick = pack(most, here_array, expert_index.T, stream, cotangent, gain)
    incoming = lax.all_to_all(outgoing, AXES, split_axis=0, concat_axis=0, tiled=True)

    key_state, mix_b = early(queries, key_vectors, value_vectors)
    gathered = lax.all_gather(key_state, "seq")
    pick_t = pick.T
    own_index = lax.dynamic_index_in_dim(expert_index, here, 0, keepdims=False)
    source = own_index // tok
    ahead = (source[None, :] == source[:, None]) & (own_index[None, :] < own_index[:, None])
    slot = source * most + jnp.sum(ahead.astype(jnp.int32), axis=1)
    place = (slot[:, None] == jnp.arange(dev_count * most)[None, :]).astype(BF16)
    place_t = (slot[None, :] == jnp.arange(dev_count * most)[:, None]).astype(BF16)
    gates = router_gates.reshape(capacity, 1)
    incoming, place, place_t, gates, mix_b, pick_t = lax.optimization_barrier(
        (incoming, place, place_t, gates, mix_b, pick_t)
    )

    back, table, grad_rows, grad_gate_pre, grad_up_pre, hidden, router = expert(
        place, place_t, gates, incoming, w_gate, w_up, w_down
    )
    returned = lax.all_to_all(back, AXES, split_axis=0, concat_axis=0, tiled=True)

    rows, dy_rows = table[:, :width], table[:, width:]
    gain_total = total((jnp.sum(grad_rows.astype(F32) * rows.astype(F32), axis=0) / norm_gain)[None, :])
    grad_gate = lax.dot_general(rows, grad_gate_pre, TN, preferred_element_type=F32).astype(BF16)
    grad_up = lax.dot_general(rows, grad_up_pre, TN, preferred_element_type=F32).astype(BF16)
    grad_down = lax.dot_general(hidden, dy_rows, TN, preferred_element_type=F32).astype(BF16)
    grad_router = router.reshape(1, capacity)
    earlier = (jnp.arange(seq_count) < lax.axis_index("seq"))[:, None, None, None]
    prior = jnp.sum(jnp.where(earlier, gathered.astype(F32), 0.0), axis=0).astype(BF16)
    returned, grad_gate, grad_up, grad_down, grad_router, prior, gain_total = lax.optimization_barrier(
        (returned, grad_gate, grad_up, grad_down, grad_router, prior, gain_total)
    )

    grad_stream, grad_state = combine(pick_t, returned, stream, cotangent, gain, queries)
    later = later_states(grad_state)
    grad_queries, part_k, part_v = local_part(
        scale, queries, key_vectors, value_vectors, grad_stream, mix_b, prior
    )
    grad_keys, grad_values = last_part(scale, key_vectors, value_vectors, part_k, part_v, later)
    return (
        grad_stream,
        grad_queries,
        grad_keys,
        grad_values,
        grad_gate[None],
        grad_up[None],
        grad_down[None],
        grad_router,
        gain_total[0],
    )


def solution(mesh):
    rows = P(AXES, None)
    cube = P(AXES, None, None)
    in_specs = (rows, rows, P(), rows, rows, rows, P(), rows, cube, cube, cube)
    out_specs = (rows, rows, rows, rows, cube, cube, cube, rows, P())
    return jax.shard_map(body, mesh=mesh, in_specs=in_specs, out_specs=out_specs, check_vma=False)
```

time: 313 us -> 229 us (0.73)
  blocking collectives: 45.5 us -> 0 us
  Pallas kernels: 0 us -> 40.8 us
  local copies, waits for them, and re-layouts: 42.1 us -> 4.16 us
  matrix products: 38.3 us -> 8.1 us
  starting transfers between devices: 11.3 us -> 25.3 us
  waiting for transfers between devices: 136 us -> 123 us
  other arithmetic: 23.4 us -> 12.3 us
    all_to_all x2, waiting for transfers between devices: 136 us -> 86.8 us  [the longest x1 86.8 us: body(): lax.all_to_all(outgoing, AXES, split_axis=0, concat_axis=0, tiled=True)]
    psum x1 -> x0, blocking collectives: 45.5 us -> none  [body(): lax.psum(jnp.sum(grad_inputs * normed, axis=0), ('grp', 'seq'))]
    pallas_call x0 -> x6, Pallas kernels: none -> 40.8 us  [the longest x1 13.9 us: expert(): pl.pallas_call(expert_kernel, in_specs=[vmem] * 3 + [hbm] * 4, out_specs=...]
    ppermute x0 -> x11, waiting for transfers between devices: none -> 36.4 us  [the longest x5 26.6 us: total(): lax.ppermute(value, AXES, [(i, i ^ 1 << b) for i in range(count)])]
    dot_general x19 -> x3, matrix products: 38.3 us -> 8.1 us  [the longest x1 2.72 us: body(): lax.dot_general(rows, grad_up_pre, TN, preferred_element_type=F32)]
    gather x4 -> x0, local copies, waits for them, and re-layouts: 24.8 us -> none  [the longest x2 12.7 us: body(): outgoing = jnp.concatenate([inputs[picked], cotangent[picked]], axis=1)]
    ppermute x0 -> x11, starting transfers between devices: none -> 13.8 us  [the longest x5 8.97 us: total(): lax.ppermute(value, AXES, [(i, i ^ 1 << b) for i in range(count)])]
    unnamed x69 -> x21, local copies, waits for them, and re-layouts: 9.44 us -> 1.56 us
  transfers between devices with their start and end apart: 4 -> 14, of which waited for: 2 -> 10; matrix products, arithmetic and copies ran while one was open for 18% -> 8% of each run, Pallas kernels for 0% -> 10%
where the time goes in v1:
time: 229 us; the launch traced here: 228 us
  waiting for transfers between devices  123 us (54%)
  Pallas kernels  40.8 us (18%)
  starting transfers between devices  25.3 us (11%)
  between operations  14.3 us (6%)
  other arithmetic  12.3 us (5%)
  matrix products  8.1 us (4%)
  local copies, waits for them, and re-layouts  4.16 us (2%)
    all_to_all x1, waiting for transfers between devices, body(): lax.all_to_all(outgoing, AXES, split_axis=0, concat_axis=0, tiled=True)  86.8 us
    ppermute x5, waiting for transfers between devices, total(): lax.ppermute(value, AXES, [(i, i ^ 1 << b) for i in range(count)])  26.6 us
    pallas_call x1, Pallas kernels, expert(): pl.pallas_call(expert_kernel, in_specs=[vmem] * 3 + [hbm] * 4, out_specs=...  13.9 us
    ppermute x6, waiting for transfers between devices, swap(): lax.ppermute(value.astype(BF16), 'seq', [(i, i ^ bit) for i in range(coun...  9.79 us
    ppermute x5, starting transfers between devices, total(): lax.ppermute(value, AXES, [(i, i ^ 1 << b) for i in range(count)])  8.97 us
    pallas_call x1, Pallas kernels, pack(): pl.pallas_call(functools.partial(pack_kernel, most), grid=(2 * width // c...  8.05 us
    all_to_all x1, starting transfers between devices, body(): lax.all_to_all(outgoing, AXES, split_axis=0, concat_axis=0, tiled=True)  7.44 us
    pallas_call x1, Pallas kernels, local_part(): pl.pallas_call(functools.partial(local_kernel, scale), grid=(width // CHU...  5.93 us
  transfers between devices with their start and end apart: 14, of which 10 were waited for; matrix products, arithmetic and copies ran while one was open for 8% of the time, Pallas kernels for 10%

profile of v1, /device:TPU:0, one launch (start us, length us, event | category | flops | bytes accessed | tf_op | source)
XLA Modules:
  0.0 228.1 jit_solution(2731540717287618665)
XLA Ops:
  7.2 1.5 copy.28
  8.7 8.0 %pack_rows.1 = (bf16[512,4096]{1,0:T(8,128)(2,1)}, bf16[512,128]{1,0:T(8,128)(2,1)}) custom-call(s32[1]{0:T(128)} %bitcast.here_ref, s32[256,32]{1,0:T(8,128)} %bitcast.44, bf16[128,2048]{1,0:T(8,128)(2,1)} %stream_hbm.1, bf16[128,2048]{1,0:T(8,128)(2,1)} %cot_hbm.1, f32[1,2048]{1,0:T(1,128)} %bitcast.45), custom_call_target="tpu_custom_call" | custom-call | flops 536870912 | bytes 4194304 | tf_op jit(solution)/shard_map/pack_rows/pallas_call | solution.py:81
  16.7 7.4 %all-to-all-start = ((bf16[32,16,4096]{2,1,0:T(8,128)(2,1)}), bf16[32,16,4096]{2,1,0:T(8,128)(2,1)}, u32[]{:S(2)}, u32[]{:S(2)}) async-start(bf16[32,16,4096]{2,1,0:T(8,128)(2,1)} %bitcast.38), calls=%async_computation | async-start | bytes 8388608 | tf_op jit(solution)/shard_map/all_to_all | solution.py:383
  24.2 4.0 %early_states.1 = (bf16[16,128,128]{2,1,0:T(8,128)(2,1)}, bf16[128,2048]{1,0:T(8,128)(2,1)}) custom-call(bf16[128,2048]{1,0:T(8,128)(2,1)} %q_ref.3, bf16[128,2048]{1,0:T(8,128)(2,1)} %k_ref.5, bf16[128,2048]{1,0:T(8,128)(2,1)} %v_ref.5), custom_call_target="tpu_custom_call" | custom-call | flops 134217728 | bytes 2621440 | tf_op jit(solution)/shard_map/early_states/pallas_call | solution.py:126
  31.6 86.8 %all-to-all-done = bf16[32,16,4096]{2,1,0:T(8,128)(2,1)} async-done(((bf16[32,16,4096]{2,1,0:T(8,128)(2,1)}), bf16[32,16,4096]{2,1,0:T(8,128)(2,1)}, u32[]{:S(2)}, u32[]{:S(2)}) %all-to-all-start) | async-done | bytes 4194336 | tf_op jit(solution)/shard_map/all_to_all | solution.py:383
  119.2 13.9 %expert_rows.1 = (bf16[512,2048]{1,0:T(8,128)(2,1)}, bf16[256,4096]{1,0:T(8,128)(2,1)}, bf16[256,2048]{1,0:T(8,128)(2,1)}, bf16[256,768]{1,0:T(8,128)(2,1)}, bf1...) custom-call(bf16[256,512]{1,0:T(8,128)(2,1)} %fusion.8.place_ref, ...), custom_call_target="tpu_custom_call" | custom-call | flops 5637144576 | bytes 15728640 | tf_op jit(solution)/shard_map/expert_rows/pallas_call | solution.py:250
  133.1 4.0 %all-to-all-start.1 = ((bf16[32,16,2048]{2,1,0:T(8,128)(2,1)}), bf16[32,16,2048]{2,1,0:T(8,128)(2,1)}, u32[]{:S(2)}, u32[]{:S(2)}) async-start(bf16[32,16,2048]{2,1,0:T(8,128)(2,1)} %bitcast.39), calls=%async_computation.1 | async-start | bytes 4194304 | tf_op jit(solution)/shard_map/all_to_all | solution.py:402
  138.8 1.6 collective-permute-start.1
  140.4 4.1 %fusion.prior_ref = bf16[16,128,128]{2,1,0:T(8,128)(2,1)} fusion(bf16[8,16,128,128]{3,2,1,0:T(8,128)(2,1)} %bitcast.37, pred[8]{0:T(512)(128)(4,1)S(1)} %iota_compare_fusion.2), kind=kLoop, calls=%fused_computation.1 | loop fusion | flops 6029312 | bytes 4718600 | tf_op jit(solution)/shard_map/reduce_sum | solution.py:411
  144.5 5.8 %collective-permute-done.1 = f32[1,2048]{1,0:T(1,128)S(1)} collective-permute-done((f32[1,2048]{1,0:T(1,128)S(1)}, f32[1,2048]{1,0:T(1,128)S(1)}, u32[]{:S(2)}, u32[]{:S(2)}) %collective-permute-start.1) | collective-permute-done | bytes 8224 | tf_op jit(solution)/shard_map/ppermute | solution.py:267
  150.3 2.4 %collective-permute-start.2 = (f32[1,2048]{1,0:T(1,128)S(1)}, f32[1,2048]{1,0:T(1,128)S(1)}, u32[]{:S(2)}, u32[]{:S(2)}) collective-permute-start(f32[1,2048]{1,0:T(1,128)S(1)} %add.76), channel_id=1, source_target_pairs={{0,4},{1,5},{2,6},{3,7},{4,0},{5,1},{6,2},{7,3},{8,12},{9,13},{10,... | collective-permute-start | bytes 24584 | tf_op jit(solution)/shard_map/ppermute | solution.py:267
  152.7 2.7 %convolution_convert_fusion.2 = bf16[2048,768]{1,0:T(8,128)(2,1)} fusion(bf16[256,768]{1,0:T(8,128)(2,1)S(1)} %copy-done.5, bf16[256,4096]{1,0:T(8,128)(2,1)S(1)} %copy-done), kind=kOutput, calls=%fused_computation.4 | convolution fusion | flops 806879232 | bytes 4587520 | tf_op jit(solution)/shard_map/dot_general | solution.py:406
  156.1 2.7 %convolution_convert_fusion.1 = bf16[2048,768]{1,0:T(8,128)(2,1)} fusion(bf16[256,768]{1,0:T(8,128)(2,1)S(1)} %copy-done.4, bf16[256,4096]{1,0:T(8,128)(2,1)S(1)} %copy-done), kind=kOutput, calls=%fused_computation.3 | convolution fusion | flops 806879232 | bytes 4587520 | tf_op jit(solution)/shard_map/dot_general | solution.py:407
  158.8 13.2 %collective-permute-done.3 = f32[1,2048]{1,0:T(1,128)S(1)} collective-permute-done((f32[1,2048]{1,0:T(1,128)S(1)}, f32[1,2048]{1,0:T(1,128)S(1)}, u32[]{:S(2)}, u32[]{:S(2)}) %collective-permute-start.3) | collective-permute-done | bytes 8224 | tf_op jit(solution)/shard_map/ppermute | solution.py:267
  172.0 4.3 %collective-permute-start.4 = (f32[1,2048]{1,0:T(1,128)S(1)}, f32[1,2048]{1,0:T(1,128)S(1)}, u32[]{:S(2)}, u32[]{:S(2)}) collective-permute-start(f32[1,2048]{1,0:T(1,128)S(1)} %add.78), channel_id=1, source_target_pairs={{0,16},{1,17},{2,18},{3,19},{4,20},{5,21},{6,22},{7,23},{8,24},{9,... | collective-permute-start | bytes 24584 | tf_op jit(solution)/shard_map/ppermute | solution.py:267
  176.3 2.7 %convolution_convert_fusion = bf16[768,2048]{1,0:T(8,128)(2,1)} fusion(bf16[256,768]{1,0:T(8,128)(2,1)S(1)} %copy-done.2, bf16[256,4096]{1,0:T(8,128)(2,1)S(1)} %copy-done), kind=kOutput, calls=%fused_computation.2 | convolution fusion | flops 806879232 | bytes 4587520 | tf_op jit(solution)/shard_map/dot_general | solution.py:408
  179.6 6.5 %collective-permute-done.4 = f32[1,2048]{1,0:T(1,128)S(1)} collective-permute-done((f32[1,2048]{1,0:T(1,128)S(1)}, f32[1,2048]{1,0:T(1,128)S(1)}, u32[]{:S(2)}, u32[]{:S(2)}) %collective-permute-start.4) | collective-permute-done | bytes 8224 | tf_op jit(solution)/shard_map/ppermute | solution.py:267
  186.7 4.6 %combine_rows.1 = (bf16[128,2048]{1,0:T(8,128)(2,1)}, bf16[16,128,128]{2,1,0:T(8,128)(2,1)}) custom-call(bf16[128,512]{1,0:T(8,128)(2,1)} %bitcast.43, f32[1,2048]{1,0:T(1,128)} %bitcast.46, bf16[512,2048]{1,0:T(8,128)(2,1)} %bitcast.15.back_hbm, bf16[128,2048]{1,0:T(8,128)(2,1)} %stream_hbm.1, bf16[128,2048]{1,0:T(8,128)(2,1)} %cot_hbm.1, ...), custom_call_target="tpu_custom_call" | custom-call | flops 335544320 | bytes 5242880 | tf_op jit(solution)/shard_map/combine_rows/pallas_call | solution.py:168
  192.5 1.5 collective-permute-done.5
  197.9 2.8 %collective-permute-done.6 = bf16[4,128,128]{2,1,0:T(8,128)(2,1)S(1)} collective-permute-done((bf16[4,128,128]{2,1,0:T(8,128)(2,1)S(1)}, bf16[4,128,128]{2,1,0:T(8,128)(2,1)S(1)}, u32[]{:S(2)}, u32[]{:S(2)}) %collective-permute-start.6) | collective-permute-done | bytes 131104 | tf_op jit(solution)/shard_map/ppermute | solution.py:328
  201.8 1.4 collective-permute-start.7
  203.8 3.1 %collective-permute-done.7 = bf16[4,128,128]{2,1,0:T(8,128)(2,1)S(1)} collective-permute-done((bf16[4,128,128]{2,1,0:T(8,128)(2,1)S(1)}, bf16[4,128,128]{2,1,0:T(8,128)(2,1)S(1)}, u32[]{:S(2)}, u32[]{:S(2)}) %collective-permute-start.7) | collective-permute-done | bytes 131104 | tf_op jit(solution)/shard_map/ppermute | solution.py:328
  209.1 5.9 %local_attention.1 = (bf16[128,2048]{1,0:T(8,128)(2,1)}, f32[128,2048]{1,0:T(8,128)}, f32[128,2048]{1,0:T(8,128)}) custom-call(bf16[128,2048]{1,0:T(8,128)(2,1)} %q_ref.3, bf16[128,2048]{1,0:T(8,128)(2,1)} %k_ref.5, bf16[128,2048]{1,0:T(8,128)(2,1)} %v_ref.5, bf16[128,2048]{1,0:T(8,128)(2,1)} %get-tuple-element.31.g_ref, ...), custom_call_target="tpu_custom_call" | custom-call | flops 402653184 | bytes 5767168 | tf_op jit(solution)/shard_map/local_attention/pallas_call | solution.py:286
  217.0 4.3 %last_attention.1 = (bf16[128,2048]{1,0:T(8,128)(2,1)}, bf16[128,2048]{1,0:T(8,128)(2,1)}) custom-call(bf16[128,2048]{1,0:T(8,128)(2,1)} %k_ref.5, bf16[128,2048]{1,0:T(8,128)(2,1)} %v_ref.5, f32[128,2048]{1,0:T(8,128)} %get-tuple-element.61.pk_ref, f32[128,2048]{1,0:T(8,128)} %get-tuple-element.62.pv_ref, bf16[16,128,128]{2,1,0:T(8,128)(2,1)} %pad_maximum_fusion.1.later_ref), custom_call_target="tpu_custom_call" | custom-call | flops 134217728 | bytes 4718592 | tf_op jit(solution)/shard_map/last_attention/pallas_call | solution.py:311
  (63 shorter events, 18.6 us)
Async XLA Ops:
  16.7 11.5 %copy-start.7 = (bf16[512,128]{1,0:T(8,128)(2,1)S(1)}, bf16[512,128]{1,0:T(8,128)(2,1)}, u32[]{:S(2)}) copy-start(bf16[512,128]{1,0:T(8,128)(2,1)} %get-tuple-element.42) | copy-start | bytes 393220
  16.7 101.6 %copy-start.9 = (f32[1,256]{1,0:T(1,128)S(1)}, f32[1,256]{1,0:T(1,128)}, u32[]{:S(2)}) copy-start(f32[1,256]{1,0:T(1,128)} %param.18) | copy-start | bytes 3076
  16.7 101.6 %all-to-all-start = ((bf16[32,16,4096]{2,1,0:T(8,128)(2,1)}), bf16[32,16,4096]{2,1,0:T(8,128)(2,1)}, u32[]{:S(2)}, u32[]{:S(2)}) async-start(bf16[32,16,4096]{2,1,0:T(8,128)(2,1)} %bitcast.38), calls=%async_computation | async-start | bytes 8388608 | tf_op jit(solution)/shard_map/all_to_all | solution.py:383
  24.2 116.2 %all-gather.3.cloned.1.call-start = ((), (), s32[]{:S(2)}) async-start(), calls=%async_computation.2 | async-start | bytes 4718592 | tf_op jit(solution)/shard_map/all_gather | solution.py:386
  133.1 4.0 %copy-start = (bf16[256,4096]{1,0:T(8,128)(2,1)S(1)}, bf16[256,4096]{1,0:T(8,128)(2,1)}, u32[]{:S(2)}) copy-start(bf16[256,4096]{1,0:T(8,128)(2,1)} %get-tuple-element.49) | copy-start | bytes 6291460
  133.1 4.0 %copy-start.3 = (bf16[256,2048]{1,0:T(8,128)(2,1)S(1)}, bf16[256,2048]{1,0:T(8,128)(2,1)}, u32[]{:S(2)}) copy-start(bf16[256,2048]{1,0:T(8,128)(2,1)} %get-tuple-element.55) | copy-start | bytes 3145732
  133.1 4.4 %copy-start.8 = (f32[2048]{0:T(1024)S(1)}, f32[2048]{0:T(1024)}, u32[]{:S(2)}) copy-start(f32[2048]{0:T(1024)} %param.13) | copy-start | bytes 24580
  133.1 53.6 %all-to-all-start.1 = ((bf16[32,16,2048]{2,1,0:T(8,128)(2,1)}), bf16[32,16,2048]{2,1,0:T(8,128)(2,1)}, u32[]{:S(2)}, u32[]{:S(2)}) async-start(bf16[32,16,2048]{2,1,0:T(8,128)(2,1)} %bitcast.39), calls=%async_computation.1 | async-start | bytes 4194304 | tf_op jit(solution)/shard_map/all_to_all | solution.py:402
  137.1 15.6 %copy-start.5 = (bf16[256,768]{1,0:T(8,128)(2,1)S(1)}, bf16[256,768]{1,0:T(8,128)(2,1)}, u32[]{:S(2)}) copy-start(bf16[256,768]{1,0:T(8,128)(2,1)} %get-tuple-element.50) | copy-start | bytes 1179652
  137.5 1.2 collective-permute-start
  138.8 11.5 %collective-permute-start.1 = (f32[1,2048]{1,0:T(1,128)S(1)}, f32[1,2048]{1,0:T(1,128)S(1)}, u32[]{:S(2)}, u32[]{:S(2)}) collective-permute-start(f32[1,2048]{1,0:T(1,128)S(1)} %add.75), channel_id=1, source_target_pairs={{0,2},{1,3},{2,0},{3,1},{4,6},{5,7},{6,4},{7,5},{8,10},{9,11},{10,... | collective-permute-start | bytes 24584 | tf_op jit(solution)/shard_map/ppermute | solution.py:267
  150.3 5.1 %collective-permute-start.2 = (f32[1,2048]{1,0:T(1,128)S(1)}, f32[1,2048]{1,0:T(1,128)S(1)}, u32[]{:S(2)}, u32[]{:S(2)}) collective-permute-start(f32[1,2048]{1,0:T(1,128)S(1)} %add.76), channel_id=1, source_target_pairs={{0,4},{1,5},{2,6},{3,7},{4,0},{5,1},{6,2},{7,3},{8,12},{9,13},{10,... | collective-permute-start | bytes 24584 | tf_op jit(solution)/shard_map/ppermute | solution.py:267
  152.7 3.4 %copy-start.4 = (bf16[256,768]{1,0:T(8,128)(2,1)S(1)}, bf16[256,768]{1,0:T(8,128)(2,1)}, u32[]{:S(2)}) copy-start(bf16[256,768]{1,0:T(8,128)(2,1)} %get-tuple-element.51) | copy-start | bytes 1179652
  155.4 16.6 %collective-permute-start.3 = (f32[1,2048]{1,0:T(1,128)S(1)}, f32[1,2048]{1,0:T(1,128)S(1)}, u32[]{:S(2)}, u32[]{:S(2)}) collective-permute-start(f32[1,2048]{1,0:T(1,128)S(1)} %add.77), channel_id=1, source_target_pairs={{0,8},{1,9},{2,10},{3,11},{4,12},{5,13},{6,14},{7,15},{8,0},{9,1},... | collective-permute-start | bytes 24584 | tf_op jit(solution)/shard_map/ppermute | solution.py:267
  156.1 20.2 %copy-start.2 = (bf16[256,768]{1,0:T(8,128)(2,1)S(1)}, bf16[256,768]{1,0:T(8,128)(2,1)}, u32[]{:S(2)}) copy-start(bf16[256,768]{1,0:T(8,128)(2,1)} %get-tuple-element.52) | copy-start | bytes 1179652
  172.0 14.1 %collective-permute-start.4 = (f32[1,2048]{1,0:T(1,128)S(1)}, f32[1,2048]{1,0:T(1,128)S(1)}, u32[]{:S(2)}, u32[]{:S(2)}) collective-permute-start(f32[1,2048]{1,0:T(1,128)S(1)} %add.78), channel_id=1, source_target_pairs={{0,16},{1,17},{2,18},{3,19},{4,20},{5,21},{6,22},{7,23},{8,24},{9,... | collective-permute-start | bytes 24584 | tf_op jit(solution)/shard_map/ppermute | solution.py:267
  176.3 2.7 %copy-start.6 = (f32[256,1]{1,0:T(8,128)S(1)}, f32[256,1]{1,0:T(8,128)}, u32[]{:S(2)}) copy-start(f32[256,1]{1,0:T(8,128)} %get-tuple-element.53) | copy-start | bytes 3076
  191.4 16.9 %copy-start.1 = (bf16[16,128,128]{2,1,0:T(8,128)(2,1)S(1)}, bf16[16,128,128]{2,1,0:T(8,128)(2,1)}, u32[]{:S(2)}) copy-start(bf16[16,128,128]{2,1,0:T(8,128)(2,1)} %get-tuple-element.63) | copy-start | bytes 1572868
  192.4 1.6 collective-permute-start.5
  195.1 5.6 %collective-permute-start.6 = (bf16[4,128,128]{2,1,0:T(8,128)(2,1)S(1)}, bf16[4,128,128]{2,1,0:T(8,128)(2,1)S(1)}, u32[]{:S(2)}, u32[]{:S(2)}) collective-permute-start(bf16[4,128,128]{2,1,0:T(8,128)(2,1)S(1)} %get-tuple-element.77), channel_id=1, source_target_pairs={{0,2},{1,3},{2,0},{3,1},{4,6},{5,7},{6,4},{7,5},{8,10},{9,11},{10,... | collective-permute-start | bytes 393224 | tf_op jit(solution)/shard_map/ppermute | solution.py:328
  196.5 5.3 %collective-permute-start.8 = (bf16[4,128,128]{2,1,0:T(8,128)(2,1)S(1)}, bf16[4,128,128]{2,1,0:T(8,128)(2,1)S(1)}, u32[]{:S(2)}, u32[]{:S(2)}) collective-permute-start(bf16[4,128,128]{2,1,0:T(8,128)(2,1)S(1)} %get-tuple-element.78), channel_id=1, source_target_pairs={{0,4},{1,5},{2,6},{3,7},{4,0},{5,1},{6,2},{7,3},{8,12},{9,13},{10,... | collective-permute-start | bytes 393224 | tf_op jit(solution)/shard_map/ppermute | solution.py:328
  201.8 5.0 %collective-permute-start.7 = (bf16[4,128,128]{2,1,0:T(8,128)(2,1)S(1)}, bf16[4,128,128]{2,1,0:T(8,128)(2,1)S(1)}, u32[]{:S(2)}, u32[]{:S(2)}) collective-permute-start(bf16[4,128,128]{2,1,0:T(8,128)(2,1)S(1)} %get-tuple-element.75), channel_id=1, source_target_pairs={{0,4},{1,5},{2,6},{3,7},{4,0},{5,1},{6,2},{7,3},{8,12},{9,13},{10,... | collective-permute-start | bytes 393224 | tf_op jit(solution)/shard_map/ppermute | solution.py:328
  203.3 5.0 %collective-permute-start.9 = (bf16[4,128,128]{2,1,0:T(8,128)(2,1)S(1)}, bf16[4,128,128]{2,1,0:T(8,128)(2,1)S(1)}, u32[]{:S(2)}, u32[]{:S(2)}) collective-permute-start(bf16[4,128,128]{2,1,0:T(8,128)(2,1)S(1)} %get-tuple-element.76), channel_id=1, source_target_pairs={{0,2},{1,3},{2,0},{3,1},{4,6},{5,7},{6,4},{7,5},{8,10},{9,11},{10,... | collective-permute-start | bytes 393224 | tf_op jit(solution)/shard_map/ppermute | solution.py:328
  209.1 5.9 %collective-permute-start.10 = (bf16[8,128,128]{2,1,0:T(8,128)(2,1)}, bf16[8,128,128]{2,1,0:T(8,128)(2,1)}, u32[]{:S(2)}, u32[]{:S(2)}) collective-permute-start(bf16[8,128,128]{2,1,0:T(8,128)(2,1)} %fusion.7), channel_id=1, source_target_pairs={{0,1},{1,0},{2,3},{3,2},{4,5},{5,4},{6,7},{7,6},{8,9},{9,8},{10,11... | collective-permute-start | bytes 786440 | tf_op jit(solution)/shard_map/ppermute | solution.py:328
Sparse Core Ops, SparseCore 0:
  28.4 62.3 all-gather.2

commit v2 on v1

v2 whole, which is shorter than its diff:
```python
import functools
import math

import jax
import jax.numpy as jnp
from jax import lax
from jax.experimental import pallas as pl
from jax.experimental.pallas import tpu as pltpu
from jax.sharding import PartitionSpec as P

HEAD = 128
EPS = 1e-06
F32 = jnp.float32
BF16 = jnp.bfloat16
AXES = ("grp", "seq")
VMEM_LIMIT = 63 * 1024 * 1024
TAIL_LIMIT = 63 * 1024 * 1024
CHUNK = 512

NN = (((1,), (0,)), ((), ()))
NT = (((1,), (1,)), ((), ()))
TN = (((0,), (0,)), ((), ()))


def mm(a, b, dims=NN):
    return lax.dot_general(a, b, dims, preferred_element_type=F32)


def params(limit=VMEM_LIMIT):
    return pltpu.CompilerParams(vmem_limit_bytes=limit)


def cost(flops, moved):
    return pl.CostEstimate(flops=flops, bytes_accessed=moved, transcendentals=0)


def one_hot_slots(most, device, index, member_ref, rows, tok):
    cap, experts = index.shape
    token = (lax.broadcasted_iota(jnp.int32, (cap, tok), 1) + device * tok).astype(F32)
    for e in range(experts):
        same = index[:, e : e + 1] == token
        member_ref[e : e + 1, :] = jnp.sum(same.astype(F32), axis=0, keepdims=True)
    member = member_ref[...]
    before = lax.broadcasted_iota(jnp.int32, (tok, tok), 0) < lax.broadcasted_iota(jnp.int32, (tok, tok), 1)
    rank = mm(member.astype(BF16), before.astype(BF16))
    value = jnp.where(member > 0.0, rank, -1.0).astype(BF16)
    row = lax.broadcasted_iota(jnp.int32, (rows, experts), 0)
    first = lax.broadcasted_iota(jnp.int32, (rows, experts), 1) * most
    owner = (row >= first) & (row < first + most)
    spread = mm(owner.astype(BF16), value)
    place = jnp.sum(jnp.where(owner, row - first, 0), axis=1, keepdims=True)
    return (spread == place.astype(F32)).astype(BF16)


def pick_kernel(most, device_ref, index_ref, pick_ref, member_ref):
    index = index_ref[...].astype(F32).T
    pick_ref[...] = one_hot_slots(most, device_ref[0], index, member_ref, *pick_ref.shape)


def picks(most, tok, device, index):
    experts, cap = index.shape
    return pl.pallas_call(
        functools.partial(pick_kernel, most),
        in_specs=[pl.BlockSpec(memory_space=pltpu.SMEM), pl.BlockSpec(memory_space=pltpu.VMEM)],
        out_specs=pl.BlockSpec(memory_space=pltpu.VMEM),
        out_shape=jax.ShapeDtypeStruct((experts * most, tok), BF16),
        scratch_shapes=[pltpu.VMEM((experts, tok), F32)],
        compiler_params=params(),
        cost_estimate=cost(1, 1),
        name="pick_slots",
    )(device, index)


def send_rows(pick_ref, sources, out_hbm, out_ref, sems):
    copies = []
    width = sources[0].shape[1]
    for i, source in enumerate(sources):
        for j in range(0, width, 2 * CHUNK):
            at = slice(i * width + j, i * width + j + 2 * CHUNK)
            out_ref[:, at] = mm(pick_ref[...], source[:, j : j + 2 * CHUNK]).astype(BF16)
            copies.append(pltpu.make_async_copy(out_ref.at[:, at], out_hbm.at[:, at], sems.at[len(copies)]))
            copies[-1].start()
    return copies


def prepare_kernel(
    most, half_ref, device_ref, index_ref, gain_ref, cot_ref, stream_ref, x_ref, out_hbm, out_ref, pick_ref, member_ref, sems
):
    del half_ref
    index = index_ref[...].astype(F32).T
    pick_ref[...] = one_hot_slots(most, device_ref[0], index, member_ref, *pick_ref.shape)
    wide = stream_ref[...].astype(F32)
    inv = lax.rsqrt(jnp.mean(wide * wide, axis=1, keepdims=True) + EPS)
    x_ref[...] = (wide * inv * gain_ref[...]).astype(BF16)
    for part in send_rows(pick_ref, (x_ref, cot_ref), out_hbm, out_ref, sems):
        part.wait()


def prepare(most, side, device, index, gain, cotangent, stream):
    tok, width = stream.shape
    experts, cap = index.shape
    experts = experts // 2
    rows = experts * most
    whole = lambda *shape: pl.BlockSpec(shape, lambda j, side: (0, 0))
    return pl.pallas_call(
        functools.partial(prepare_kernel, most),
        grid_spec=pltpu.PrefetchScalarGridSpec(
            num_scalar_prefetch=1,
            grid=(1,),
            in_specs=[
                pl.BlockSpec(memory_space=pltpu.SMEM),
                pl.BlockSpec((experts, cap), lambda j, side: (side[0], 0)),
                whole(1, width),
                whole(tok, width),
                whole(tok, width),
            ],
            out_specs=[whole(tok, width), pl.BlockSpec(memory_space=pl.ANY)],
            scratch_shapes=[
                pltpu.VMEM((rows, 2 * width), BF16),
                pltpu.VMEM((rows, tok), BF16),
                pltpu.VMEM((experts, tok), F32),
                pltpu.SemaphoreType.DMA((width // CHUNK,)),
            ],
        ),
        out_shape=[jax.ShapeDtypeStruct((tok, width), BF16), jax.ShapeDtypeStruct((rows, 2 * width), BF16)],
        compiler_params=params(),
        cost_estimate=cost(1, 1),
        name="prepare_rows",
    )(side, device, index, gain, cotangent, stream)


def pack_kernel(pick_ref, x_ref, cot_ref, out_hbm, out_ref, sems):
    for part in send_rows(pick_ref, (x_ref, cot_ref), out_hbm, out_ref, sems):
        part.wait()


def pack(pick, inputs, cotangent):
    width = inputs.shape[1]
    shape = (pick.shape[0], 2 * width)
    return pl.pallas_call(
        pack_kernel,
        in_specs=[pl.BlockSpec(memory_space=pltpu.VMEM)] * 3,
        out_specs=pl.BlockSpec(memory_space=pl.ANY),
        out_shape=jax.ShapeDtypeStruct(shape, BF16),
        scratch_shapes=[pltpu.VMEM(shape, BF16), pltpu.SemaphoreType.DMA((width // CHUNK,))],
        compiler_params=params(),
        cost_estimate=cost(1, 1),
        name="pack_rows",
    )(pick, inputs, cotangent)


def columns(rows):
    return pl.BlockSpec((rows, CHUNK), lambda j: (0, j))


def states():
    return pl.BlockSpec((CHUNK // HEAD, HEAD, HEAD), lambda j: (j, 0, 0))


def heads_of(ref):
    return [slice(h * HEAD, (h + 1) * HEAD) for h in range(ref.shape[1] // HEAD)]


def early_kernel(q_ref, k_ref, v_ref, state_ref, mix_ref):
    tok = q_ref.shape[0]
    upper = lax.broadcasted_iota(jnp.int32, (tok, tok), 0) <= lax.broadcasted_iota(jnp.int32, (tok, tok), 1)
    for h, at in enumerate(heads_of(q_ref)):
        k = k_ref[:, at]
        state_ref[h] = mm(k, v_ref[:, at], TN).astype(BF16)
        mix_ref[:, at] = jnp.where(upper, mm(k, q_ref[:, at], NT), 0.0).astype(BF16)


def early(queries, keys, values):
    tok, width = queries.shape
    return pl.pallas_call(
        early_kernel,
        grid=(width // CHUNK,),
        in_specs=[columns(tok)] * 3,
        out_specs=[states(), columns(tok)],
        out_shape=[
            jax.ShapeDtypeStruct((width // HEAD, HEAD, HEAD), BF16),
            jax.ShapeDtypeStruct((tok, width), BF16),
        ],
        compiler_params=params(),
        cost_estimate=cost(1, 1),
        name="early_states",
    )(queries, keys, values)


def combine_kernel(
    parity_ref, pick_ref, gain_ref, back_hbm, stream_hbm, cot_hbm, q_hbm, grad_ref, mine_ref, other_ref,
    back_ref, stream_ref, cot_ref, q_ref, sems,
):
    pairs = [(stream_hbm, stream_ref), (back_hbm, back_ref), (cot_hbm, cot_ref), (q_hbm, q_ref)]
    copies = [pltpu.make_async_copy(a, b, sems.at[i]) for i, (a, b) in enumerate(pairs)]
    for copy in copies:
        copy.start()
    copies[0].wait()
    wide = stream_ref[...].astype(F32)
    inv = lax.rsqrt(jnp.mean(wide * wide, axis=1, keepdims=True) + EPS)
    normed = wide * inv
    copies[1].wait()
    grad_normed = mm(pick_ref[...], back_ref[...]) * gain_ref[...]
    mean = jnp.mean(grad_normed * normed, axis=1, keepdims=True)
    copies[2].wait()
    grad = cot_ref[...].astype(F32) + inv * (grad_normed - normed * mean)
    grad_ref[...] = grad.astype(BF16)
    copies[3].wait()
    half = mine_ref.shape[0]
    for state_ref, first in ((other_ref, (1 - parity_ref[0]) * half), (mine_ref, parity_ref[0] * half)):
        for h in range(half):
            at = pl.ds(pl.multiple_of((first + h) * HEAD, HEAD), HEAD)
            state_ref[h] = mm(q_ref[:, at], grad_ref[:, at], TN).astype(BF16)


def combine(parity, pick_t, back, stream, cotangent, gain, queries):
    tok, width = stream.shape
    vmem = pl.BlockSpec(memory_space=pltpu.VMEM)
    hbm = pl.BlockSpec(memory_space=pl.ANY)
    return pl.pallas_call(
        combine_kernel,
        in_specs=[pl.BlockSpec(memory_space=pltpu.SMEM)] + [vmem] * 2 + [hbm] * 4,
        out_specs=[vmem] * 3,
        out_shape=[jax.ShapeDtypeStruct((tok, width), BF16)]
        + [jax.ShapeDtypeStruct((width // HEAD // 2, HEAD, HEAD), BF16)] * 2,
        scratch_shapes=[pltpu.VMEM(back.shape, BF16)]
        + [pltpu.VMEM((tok, width), BF16)] * 3
        + [pltpu.SemaphoreType.DMA((4,))],
        compiler_params=params(),
        cost_estimate=cost(2 * tok * width * (back.shape[0] + HEAD), 2 * width * (back.shape[0] + 6 * tok)),
        name="combine_rows",
    )(parity, pick_t, gain, back, stream, cotangent, queries)


def expert_kernel(
    place_ref, place_t_ref, gates_ref, own_hbm, far_hbm, wg_hbm, wu_hbm, wd_hbm,
    back_hbm, table_hbm, rows_hbm, ggp_hbm, gup_hbm, hid_hbm, router_ref,
    in_ref, wg_ref, wu_ref, wd_ref, back_ref, table_ref, rows_ref, ggp_ref, gup_ref, hid_ref, sems,
):
    width = wg_ref.shape[0]
    steps = width // CHUNK
    count = iter(range(sems.shape[0]))
    pieces = [slice(j * CHUNK, (j + 1) * CHUNK) for j in range(2 * steps)]

    def copy(source, target):
        made = pltpu.make_async_copy(source, target, sems.at[next(count)])
        made.start()
        return made

    near = own_hbm.shape[0]

    def fetch(at):
        first = copy(own_hbm.at[:, at], in_ref.at[:near, at])
        return first, copy(far_hbm.at[:, at], in_ref.at[near:, at])

    arrived = [fetch(at) for at in pieces[:steps]]
    gate_in = copy(wg_hbm, wg_ref)
    up_in = copy(wu_hbm, wu_ref)
    arrived += [fetch(at) for at in pieces[steps:]]
    down_in = copy(wd_hbm, wd_ref)
    place = place_ref[...]
    for at, part in zip(pieces[:steps], arrived):
        part[0].wait()
        part[1].wait()
        table_ref[:, at] = mm(place, in_ref[:, at]).astype(BF16)
    rows = table_ref[:, :width]
    gate_in.wait()
    gate_pre = mm(rows, wg_ref[...])
    up_in.wait()
    up_pre = mm(rows, wu_ref[...])
    for at, part in zip(pieces[steps:], arrived[steps:]):
        part[0].wait()
        part[1].wait()
        table_ref[:, at] = mm(place, in_ref[:, at]).astype(BF16)
    out = [copy(table_ref, table_hbm)]
    down_in.wait()
    raw_hidden = mm(table_ref[:, width:], wd_ref[...], NT)
    cap = place_ref.shape[0]
    same = lax.broadcasted_iota(jnp.int32, (cap, cap), 0) == lax.broadcasted_iota(jnp.int32, (cap, cap), 1)
    gates = jnp.sum(jnp.where(same, gates_ref[...], 0.0), axis=1, keepdims=True)
    sigmoid = 1.0 / (1.0 + jnp.exp(-gate_pre))
    silu = gate_pre * sigmoid
    hidden = silu * up_pre
    grad_hidden = gates * raw_hidden
    slope = sigmoid * (1.0 + gate_pre * (1.0 - sigmoid))
    ggp_ref[...] = (grad_hidden * up_pre * slope).astype(BF16)
    gup_ref[...] = (grad_hidden * silu).astype(BF16)
    out += [copy(ggp_ref, ggp_hbm), copy(gup_ref, gup_hbm)]
    place_t = place_t_ref[...]
    for at in pieces[:steps]:
        grad = mm(ggp_ref[...], wg_ref[at, :], NT) + mm(gup_ref[...], wu_ref[at, :], NT)
        rows_ref[:, at] = grad.astype(BF16)
        back_ref[:, at] = mm(place_t, rows_ref[:, at]).astype(BF16)
        out += [copy(back_ref.at[:, at], back_hbm.at[:, at])]
    hid_ref[...] = (hidden * gates).astype(BF16)
    router = jnp.sum(hidden.astype(BF16).astype(F32) * raw_hidden, axis=1, keepdims=True)
    router_ref[...] = jnp.sum(jnp.where(same, router, 0.0), axis=0, keepdims=True)
    out += [copy(hid_ref, hid_hbm), copy(rows_ref, rows_hbm)]
    for part in out:
        part.wait()


def expert(place, place_t, gates, own, far, w_gate, w_up, w_down):
    cap, slots = place.shape
    width, inner = w_gate.shape
    steps = width // CHUNK
    vmem = pl.BlockSpec(memory_space=pltpu.VMEM)
    hbm = pl.BlockSpec(memory_space=pl.ANY)
    results = [(slots, width), (cap, 2 * width), (cap, width), (cap, inner), (cap, inner), (cap, inner)]
    held = [(slots, 2 * width), w_gate.shape, w_up.shape, w_down.shape] + results
    return pl.pallas_call(
        expert_kernel,
        in_specs=[vmem] * 3 + [hbm] * 5,
        out_specs=[hbm] * 6 + [vmem],
        out_shape=[jax.ShapeDtypeStruct(shape, BF16) for shape in results] + [jax.ShapeDtypeStruct((1, cap), F32)],
        scratch_shapes=[pltpu.VMEM(shape, BF16) for shape in held] + [pltpu.SemaphoreType.DMA((5 * steps + 8,))],
        compiler_params=params(),
        cost_estimate=cost(10 * cap * width * inner + 6 * cap * slots * width, 2 * width * (3 * inner + 3 * slots)),
        name="expert_rows",
    )(place, place_t, gates, own, far, w_gate, w_up, w_down)


def total(value):
    count = lax.axis_size("grp") * lax.axis_size("seq")
    if count & (count - 1):
        return lax.psum(value, AXES)
    for b in range(count.bit_length() - 1):
        value = value + lax.ppermute(value, AXES, [(i, i ^ (1 << b)) for i in range(count)])
    return value


def local_kernel(scale, q_ref, k_ref, v_ref, g_ref, mix_ref, prior_ref, gq_ref, pk_ref, pv_ref):
    tok = q_ref.shape[0]
    row = lax.broadcasted_iota(jnp.int32, (tok, tok), 0)
    col = lax.broadcasted_iota(jnp.int32, (tok, tok), 1)
    for h, at in enumerate(heads_of(q_ref)):
        k, v, g = k_ref[:, at], v_ref[:, at], g_ref[:, at]
        mix_a = jnp.where(row >= col, mm(g, v, NT), 0.0).astype(BF16)
        mix_t = jnp.where(row <= col, mm(v, g, NT), 0.0).astype(BF16)
        gq_ref[:, at] = (scale * (mm(mix_a, k) + mm(g, prior_ref[h], NT))).astype(BF16)
        pk_ref[:, at] = mm(mix_t, q_ref[:, at])
        pv_ref[:, at] = mm(mix_ref[:, at], g)


def local_part(scale, queries, keys, values, grad, mix, prior):
    tok, width = queries.shape
    return pl.pallas_call(
        functools.partial(local_kernel, scale),
        grid=(width // CHUNK,),
        in_specs=[columns(tok)] * 5 + [states()],
        out_specs=[columns(tok)] * 3,
        out_shape=[
            jax.ShapeDtypeStruct((tok, width), BF16),
            jax.ShapeDtypeStruct((tok, width), F32),
            jax.ShapeDtypeStruct((tok, width), F32),
        ],
        compiler_params=params(),
        cost_estimate=cost(12 * tok * HEAD * width, 22 * tok * width),
        name="local_attention",
    )(queries, keys, values, grad, mix, prior)


def last_kernel(scale, split, parity_ref, k_ref, v_ref, pk_ref, pv_ref, own_ref, add_ref, other_ref, gk_ref, gv_ref):
    parity = parity_ref[0]
    is_own = (pl.program_id(0) >= split) == (parity == 1)
    for h, at in enumerate(heads_of(k_ref)):
        own = own_ref[h] + jnp.where(parity == 0, add_ref[h], 0.0)
        later = jnp.where(is_own, own.astype(BF16), other_ref[h])
        gk_ref[:, at] = (scale * (pk_ref[:, at] + mm(v_ref[:, at], later, NT))).astype(BF16)
        gv_ref[:, at] = (scale * (pv_ref[:, at] + mm(k_ref[:, at], later))).astype(BF16)


def last_part(scale, parity, keys, values, pk, pv, own, add, other):
    tok, width = keys.shape
    split = own.shape[0] * HEAD // CHUNK
    state = pl.BlockSpec((CHUNK // HEAD, HEAD, HEAD), lambda j: (lax.rem(j, split), 0, 0))
    return pl.pallas_call(
        functools.partial(last_kernel, scale, split),
        grid=(width // CHUNK,),
        in_specs=[pl.BlockSpec(memory_space=pltpu.SMEM)] + [columns(tok)] * 4 + [state] * 3,
        out_specs=[columns(tok)] * 2,
        out_shape=[jax.ShapeDtypeStruct((tok, width), BF16)] * 2,
        compiler_params=params(TAIL_LIMIT),
        cost_estimate=cost(4 * tok * HEAD * width, 18 * tok * width),
        name="last_attention",
    )(parity, keys, values, pk, pv, own, add, other)


def later_states(mine, other, beside):
    count = lax.axis_size("seq")
    place = lax.axis_index("seq")
    parity = place & 1

    def swap(value, bit):
        return lax.ppermute(value.astype(BF16), "seq", [(i, i ^ bit) for i in range(count)])

    bits = [1 << b for b in range(1, count.bit_length() - 1)]
    quarter = mine.shape[0] // 2
    partner = swap(other, 1).astype(F32)
    mine = mine.astype(F32)
    both = mine + partner
    rising_sum, falling_base = both[:quarter], both[quarter:]
    rising = jnp.zeros_like(rising_sum)
    falling = jnp.zeros_like(falling_base)
    beside_out = []
    for up, down in zip(bits, reversed(bits)):
        got_up = swap(rising_sum, up)
        got_down = swap(falling + jnp.where((place & down) == 0, 0.0, falling_base), down)
        if beside:
            got_up, got_down, done = lax.optimization_barrier((got_up, got_down, beside.pop(0)()))
            beside_out.append(done)
        got_up, got_down = got_up.astype(F32), got_down.astype(F32)
        rising = rising + jnp.where((place & up) == 0, got_up, 0.0)
        rising_sum = rising_sum + got_up
        falling = falling + got_down
    own = jnp.concatenate([rising, falling])
    theirs = swap(own + jnp.where(parity == 1, mine, 0.0), 1)
    return own, partner, theirs, beside_out + [work() for work in beside]


def body(
    stream,
    cotangent,
    norm_gain,
    queries,
    key_vectors,
    value_vectors,
    expert_index,
    router_gates,
    gate_proj,
    up_proj,
    down_proj,
):
    tok, width = stream.shape
    seq_count = lax.axis_size("seq")
    dev_count = seq_count * lax.axis_size("grp")
    experts, capacity = expert_index.shape
    most = 2 * capacity // dev_count
    here = lax.axis_index("grp") * seq_count + lax.axis_index("seq")
    scale = 1.0 / math.sqrt(HEAD * tok * seq_count)
    gain = norm_gain[None, :]
    w_gate, w_up, w_down = gate_proj[0], up_proj[0], down_proj[0]

    halves = dev_count // 2
    swap = [(i, (i + halves) % dev_count) for i in range(dev_count)]
    groups = [[side * halves + i for i in range(halves)] for side in range(2)]
    side = here // halves
    side_array = side.astype(jnp.int32)[None]
    parity = (lax.axis_index("seq") & 1).astype(jnp.int32)[None]
    here_array = here.astype(jnp.int32)[None]
    there_array = ((here + halves) % dev_count).astype(jnp.int32)[None]

    def exchange(value):
        return lax.all_to_all(value, AXES, split_axis=0, concat_axis=0, tiled=True, axis_index_groups=groups)

    inputs, out_own = prepare(most, side_array, here_array, expert_index, gain, cotangent, stream)
    own = exchange(out_own)
    far_cot = lax.ppermute(cotangent, AXES, swap)
    far_inputs = lax.ppermute(inputs, AXES, swap)

    key_state, mix_b = early(queries, key_vectors, value_vectors)
    gathered = lax.all_gather(key_state, "seq")
    pick_t = picks(most, tok, here_array, expert_index).T
    half_index = lax.dynamic_slice_in_dim(expert_index, side * (experts // 2), experts // 2, 0)
    far_pick = picks(most, tok, there_array, half_index)
    own_index = lax.dynamic_index_in_dim(expert_index, here, 0, keepdims=False)
    source = own_index // tok
    ahead = (source[None, :] == source[:, None]) & (own_index[None, :] < own_index[:, None])
    before = jnp.sum(ahead.astype(jnp.int32), axis=1)
    slot = source * most + before
    arrival = jnp.where(source // halves == side, source % halves, halves + source % halves) * most + before
    place = (arrival[:, None] == jnp.arange(dev_count * most)[None, :]).astype(BF16)
    place_t = (slot[None, :] == jnp.arange(dev_count * most)[:, None]).astype(BF16)
    far_cot, far_inputs, own, place, place_t, mix_b, pick_t, far_pick = lax.optimization_barrier(
        (far_cot, far_inputs, own, place, place_t, mix_b, pick_t, far_pick)
    )
    far = exchange(pack(far_pick, far_inputs, far_cot))

    back, table, grad_rows, grad_gate_pre, grad_up_pre, hidden, router = expert(
        place, place_t, router_gates, own, far, w_gate, w_up, w_down
    )
    returned = lax.all_to_all(back, AXES, split_axis=0, concat_axis=0, tiled=True)

    rows, dy_rows = table[:, :width], table[:, width:]
    gain_total = total((jnp.sum(grad_rows.astype(F32) * rows.astype(F32), axis=0) / norm_gain)[None, :])
    grad_gate = lax.dot_general(rows, grad_gate_pre, TN, preferred_element_type=F32).astype(BF16)
    grad_up = lax.dot_general(rows, grad_up_pre, TN, preferred_element_type=F32).astype(BF16)
    grad_down = lax.dot_general(hidden, dy_rows, TN, preferred_element_type=F32).astype(BF16)
    earlier = (jnp.arange(seq_count) < lax.axis_index("seq"))[:, None, None, None]
    prior = jnp.sum(jnp.where(earlier, gathered.astype(F32), 0.0), axis=0).astype(BF16)
    returned, grad_gate, grad_up, grad_down, router, prior, gain_total = lax.optimization_barrier(
        (returned, grad_gate, grad_up, grad_down, router, prior, gain_total)
    )

    grad_stream, mine, other = combine(parity, pick_t, returned, stream, cotangent, gain, queries)
    local = lambda: local_part(scale, queries, key_vectors, value_vectors, grad_stream, mix_b, prior)
    own_state, add_state, other_state, (done,) = later_states(mine, other, [local])
    grad_queries, part_k, part_v = done
    grad_keys, grad_values = last_part(
        scale, parity, key_vectors, value_vectors, part_k, part_v, own_state, add_state, other_state
    )
    return (
        grad_stream,
        grad_queries,
        grad_keys,
        grad_values,
        grad_gate[None],
        grad_up[None],
        grad_down[None],
        router,
        gain_total[0],
    )


def solution(mesh):
    rows = P(AXES, None)
    cube = P(AXES, None, None)
    in_specs = (rows, rows, P(), rows, rows, rows, P(), rows, cube, cube, cube)
    out_specs = (rows, rows, rows, rows, cube, cube, cube, rows, P())
    return jax.shard_map(body, mesh=mesh, in_specs=in_specs, out_specs=out_specs, check_vma=False)
```

time: 229 us -> 213 us (0.930)
  waiting for transfers between devices: 123 us -> 66.4 us
  blocking collectives: 0 us -> 34.7 us
  Pallas kernels: 40.8 us -> 46.4 us
    all_to_all x1, waiting for transfers between devices: 86.8 us -> 1.78 us  [exchange(): lax.all_to_all(value, AXES, split_axis=0, concat_axis=0, tiled=True, axis...]
    all_to_all x0 -> x1, blocking collectives: none -> 34.7 us  [exchange(): lax.all_to_all(value, AXES, split_axis=0, concat_axis=0, tiled=True, axis...]
    ppermute x0 -> x2, waiting for transfers between devices: none -> 31.6 us  [the longest x1 20.5 us: body(): far_cot = lax.ppermute(cotangent, AXES, swap)]
    pallas_call x4 -> x7, Pallas kernels: 30.9 us -> 36.5 us  [the longest x1 13.9 us: expert(): pl.pallas_call(expert_kernel, in_specs=[vmem] * 3 + [hbm] * 5, out_specs=...]
    ppermute x6, waiting for transfers between devices: 9.79 us -> 5.92 us  [swap(): lax.ppermute(value.astype(BF16), 'seq', [(i, i ^ bit) for i in range(coun...]
    ppermute x0 -> x2, starting transfers between devices: none -> 3.05 us  [the longest x1 2.65 us: body(): far_cot = lax.ppermute(cotangent, AXES, swap)]
  transfers between devices with their start and end apart: 14 -> 16, of which waited for: 10 -> 10; matrix products, arithmetic and copies ran while one was open for 8% -> 9% of each run, Pallas kernels for 10% -> 15%
where the time goes in v2:
time: 213 us
  waiting for transfers between devices  66.4 us (31%)
  Pallas kernels  46.4 us (22%)
  blocking collectives  34.7 us (16%)
  starting transfers between devices  26.8 us (13%)
  between operations  14.3 us (7%)
  other arithmetic  12.4 us (6%)
  matrix products  8.11 us (4%)
  local copies, waits for them, and re-layouts  3.34 us (2%)
    all_to_all x1, blocking collectives, exchange(): lax.all_to_all(value, AXES, split_axis=0, concat_axis=0, tiled=True, axis...  34.7 us
    ppermute x5, waiting for transfers between devices, total(): lax.ppermute(value, AXES, [(i, i ^ 1 << b) for i in range(count)])  27 us
    ppermute x1, waiting for transfers between devices, body(): far_cot = lax.ppermute(cotangent, AXES, swap)  20.5 us
    pallas_call x1, Pallas kernels, expert(): pl.pallas_call(expert_kernel, in_specs=[vmem] * 3 + [hbm] * 5, out_specs=...  13.9 us
    ppermute x1, waiting for transfers between devices, body(): far_inputs = lax.ppermute(inputs, AXES, swap)  11.2 us
    ppermute x5, starting transfers between devices, total(): lax.ppermute(value, AXES, [(i, i ^ 1 << b) for i in range(count)])  9.08 us
    all_to_all x1, starting transfers between devices, exchange(): lax.all_to_all(value, AXES, split_axis=0, concat_axis=0, tiled=True, axis...  6.48 us
    ppermute x6, waiting for transfers between devices, swap(): lax.ppermute(value.astype(BF16), 'seq', [(i, i ^ bit) for i in range(coun...  5.92 us
  transfers between devices with their start and end apart: 16, of which 10 were waited for; matrix products, arithmetic and copies ran while one was open for 9% of the time, Pallas kernels for 15%

profile of v2, /device:TPU:0, one launch (start us, length us, event | category | flops | bytes accessed | tf_op | source)
XLA Modules:
  0.0 212.6 jit_solution(5659112778259515761)
XLA Ops:
  7.2 4.9 %prepare_rows.1 = (bf16[128,2048]{1,0:T(8,128)(2,1)}, bf16[256,4096]{1,0:T(8,128)(2,1)}) custom-call(s32[1]{0:T(128)} %bitcast.1.half_ref, s32[1]{0:T(128)} %bitcast.2.device_ref, s32[32,256]{1,0:T(8,128)} %index_ref.3, f32[1,2048]{1,0:T(1,128)} %bitcast.38, bf16[128,2048]{1,0:T(8,128)(2,1)} %cot_hbm.1, bf16[128,2048]{1,0:T(8,128)(2,1)} %stream_hbm.1), custom_call_target="tpu_custom_call" | custom-call | flops 1 | bytes 1 | tf_op jit(solution)/shard_map/prepare_rows/pallas_call | solution.py:105
  12.1 6.5 %all-to-all-start = ((bf16[16,16,4096]{2,1,0:T(8,128)(2,1)}), bf16[16,16,4096]{2,1,0:T(8,128)(2,1)}, u32[]{:S(2)}, u32[]{:S(2)}) async-start(bf16[16,16,4096]{2,1,0:T(8,128)(2,1)} %bitcast.34), calls=%async_computation | async-start | bytes 4194304 | tf_op jit(solution)/shard_map/all_to_all | solution.py:454
  18.7 2.7 %collective-permute-start = (bf16[128,2048]{1,0:T(8,128)(2,1)S(1)}, bf16[128,2048]{1,0:T(8,128)(2,1)}, u32[]{:S(2)}, u32[]{:S(2)}) collective-permute-start(bf16[128,2048]{1,0:T(8,128)(2,1)S(1)} %copy-done.1), channel_id=1, source_target_pairs={{0,16},{1,17},{2,18},{3,19},{4,20},{5,21},{6,22},{7,23},{8,24},{9,... | collective-permute-start | bytes 1572872 | tf_op jit(solution)/shard_map/ppermute | solution.py:458
  21.3 4.0 %early_states.1 = (bf16[16,128,128]{2,1,0:T(8,128)(2,1)}, bf16[128,2048]{1,0:T(8,128)(2,1)}) custom-call(bf16[128,2048]{1,0:T(8,128)(2,1)} %q_ref.3, bf16[128,2048]{1,0:T(8,128)(2,1)} %k_ref.5, bf16[128,2048]{1,0:T(8,128)(2,1)} %v_ref.5), custom_call_target="tpu_custom_call" | custom-call | flops 1 | bytes 1 | tf_op jit(solution)/shard_map/early_states/pallas_call | solution.py:175
  27.5 3.1 %pick_slots.2 = bf16[512,128]{1,0:T(8,128)(2,1)} custom-call(s32[1]{0:T(128)} %bitcast.2.device_ref, s32[32,256]{1,0:T(8,128)} %index_ref.3), custom_call_target="tpu_custom_call" | custom-call | flops 1 | bytes 1 | tf_op jit(solution)/shard_map/pick_slots/pallas_call | solution.py:62
  35.4 20.5 %collective-permute-done.cot_ref = bf16[128,2048]{1,0:T(8,128)(2,1)} collective-permute-done((bf16[128,2048]{1,0:T(8,128)(2,1)S(1)}, bf16[128,2048]{1,0:T(8,128)(2,1)}, u32[]{:S(2)}, u32[]{:S(2)}) %collective-permute-start) | collective-permute-done | bytes 524320 | tf_op jit(solution)/shard_map/ppermute | solution.py:458
  55.9 11.2 %collective-permute-done.1.x_ref = bf16[128,2048]{1,0:T(8,128)(2,1)} collective-permute-done((bf16[128,2048]{1,0:T(8,128)(2,1)}, bf16[128,2048]{1,0:T(8,128)(2,1)}, u32[]{:S(2)}, u32[]{:S(2)}) %collective-permute-start.1) | collective-permute-done | bytes 524320 | tf_op jit(solution)/shard_map/ppermute | solution.py:459
  68.8 2.9 %pack_rows.1 = bf16[256,4096]{1,0:T(8,128)(2,1)} custom-call(bf16[256,128]{1,0:T(8,128)(2,1)} %pick_slots.3.pick_ref, bf16[128,2048]{1,0:T(8,128)(2,1)} %collective-permute-done.1.x_ref, bf16[128,2048]{1,0:T(8,128)(2,1)} %collective-permute-done.cot_ref), custom_call_target="tpu_custom_call" | custom-call | flops 1 | bytes 1 | tf_op jit(solution)/shard_map/pack_rows/pallas_call | solution.py:140
  71.7 34.7 %all_to_all.35 = bf16[16,16,4096]{2,1,0:T(8,128)(2,1)} all-to-all(bf16[16,16,4096]{2,1,0:T(8,128)(2,1)} %bitcast.32), channel_id=1, replica_groups={{0,1,2,3,4,5,6,7,8,9,10,11,12,13,14,15},{16,17,18,19,20,21,22,23,24,25,..., dimensions={0} | all-to-all | bytes 4194304 | tf_op jit(solution)/shard_map/all_to_all | solution.py:454
  106.4 13.9 %expert_rows.1 = (bf16[512,2048]{1,0:T(8,128)(2,1)}, bf16[256,4096]{1,0:T(8,128)(2,1)}, bf16[256,2048]{1,0:T(8,128)(2,1)}, bf16[256,768]{1,0:T(8,128)(2,1)}, bf1...) custom-call(bf16[256,512]{1,0:T(8,128)(2,1)} %fusion.6.place_ref, ...), custom_call_target="tpu_custom_call" | custom-call | flops 5637144576 | bytes 15728640 | tf_op jit(solution)/shard_map/expert_rows/pallas_call | solution.py:311
  120.3 4.0 %all-to-all-start.2 = ((bf16[32,16,2048]{2,1,0:T(8,128)(2,1)}), bf16[32,16,2048]{2,1,0:T(8,128)(2,1)}, u32[]{:S(2)}, u32[]{:S(2)}) async-start(bf16[32,16,2048]{2,1,0:T(8,128)(2,1)} %bitcast.35), calls=%async_computation.2 | async-start | bytes 4194304 | tf_op jit(solution)/shard_map/all_to_all | solution.py:482
  127.7 4.1 %fusion.prior_ref = bf16[16,128,128]{2,1,0:T(8,128)(2,1)} fusion(bf16[8,16,128,128]{3,2,1,0:T(8,128)(2,1)} %bitcast.33, pred[8]{0:T(512)(128)(4,1)S(1)} %iota_compare_fusion.2), kind=kLoop, calls=%fused_computation.1 | loop fusion | flops 6029312 | bytes 4718600 | tf_op jit(solution)/shard_map/reduce_sum | solution.py:490
  131.8 5.5 %collective-permute-done.3 = f32[1,2048]{1,0:T(1,128)S(1)} collective-permute-done((f32[1,2048]{1,0:T(1,128)S(1)}, f32[1,2048]{1,0:T(1,128)S(1)}, u32[]{:S(2)}, u32[]{:S(2)}) %collective-permute-start.3) | collective-permute-done | bytes 8224 | tf_op jit(solution)/shard_map/ppermute | solution.py:328
  137.3 2.4 %collective-permute-start.4 = (f32[1,2048]{1,0:T(1,128)S(1)}, f32[1,2048]{1,0:T(1,128)S(1)}, u32[]{:S(2)}, u32[]{:S(2)}) collective-permute-start(f32[1,2048]{1,0:T(1,128)S(1)} %add.106), channel_id=1, source_target_pairs={{0,4},{1,5},{2,6},{3,7},{4,0},{5,1},{6,2},{7,3},{8,12},{9,13},{10,... | collective-permute-start | bytes 24584 | tf_op jit(solution)/shard_map/ppermute | solution.py:328
  139.8 2.7 %convolution_convert_fusion.2 = bf16[2048,768]{1,0:T(8,128)(2,1)} fusion(bf16[256,768]{1,0:T(8,128)(2,1)S(1)} %copy-done.6, bf16[256,4096]{1,0:T(8,128)(2,1)S(1)} %copy-done), kind=kOutput, calls=%fused_computation.4 | convolution fusion | flops 806879232 | bytes 4587520 | tf_op jit(solution)/shard_map/dot_general | solution.py:486
  143.2 2.7 %convolution_convert_fusion.1 = bf16[2048,768]{1,0:T(8,128)(2,1)} fusion(bf16[256,768]{1,0:T(8,128)(2,1)S(1)} %copy-done.5, bf16[256,4096]{1,0:T(8,128)(2,1)S(1)} %copy-done), kind=kOutput, calls=%fused_computation.3 | convolution fusion | flops 806879232 | bytes 4587520 | tf_op jit(solution)/shard_map/dot_general | solution.py:487
  145.9 13.0 %collective-permute-done.5 = f32[1,2048]{1,0:T(1,128)S(1)} collective-permute-done((f32[1,2048]{1,0:T(1,128)S(1)}, f32[1,2048]{1,0:T(1,128)S(1)}, u32[]{:S(2)}, u32[]{:S(2)}) %collective-permute-start.5) | collective-permute-done | bytes 8224 | tf_op jit(solution)/shard_map/ppermute | solution.py:328
  158.9 4.5 %collective-permute-start.6 = (f32[1,2048]{1,0:T(1,128)S(1)}, f32[1,2048]{1,0:T(1,128)S(1)}, u32[]{:S(2)}, u32[]{:S(2)}) collective-permute-start(f32[1,2048]{1,0:T(1,128)S(1)} %add.108), channel_id=1, source_target_pairs={{0,16},{1,17},{2,18},{3,19},{4,20},{5,21},{6,22},{7,23},{8,24},{9,... | collective-permute-start | bytes 24584 | tf_op jit(solution)/shard_map/ppermute | solution.py:328
  163.4 2.7 %convolution_convert_fusion = bf16[768,2048]{1,0:T(8,128)(2,1)} fusion(bf16[256,768]{1,0:T(8,128)(2,1)S(1)} %copy-done.2, bf16[256,4096]{1,0:T(8,128)(2,1)S(1)} %copy-done), kind=kOutput, calls=%fused_computation.2 | convolution fusion | flops 806879232 | bytes 4587520 | tf_op jit(solution)/shard_map/dot_general | solution.py:488
  166.1 7.3 %collective-permute-done.6 = f32[1,2048]{1,0:T(1,128)S(1)} collective-permute-done((f32[1,2048]{1,0:T(1,128)S(1)}, f32[1,2048]{1,0:T(1,128)S(1)}, u32[]{:S(2)}, u32[]{:S(2)}) %collective-permute-start.6) | collective-permute-done | bytes 8224 | tf_op jit(solution)/shard_map/ppermute | solution.py:328
  174.1 4.8 %combine_rows.1 = (bf16[128,2048]{1,0:T(8,128)(2,1)}, bf16[8,128,128]{2,1,0:T(8,128)(2,1)}, bf16[8,128,128]{2,1,0:T(8,128)(2,1)}) custom-call(s32[1]{0:T(128)} %bitcast.parity_ref, bf16[128,512]{1,0:T(8,128)(2,1)} %bitcast.37, f32[1,2048]{1,0:T(1,128)} %bitcast.39, bf16[512,2048]{1,0:T(8,128)(2,1)} %bitcast.18.back_hbm, bf16[128,2048]{1,0:T(8,128)(2,1)} %stream_hbm.1, ...), custom_call_target="tpu_custom_call" | custom-call | flops 335544320 | bytes 5242880 | tf_op jit(solution)/shard_map/combine_rows/pallas_call | solution.py:220
  185.0 5.9 %local_attention.1 = (bf16[128,2048]{1,0:T(8,128)(2,1)}, f32[128,2048]{1,0:T(8,128)}, f32[128,2048]{1,0:T(8,128)}) custom-call(bf16[128,2048]{1,0:T(8,128)(2,1)} %q_ref.3, bf16[128,2048]{1,0:T(8,128)(2,1)} %k_ref.5, bf16[128,2048]{1,0:T(8,128)(2,1)} %v_ref.5, bf16[128,2048]{1,0:T(8,128)(2,1)} %get-tuple-element.39.g_ref, ...), custom_call_target="tpu_custom_call" | custom-call | flops 402653184 | bytes 5767168 | tf_op jit(solution)/shard_map/local_attention/pallas_call | solution.py:347
  193.5 3.5 %collective-permute-done.10 = bf16[4,128,128]{2,1,0:T(8,128)(2,1)S(1)} collective-permute-done((bf16[4,128,128]{2,1,0:T(8,128)(2,1)S(1)}, bf16[4,128,128]{2,1,0:T(8,128)(2,1)S(1)}, u32[]{:S(2)}, u32[]{:S(2)}) %collective-permute-start.10) | collective-permute-done | bytes 131104 | tf_op jit(solution)/shard_map/ppermute | solution.py:395
  201.1 4.6 %last_attention.1 = (bf16[128,2048]{1,0:T(8,128)(2,1)}, bf16[128,2048]{1,0:T(8,128)(2,1)}) custom-call(s32[1]{0:T(128)} %bitcast.parity_ref, bf16[128,2048]{1,0:T(8,128)(2,1)} %k_ref.5, bf16[128,2048]{1,0:T(8,128)(2,1)} %v_ref.5, f32[128,2048]{1,0:T(8,128)} %get-tuple-element.76.pk_ref, f32[128,2048]{1,0:T(8,128)} %get-tuple-element.77.pv_ref, ...), custom_call_target="tpu_custom_call" | custom-call | flops 134217728 | bytes 4718592 | tf_op jit(solution)/shard_map/last_attention/pallas_call | solution.py:377
  (67 shorter events, 26.2 us)
Async XLA Ops:
  12.1 6.6 %copy-start.1 = (bf16[128,2048]{1,0:T(8,128)(2,1)S(1)}, bf16[128,2048]{1,0:T(8,128)(2,1)}, u32[]{:S(2)}) copy-start(bf16[128,2048]{1,0:T(8,128)(2,1)} %cot_hbm.1) | copy-start | bytes 1572868
  12.1 56.7 %all-to-all-start = ((bf16[16,16,4096]{2,1,0:T(8,128)(2,1)}), bf16[16,16,4096]{2,1,0:T(8,128)(2,1)}, u32[]{:S(2)}, u32[]{:S(2)}) async-start(bf16[16,16,4096]{2,1,0:T(8,128)(2,1)} %bitcast.34), calls=%async_computation | async-start | bytes 4194304 | tf_op jit(solution)/shard_map/all_to_all | solution.py:454
  18.6 7.2 %copy-start.8 = (s32[32,256]{1,0:T(8,128)S(1)}, s32[32,256]{1,0:T(8,128)}, u32[]{:S(2)}) copy-start(s32[32,256]{1,0:T(8,128)} %index_ref.3) | copy-start | bytes 98308
  18.6 109.0 %all-gather.3.cloned.1.call-start = ((), (), s32[]{:S(2)}) async-start(), calls=%async_computation.3 | async-start | bytes 4718592 | tf_op jit(solution)/shard_map/all_gather | solution.py:462
  18.7 37.2 %collective-permute-start = (bf16[128,2048]{1,0:T(8,128)(2,1)S(1)}, bf16[128,2048]{1,0:T(8,128)(2,1)}, u32[]{:S(2)}, u32[]{:S(2)}) collective-permute-start(bf16[128,2048]{1,0:T(8,128)(2,1)S(1)} %copy-done.1), channel_id=1, source_target_pairs={{0,16},{1,17},{2,18},{3,19},{4,20},{5,21},{6,22},{7,23},{8,24},{9,... | collective-permute-start | bytes 1572872 | tf_op jit(solution)/shard_map/ppermute | solution.py:458
  25.4 41.7 %collective-permute-start.1 = (bf16[128,2048]{1,0:T(8,128)(2,1)}, bf16[128,2048]{1,0:T(8,128)(2,1)}, u32[]{:S(2)}, u32[]{:S(2)}) collective-permute-start(bf16[128,2048]{1,0:T(8,128)(2,1)} %get-tuple-element.48), channel_id=1, source_target_pairs={{0,16},{1,17},{2,18},{3,19},{4,20},{5,21},{6,22},{7,23},{8,24},{9,... | collective-permute-start | bytes 1572872 | tf_op jit(solution)/shard_map/ppermute | solution.py:459
  120.3 4.0 %copy-start = (bf16[256,4096]{1,0:T(8,128)(2,1)S(1)}, bf16[256,4096]{1,0:T(8,128)(2,1)}, u32[]{:S(2)}) copy-start(bf16[256,4096]{1,0:T(8,128)(2,1)} %get-tuple-element.59) | copy-start | bytes 6291460
  120.3 4.0 %copy-start.3 = (bf16[256,2048]{1,0:T(8,128)(2,1)S(1)}, bf16[256,2048]{1,0:T(8,128)(2,1)}, u32[]{:S(2)}) copy-start(bf16[256,2048]{1,0:T(8,128)(2,1)} %get-tuple-element.65) | copy-start | bytes 3145732
  120.3 53.8 %all-to-all-start.2 = ((bf16[32,16,2048]{2,1,0:T(8,128)(2,1)}), bf16[32,16,2048]{2,1,0:T(8,128)(2,1)}, u32[]{:S(2)}, u32[]{:S(2)}) async-start(bf16[32,16,2048]{2,1,0:T(8,128)(2,1)} %bitcast.35), calls=%async_computation.2 | async-start | bytes 4194304 | tf_op jit(solution)/shard_map/all_to_all | solution.py:482
  125.0 1.2 collective-permute-start.2
  126.2 11.1 %collective-permute-start.3 = (f32[1,2048]{1,0:T(1,128)S(1)}, f32[1,2048]{1,0:T(1,128)S(1)}, u32[]{:S(2)}, u32[]{:S(2)}) collective-permute-start(f32[1,2048]{1,0:T(1,128)S(1)} %add.105), channel_id=1, source_target_pairs={{0,2},{1,3},{2,0},{3,1},{4,6},{5,7},{6,4},{7,5},{8,10},{9,11},{10,... | collective-permute-start | bytes 24584 | tf_op jit(solution)/shard_map/ppermute | solution.py:328
  127.7 12.1 %copy-start.6 = (bf16[256,768]{1,0:T(8,128)(2,1)S(1)}, bf16[256,768]{1,0:T(8,128)(2,1)}, u32[]{:S(2)}) copy-start(bf16[256,768]{1,0:T(8,128)(2,1)} %get-tuple-element.60) | copy-start | bytes 1179652
  137.3 5.2 %collective-permute-start.4 = (f32[1,2048]{1,0:T(1,128)S(1)}, f32[1,2048]{1,0:T(1,128)S(1)}, u32[]{:S(2)}, u32[]{:S(2)}) collective-permute-start(f32[1,2048]{1,0:T(1,128)S(1)} %add.106), channel_id=1, source_target_pairs={{0,4},{1,5},{2,6},{3,7},{4,0},{5,1},{6,2},{7,3},{8,12},{9,13},{10,... | collective-permute-start | bytes 24584 | tf_op jit(solution)/shard_map/ppermute | solution.py:328
  139.8 3.4 %copy-start.5 = (bf16[256,768]{1,0:T(8,128)(2,1)S(1)}, bf16[256,768]{1,0:T(8,128)(2,1)}, u32[]{:S(2)}) copy-start(bf16[256,768]{1,0:T(8,128)(2,1)} %get-tuple-element.61) | copy-start | bytes 1179652
  142.5 16.4 %collective-permute-start.5 = (f32[1,2048]{1,0:T(1,128)S(1)}, f32[1,2048]{1,0:T(1,128)S(1)}, u32[]{:S(2)}, u32[]{:S(2)}) collective-permute-start(f32[1,2048]{1,0:T(1,128)S(1)} %add.107), channel_id=1, source_target_pairs={{0,8},{1,9},{2,10},{3,11},{4,12},{5,13},{6,14},{7,15},{8,0},{9,1},... | collective-permute-start | bytes 24584 | tf_op jit(solution)/shard_map/ppermute | solution.py:328
  143.2 20.3 %copy-start.2 = (bf16[256,768]{1,0:T(8,128)(2,1)S(1)}, bf16[256,768]{1,0:T(8,128)(2,1)}, u32[]{:S(2)}) copy-start(bf16[256,768]{1,0:T(8,128)(2,1)} %get-tuple-element.62) | copy-start | bytes 1179652
  158.9 14.6 %collective-permute-start.6 = (f32[1,2048]{1,0:T(1,128)S(1)}, f32[1,2048]{1,0:T(1,128)S(1)}, u32[]{:S(2)}, u32[]{:S(2)}) collective-permute-start(f32[1,2048]{1,0:T(1,128)S(1)} %add.108), channel_id=1, source_target_pairs={{0,16},{1,17},{2,18},{3,19},{4,20},{5,21},{6,22},{7,23},{8,24},{9,... | collective-permute-start | bytes 24584 | tf_op jit(solution)/shard_map/ppermute | solution.py:328
  178.9 1.8 collective-permute-start.7
  182.4 8.5 %collective-permute-start.9 = (bf16[4,128,128]{2,1,0:T(8,128)(2,1)}, bf16[4,128,128]{2,1,0:T(8,128)(2,1)S(1)}, u32[]{:S(2)}, u32[]{:S(2)}) collective-permute-start(bf16[4,128,128]{2,1,0:T(8,128)(2,1)} %get-tuple-element.93), channel_id=1, source_target_pairs={{0,4},{1,5},{2,6},{3,7},{4,0},{5,1},{6,2},{7,3},{8,12},{9,13},{10,... | collective-permute-start | bytes 393224 | tf_op jit(solution)/shard_map/ppermute | solution.py:395
  183.5 7.4 %collective-permute-start.8 = (bf16[4,128,128]{2,1,0:T(8,128)(2,1)}, bf16[4,128,128]{2,1,0:T(8,128)(2,1)}, u32[]{:S(2)}, u32[]{:S(2)}) collective-permute-start(bf16[4,128,128]{2,1,0:T(8,128)(2,1)} %get-tuple-element.94), channel_id=1, source_target_pairs={{0,2},{1,3},{2,0},{3,1},{4,6},{5,7},{6,4},{7,5},{8,10},{9,11},{10,... | collective-permute-start | bytes 393224 | tf_op jit(solution)/shard_map/ppermute | solution.py:395
  190.9 7.1 %copy-start.4 = (bf16[8,128,128]{2,1,0:T(8,128)(2,1)S(1)}, bf16[8,128,128]{2,1,0:T(8,128)(2,1)}, u32[]{:S(2)}) copy-start(bf16[8,128,128]{2,1,0:T(8,128)(2,1)} %get-tuple-element.68) | copy-start | bytes 786436
  191.9 5.0 %collective-permute-start.10 = (bf16[4,128,128]{2,1,0:T(8,128)(2,1)S(1)}, bf16[4,128,128]{2,1,0:T(8,128)(2,1)S(1)}, u32[]{:S(2)}, u32[]{:S(2)}) collective-permute-start(bf16[4,128,128]{2,1,0:T(8,128)(2,1)S(1)} %get-tuple-element.91), channel_id=1, source_target_pairs={{0,4},{1,5},{2,6},{3,7},{4,0},{5,1},{6,2},{7,3},{8,12},{9,13},{10,... | collective-permute-start | bytes 393224 | tf_op jit(solution)/shard_map/ppermute | solution.py:395
  192.6 5.4 %collective-permute-start.11 = (bf16[4,128,128]{2,1,0:T(8,128)(2,1)S(1)}, bf16[4,128,128]{2,1,0:T(8,128)(2,1)S(1)}, u32[]{:S(2)}, u32[]{:S(2)}) collective-permute-start(bf16[4,128,128]{2,1,0:T(8,128)(2,1)S(1)} %get-tuple-element.92), channel_id=1, source_target_pairs={{0,2},{1,3},{2,0},{3,1},{4,6},{5,7},{6,4},{7,5},{8,10},{9,11},{10,... | collective-permute-start | bytes 393224 | tf_op jit(solution)/shard_map/ppermute | solution.py:395
  198.9 1.5 collective-permute-start.12
  (2 other events, 1.4 us)
Sparse Core Ops, SparseCore 0:
  25.5 50.3 all-gather.2

commit v3 on v2

v3 whole, which is shorter than its diff:
```python
import functools
import math

import jax
import jax.numpy as jnp
from jax import lax
from jax.experimental import pallas as pl
from jax.experimental.pallas import tpu as pltpu
from jax.sharding import PartitionSpec as P

HEAD = 128
EPS = 1e-06
F32 = jnp.float32
BF16 = jnp.bfloat16
AXES = ("grp", "seq")
VMEM_LIMIT = 63 * 1024 * 1024
CHUNK = 512

NN = (((1,), (0,)), ((), ()))
NT = (((1,), (1,)), ((), ()))
TN = (((0,), (0,)), ((), ()))


def mm(a, b, dims=NN):
    return lax.dot_general(a, b, dims, preferred_element_type=F32)


def params():
    return pltpu.CompilerParams(vmem_limit_bytes=VMEM_LIMIT)


def cost(flops, moved):
    return pl.CostEstimate(flops=flops, bytes_accessed=moved, transcendentals=0)


def one_hot_slots(most, device, index, member_ref, rows, tok):
    cap, experts = index.shape
    token = (lax.broadcasted_iota(jnp.int32, (cap, tok), 1) + device * tok).astype(F32)
    for e in range(experts):
        same = index[:, e : e + 1] == token
        member_ref[e : e + 1, :] = jnp.sum(same.astype(F32), axis=0, keepdims=True)
    member = member_ref[...]
    before = lax.broadcasted_iota(jnp.int32, (tok, tok), 0) < lax.broadcasted_iota(jnp.int32, (tok, tok), 1)
    rank = mm(member.astype(BF16), before.astype(BF16))
    value = jnp.where(member > 0.0, rank, -1.0).astype(BF16)
    row = lax.broadcasted_iota(jnp.int32, (rows, experts), 0)
    first = lax.broadcasted_iota(jnp.int32, (rows, experts), 1) * most
    owner = (row >= first) & (row < first + most)
    spread = mm(owner.astype(BF16), value)
    place = jnp.sum(jnp.where(owner, row - first, 0), axis=1, keepdims=True)
    return (spread == place.astype(F32)).astype(BF16)


def pick_kernel(most, device_ref, index_ref, pick_ref, member_ref):
    index = index_ref[...].astype(F32).T
    pick_ref[...] = one_hot_slots(most, device_ref[0], index, member_ref, *pick_ref.shape)


def picks(most, tok, device, index):
    experts, cap = index.shape
    return pl.pallas_call(
        functools.partial(pick_kernel, most),
        in_specs=[pl.BlockSpec(memory_space=pltpu.SMEM), pl.BlockSpec(memory_space=pltpu.VMEM)],
        out_specs=pl.BlockSpec(memory_space=pltpu.VMEM),
        out_shape=jax.ShapeDtypeStruct((experts * most, tok), BF16),
        scratch_shapes=[pltpu.VMEM((experts, tok), F32)],
        compiler_params=params(),
        cost_estimate=cost(1, 1),
        name="pick_slots",
    )(device, index)


def send_rows(pick_ref, sources, out_hbm, out_ref, sems):
    copies = []
    width = sources[0].shape[1]
    for i, source in enumerate(sources):
        for j in range(0, width, 2 * CHUNK):
            at = slice(i * width + j, i * width + j + 2 * CHUNK)
            out_ref[:, at] = mm(pick_ref[...], source[:, j : j + 2 * CHUNK]).astype(BF16)
            copies.append(pltpu.make_async_copy(out_ref.at[:, at], out_hbm.at[:, at], sems.at[len(copies)]))
            copies[-1].start()
    return copies


def prepare_kernel(
    most, half_ref, device_ref, index_ref, gain_ref, cot_ref, stream_ref, x_ref, out_hbm, out_ref, pick_ref, member_ref, sems
):
    del half_ref
    index = index_ref[...].astype(F32).T
    pick_ref[...] = one_hot_slots(most, device_ref[0], index, member_ref, *pick_ref.shape)
    wide = stream_ref[...].astype(F32)
    inv = lax.rsqrt(jnp.mean(wide * wide, axis=1, keepdims=True) + EPS)
    x_ref[...] = (wide * inv * gain_ref[...]).astype(BF16)
    for part in send_rows(pick_ref, (x_ref, cot_ref), out_hbm, out_ref, sems):
        part.wait()


def prepare(most, side, device, index, gain, cotangent, stream):
    tok, width = stream.shape
    experts, cap = index.shape
    experts = experts // 2
    rows = experts * most
    whole = lambda *shape: pl.BlockSpec(shape, lambda j, side: (0, 0))
    return pl.pallas_call(
        functools.partial(prepare_kernel, most),
        grid_spec=pltpu.PrefetchScalarGridSpec(
            num_scalar_prefetch=1,
            grid=(1,),
            in_specs=[
                pl.BlockSpec(memory_space=pltpu.SMEM),
                pl.BlockSpec((experts, cap), lambda j, side: (side[0], 0)),
                whole(1, width),
                whole(tok, width),
                whole(tok, width),
            ],
            out_specs=[whole(tok, width), pl.BlockSpec(memory_space=pl.ANY)],
            scratch_shapes=[
                pltpu.VMEM((rows, 2 * width), BF16),
                pltpu.VMEM((rows, tok), BF16),
                pltpu.VMEM((experts, tok), F32),
                pltpu.SemaphoreType.DMA((width // CHUNK,)),
            ],
        ),
        out_shape=[jax.ShapeDtypeStruct((tok, width), BF16), jax.ShapeDtypeStruct((rows, 2 * width), BF16)],
        compiler_params=params(),
        cost_estimate=cost(1, 1),
        name="prepare_rows",
    )(side, device, index, gain, cotangent, stream)


def pack_kernel(pick_ref, x_ref, cot_ref, out_hbm, out_ref, sems):
    for part in send_rows(pick_ref, (x_ref, cot_ref), out_hbm, out_ref, sems):
        part.wait()


def pack(pick, inputs, cotangent):
    width = inputs.shape[1]
    shape = (pick.shape[0], 2 * width)
    return pl.pallas_call(
        pack_kernel,
        in_specs=[pl.BlockSpec(memory_space=pltpu.VMEM)] * 3,
        out_specs=pl.BlockSpec(memory_space=pl.ANY),
        out_shape=jax.ShapeDtypeStruct(shape, BF16),
        scratch_shapes=[pltpu.VMEM(shape, BF16), pltpu.SemaphoreType.DMA((width // CHUNK,))],
        compiler_params=params(),
        cost_estimate=cost(1, 1),
        name="pack_rows",
    )(pick, inputs, cotangent)


def streamed(work, name, scalar, ins, outs):
    width = max(x.shape[-1] for x in ins)
    steps = width // CHUNK
    group = CHUNK // HEAD

    def part(ref, j):
        if len(ref.shape) == 2:
            return ref.at[:, j * CHUNK : (j + 1) * CHUNK]
        return ref.at[j * group : (j + 1) * group]

    def kernel(*refs):
        scalar_ref, refs = refs[0], refs[1:]
        n, m = len(ins), len(outs)
        in_hbm, out_hbm, in_ref, out_ref = refs[:n], refs[n : n + m], refs[n + m : 2 * n + m], refs[2 * n + m : -1]
        count = iter(range(steps * (n + m)))

        def copy(source, target):
            made = pltpu.make_async_copy(source, target, refs[-1].at[next(count)])
            made.start()
            return made

        def used(ref):
            return [j for j in range(steps) if len(ref.shape) == 2 or j * group < ref.shape[0]]

        loads = [[] for _ in range(steps)]
        for j in range(steps):
            for a, b in zip(in_hbm, in_ref):
                if j in used(a):
                    loads[j].append(copy(part(a, j), part(b, j)))
        stores = []
        for j in range(steps):
            for load in loads[j]:
                load.wait()
            for h in range(j * group, (j + 1) * group):
                work(scalar_ref, h, slice(h * HEAD, (h + 1) * HEAD), in_ref, out_ref)
            stores += [copy(part(a, j), part(b, j)) for a, b in zip(out_ref, out_hbm) if len(a.shape) == 2]
        stores += [copy(a, b) for a, b in zip(out_ref, out_hbm) if len(a.shape) == 3]
        for store in stores:
            store.wait()

    hbm = pl.BlockSpec(memory_space=pl.ANY)
    return pl.pallas_call(
        kernel,
        in_specs=[pl.BlockSpec(memory_space=pltpu.SMEM)] + [hbm] * len(ins),
        out_specs=[hbm] * len(outs),
        out_shape=outs,
        scratch_shapes=[pltpu.VMEM(x.shape, x.dtype) for x in [*ins, *outs]]
        + [pltpu.SemaphoreType.DMA((steps * (len(ins) + len(outs)),))],
        compiler_params=params(),
        cost_estimate=cost(1, 1),
        name=name,
    )(scalar, *ins)


def triangle(tok):
    return lax.broadcasted_iota(jnp.int32, (tok, tok), 0), lax.broadcasted_iota(jnp.int32, (tok, tok), 1)


def early(parity, queries, keys, values):
    tok, width = queries.shape
    heads = width // HEAD

    def work(parity_ref, h, at, ins, outs):
        q_ref, k_ref, v_ref = ins
        state_ref, mix_ref = outs
        row, col = triangle(tok)
        k = k_ref[:, at]
        state_ref[lax.rem(h + parity_ref[0] * (heads // 2), heads)] = mm(k, v_ref[:, at], TN).astype(BF16)
        mix_ref[:, at] = jnp.where(row <= col, mm(k, q_ref[:, at], NT), 0.0).astype(BF16)

    states = jax.ShapeDtypeStruct((heads, HEAD, HEAD), BF16)
    outs = [states, jax.ShapeDtypeStruct((tok, width), BF16)]
    return streamed(work, "early_states", parity, [queries, keys, values], outs)


def combine_kernel(
    parity_ref, pick_ref, gain_ref, stream_hbm, back_hbm, cot_hbm, q_hbm, grad_hbm, mine_ref, other_ref,
    stream_ref, back_ref, cot_ref, q_ref, grad_ref, normed_ref, sum_ref, sems,
):
    width = stream_ref.shape[1]
    count = iter(range(sems.shape[0]))
    pieces = [slice(j, j + CHUNK) for j in range(0, width, CHUNK)]

    def copy(source, target):
        made = pltpu.make_async_copy(source, target, sems.at[next(count)])
        made.start()
        return made

    stream_in = copy(stream_hbm, stream_ref)
    back_in = [copy(back_hbm.at[:, at], back_ref.at[:, at]) for at in pieces]
    cot_in = copy(cot_hbm, cot_ref)
    q_in = copy(q_hbm, q_ref)
    stream_in.wait()
    wide = stream_ref[...].astype(F32)
    inv = lax.rsqrt(jnp.mean(wide * wide, axis=1, keepdims=True) + EPS)
    normed_ref[...] = wide * inv
    total = 0.0
    for part, at in zip(back_in, pieces):
        part.wait()
        grad_normed = mm(pick_ref[...], back_ref[:, at]) * gain_ref[:, at]
        sum_ref[:, at] = grad_normed
        total += jnp.sum(grad_normed * normed_ref[:, at], axis=1, keepdims=True)
    mean = total * (1.0 / width)
    cot_in.wait()
    for at in pieces:
        grad = cot_ref[:, at].astype(F32) + inv * (sum_ref[:, at] - normed_ref[:, at] * mean)
        grad_ref[:, at] = grad.astype(BF16)
    grad_out = copy(grad_ref, grad_hbm)
    q_in.wait()
    half = mine_ref.shape[0]
    for state_ref, first in ((other_ref, (1 - parity_ref[0]) * half), (mine_ref, parity_ref[0] * half)):
        for h in range(half):
            at = pl.ds(pl.multiple_of((first + h) * HEAD, HEAD), HEAD)
            state_ref[h] = mm(q_ref[:, at], grad_ref[:, at], TN).astype(BF16)
    grad_out.wait()


def combine(parity, pick_t, gain, stream, back, cotangent, queries):
    tok, width = stream.shape
    vmem = pl.BlockSpec(memory_space=pltpu.VMEM)
    hbm = pl.BlockSpec(memory_space=pl.ANY)
    return pl.pallas_call(
        combine_kernel,
        in_specs=[pl.BlockSpec(memory_space=pltpu.SMEM)] + [vmem] * 2 + [hbm] * 4,
        out_specs=[hbm] + [vmem] * 2,
        out_shape=[jax.ShapeDtypeStruct((tok, width), BF16)]
        + [jax.ShapeDtypeStruct((width // HEAD // 2, HEAD, HEAD), BF16)] * 2,
        scratch_shapes=[pltpu.VMEM((tok, width), BF16), pltpu.VMEM(back.shape, BF16)]
        + [pltpu.VMEM((tok, width), BF16)] * 3
        + [pltpu.VMEM((tok, width), F32)] * 2
        + [pltpu.SemaphoreType.DMA((width // CHUNK + 4,))],
        compiler_params=params(),
        cost_estimate=cost(2 * tok * width * (back.shape[0] + HEAD), 2 * width * (back.shape[0] + 6 * tok)),
        name="combine_rows",
    )(parity, pick_t, gain, stream, back, cotangent, queries)


def expert_kernel(
    first_ref, gates_ref, in_hbm, wg_hbm, wu_hbm, wd_hbm, _,
    back_hbm, ggp_hbm, gup_hbm, hid_hbm, router_ref, gain_ref,
    in_ref, wg_ref, wu_ref, wd_ref, back_ref, ggp_ref, gup_ref, hid_ref, sems,
):
    width = wg_ref.shape[0]
    slots = in_ref.shape[0]
    count = iter(range(sems.shape[0]))
    pieces = [slice(j, j + CHUNK) for j in range(0, width, CHUNK)]
    shifted = [slice(j, j + CHUNK) for j in range(width, 2 * width, CHUNK)]

    def copy(source, target):
        made = pltpu.make_async_copy(source, target, sems.at[next(count)])
        made.start()
        return made

    loads = []
    for at in pieces:
        loads += [copy(in_hbm.at[:, at], in_ref.at[:, at]), copy(wg_hbm.at[at, :], wg_ref.at[at, :])]
        loads += [copy(wu_hbm.at[at, :], wu_ref.at[at, :])]
    for at, there in zip(pieces, shifted):
        loads += [copy(in_hbm.at[:, there], in_ref.at[:, there]), copy(wd_hbm.at[:, at], wd_ref.at[:, at])]
    loads = iter(loads)
    gate_pre = up_pre = raw_hidden = 0.0
    for at in pieces:
        for _ in range(3):
            next(loads).wait()
        gate_pre += mm(in_ref[:, at], wg_ref[at, :])
        up_pre += mm(in_ref[:, at], wu_ref[at, :])
    for at, there in zip(pieces, shifted):
        for _ in range(2):
            next(loads).wait()
        raw_hidden += mm(in_ref[:, there], wd_ref[:, at], NT)
    same = lax.broadcasted_iota(jnp.int32, (slots, slots), 0) == lax.broadcasted_iota(jnp.int32, (slots, slots), 1)
    gates = jnp.sum(jnp.where(same, gates_ref[...], 0.0), axis=1, keepdims=True)
    sigmoid = 1.0 / (1.0 + jnp.exp(-gate_pre))
    silu = gate_pre * sigmoid
    hidden = silu * up_pre
    grad_hidden = gates * raw_hidden
    slope = sigmoid * (1.0 + gate_pre * (1.0 - sigmoid))
    ggp_ref[...] = (grad_hidden * up_pre * slope).astype(BF16)
    gup_ref[...] = (grad_hidden * silu).astype(BF16)
    out = [copy(ggp_ref, ggp_hbm), copy(gup_ref, gup_hbm)]
    hid_ref[...] = (hidden * gates).astype(BF16)
    router = jnp.sum(hidden.astype(BF16).astype(F32) * raw_hidden, axis=1, keepdims=True)
    router_ref[...] = jnp.sum(jnp.where(same, router, 0.0), axis=0, keepdims=True)
    out += [copy(hid_ref, hid_hbm)]
    first = pl.ds(pl.multiple_of(first_ref[0] * slots, slots), slots)
    for at in pieces:
        grad = mm(ggp_ref[...], wg_ref[at, :], NT) + mm(gup_ref[...], wu_ref[at, :], NT)
        back_ref[:, at] = grad.astype(BF16)
        out += [copy(back_ref.at[:, at], back_hbm.at[first, at])]
    for at in pieces:
        gain_ref[:, at] = jnp.sum(back_ref[:, at].astype(F32) * in_ref[:, at].astype(F32), axis=0, keepdims=True)
    for part in out:
        part.wait()


def expert(first, gates, incoming, w_gate, w_up, w_down, back=None):
    slots = incoming.shape[0]
    width, inner = w_gate.shape
    vmem = pl.BlockSpec(memory_space=pltpu.VMEM)
    hbm = pl.BlockSpec(memory_space=pl.ANY)
    small = [(slots, inner)] * 3
    held = [incoming.shape, w_gate.shape, w_up.shape, w_down.shape, (slots, width)] + small
    alias = {} if back is None else {6: 0}
    if back is None:
        back = gates
    return pl.pallas_call(
        expert_kernel,
        in_specs=[pl.BlockSpec(memory_space=pltpu.SMEM), vmem] + [hbm] * 5,
        out_specs=[hbm] * 4 + [vmem] * 2,
        out_shape=[jax.ShapeDtypeStruct(shape, BF16) for shape in [(2 * slots, width)] + small]
        + [jax.ShapeDtypeStruct((1, slots), F32), jax.ShapeDtypeStruct((1, width), F32)],
        scratch_shapes=[pltpu.VMEM(shape, BF16) for shape in held] + [pltpu.SemaphoreType.DMA((6 * width // CHUNK + 3,))],
        input_output_aliases=alias,
        compiler_params=params(),
        cost_estimate=cost(10 * slots * width * inner, 6 * width * (inner + slots)),
        name="expert_rows",
    )(first, gates, incoming, w_gate, w_up, w_down, back)


def total(value):
    count = lax.axis_size("grp") * lax.axis_size("seq")
    if count & (count - 1):
        return lax.psum(value, AXES)
    for b in range(count.bit_length() - 1):
        value = value + lax.ppermute(value, AXES, [(i, i ^ (1 << b)) for i in range(count)])
    return value


def local_part(scale, parity, queries, keys, values, grad, mix, prior):
    tok, width = queries.shape

    def work(_, h, at, ins, outs):
        q_ref, k_ref, v_ref, g_ref, mix_ref, prior_ref = ins
        gq_ref, pk_ref, pv_ref = outs
        row, col = triangle(tok)
        k, v, g = k_ref[:, at], v_ref[:, at], g_ref[:, at]
        mix_a = jnp.where(row >= col, mm(g, v, NT), 0.0).astype(BF16)
        mix_t = jnp.where(row <= col, mm(v, g, NT), 0.0).astype(BF16)
        gq_ref[:, at] = (scale * (mm(mix_a, k) + mm(g, prior_ref[h], NT))).astype(BF16)
        pk_ref[:, at] = mm(mix_t, q_ref[:, at]).astype(BF16)
        pv_ref[:, at] = mm(mix_ref[:, at], g).astype(BF16)

    outs = [jax.ShapeDtypeStruct((tok, width), BF16)] * 3
    return streamed(work, "local_attention", parity, [queries, keys, values, grad, mix, prior], outs)


def last_part(scale, parity, keys, values, pk, pv, own, other):
    tok, width = keys.shape
    half = own.shape[0]

    def work(parity_ref, h, at, ins, outs):
        k_ref, v_ref, pk_ref, pv_ref, own_ref, other_ref = ins
        gk_ref, gv_ref = outs
        later = jnp.where(parity_ref[0] == h // half, own_ref[h % half], other_ref[h % half])
        gk_ref[:, at] = (scale * (pk_ref[:, at].astype(F32) + mm(v_ref[:, at], later, NT))).astype(BF16)
        gv_ref[:, at] = (scale * (pv_ref[:, at].astype(F32) + mm(k_ref[:, at], later))).astype(BF16)

    outs = [jax.ShapeDtypeStruct((tok, width), BF16)] * 2
    return streamed(work, "last_attention", parity, [keys, values, pk, pv, own, other], outs)


def states_beyond(place, mine, other, beside):
    count = lax.axis_size("seq")
    parity = place & 1

    def swap(value, bit):
        return lax.ppermute(value.astype(BF16), "seq", [(i, i ^ bit) for i in range(count)])

    bits = [1 << b for b in range(1, count.bit_length() - 1)]
    quarter = mine.shape[0] // 2
    partner = swap(other, 1).astype(F32)
    mine = mine.astype(F32)
    both = mine + partner
    rising_sum, falling_base = both[:quarter], both[quarter:]
    rising = jnp.zeros_like(rising_sum)
    falling = jnp.zeros_like(falling_base)
    beside_out = None
    for up, down in zip(bits, reversed(bits)):
        got_up = swap(rising_sum, up)
        got_down = swap(falling + jnp.where((place & down) == 0, 0.0, falling_base), down)
        if beside is not None and beside_out is None:
            got_up, got_down, beside_out = lax.optimization_barrier((got_up, got_down, beside()))
        got_up, got_down = got_up.astype(F32), got_down.astype(F32)
        rising = rising + jnp.where((place & up) == 0, got_up, 0.0)
        rising_sum = rising_sum + got_up
        falling = falling + got_down
    own = jnp.concatenate([rising, falling])
    theirs = swap(own + jnp.where(parity == 1, mine, 0.0), 1)
    own = (own + jnp.where(parity == 0, partner, 0.0)).astype(BF16)
    return own, theirs, beside_out


def body(
    stream,
    cotangent,
    norm_gain,
    queries,
    key_vectors,
    value_vectors,
    expert_index,
    router_gates,
    gate_proj,
    up_proj,
    down_proj,
):
    tok, width = stream.shape
    seq_count = lax.axis_size("seq")
    dev_count = seq_count * lax.axis_size("grp")
    experts, capacity = expert_index.shape
    most = 2 * capacity // dev_count
    here = lax.axis_index("grp") * seq_count + lax.axis_index("seq")
    scale = 1.0 / math.sqrt(HEAD * tok * seq_count)
    gain = norm_gain[None, :]
    w_gate, w_up, w_down = gate_proj[0], up_proj[0], down_proj[0]

    halves = dev_count // 2
    swap = [(i, (i + halves) % dev_count) for i in range(dev_count)]
    groups = [[side * halves + i for i in range(halves)] for side in range(2)]
    side = here // halves
    side_array = side.astype(jnp.int32)[None]
    parity = (lax.axis_index("seq") & 1).astype(jnp.int32)[None]
    here_array = here.astype(jnp.int32)[None]
    there_array = ((here + halves) % dev_count).astype(jnp.int32)[None]

    def exchange(value):
        return lax.all_to_all(value, AXES, split_axis=0, concat_axis=0, tiled=True, axis_index_groups=groups)

    inputs, out_own = prepare(most, side_array, here_array, expert_index, gain, cotangent, stream)
    own = exchange(out_own)
    far_cot = lax.ppermute(cotangent, AXES, swap)
    far_inputs = lax.ppermute(inputs, AXES, swap)

    key_states, mix_b = early(parity, queries, key_vectors, value_vectors)
    heads = width // HEAD
    place = lax.axis_index("seq")
    own_prior, other_prior, _ = states_beyond(
        seq_count - 1 - place, key_states[: heads // 2], key_states[heads // 2 :], None
    )
    is_low = parity[0] == 0
    prior = jnp.concatenate(
        [jnp.where(is_low, own_prior, other_prior), jnp.where(is_low, other_prior, own_prior)]
    )
    pick_t = picks(most, tok, here_array, expert_index).T
    half_index = lax.dynamic_slice_in_dim(expert_index, side * (experts // 2), experts // 2, 0)
    far_pick = picks(most, tok, there_array, half_index)
    own_index = lax.dynamic_index_in_dim(expert_index, here, 0, keepdims=False)
    source = own_index // tok
    ahead = (source[None, :] == source[:, None]) & (own_index[None, :] < own_index[:, None])
    before = jnp.sum(ahead.astype(jnp.int32), axis=1)
    arrival = jnp.where(source // halves == side, source % halves, halves + source % halves) * most + before
    place_t = arrival[None, :] == jnp.arange(dev_count * most)[:, None]
    slot_gates = jnp.sum(jnp.where(place_t, router_gates, 0.0), axis=1).reshape(2, 1, halves * most)
    far_cot, far_inputs, mix_b, pick_t, far_pick, slot_gates, prior = lax.optimization_barrier(
        (far_cot, far_inputs, mix_b, pick_t, far_pick, slot_gates, prior)
    )
    far_out = pack(far_pick, far_inputs, far_cot)
    far = exchange(far_out)

    own, far_out = lax.optimization_barrier((own, far_out))
    back, own_ggp, own_gup, own_hidden, own_router, own_gain = expert(
        side_array, slot_gates[0], own, w_gate, w_up, w_down
    )
    far, back = lax.optimization_barrier((far, back))
    back, far_ggp, far_gup, far_hidden, far_router, far_gain = expert(
        1 - side_array, slot_gates[1], far, w_gate, w_up, w_down, back
    )
    returned = lax.all_to_all(back, AXES, split_axis=0, concat_axis=0, tiled=True)

    gain_total = total((own_gain + far_gain) / gain)
    own, far, far_ggp, back = lax.optimization_barrier((own, far, far_ggp, back))
    arrived = jnp.concatenate([own, far])
    rows, dy_rows = arrived[:, :width], arrived[:, width:]
    grad_gate_pre = jnp.concatenate([own_ggp, far_ggp])
    grad_up_pre = jnp.concatenate([own_gup, far_gup])
    hidden = jnp.concatenate([own_hidden, far_hidden])
    grad_gate = lax.dot_general(rows, grad_gate_pre, TN, preferred_element_type=F32).astype(BF16)
    grad_up = lax.dot_general(rows, grad_up_pre, TN, preferred_element_type=F32).astype(BF16)
    grad_down = lax.dot_general(hidden, dy_rows, TN, preferred_element_type=F32).astype(BF16)
    slot_router = jnp.concatenate([own_router, far_router], axis=1).reshape(dev_count * most, 1)
    router = jnp.sum(jnp.where(place_t, slot_router, 0.0), axis=0, keepdims=True)
    returned, grad_gate, grad_up, grad_down, router, gain_total = lax.optimization_barrier(
        (returned, grad_gate, grad_up, grad_down, router, gain_total)
    )

    grad_stream, mine, other = combine(parity, pick_t, gain, stream, returned, cotangent, queries)
    local = lambda: local_part(scale, parity, queries, key_vectors, value_vectors, grad_stream, mix_b, prior)
    own_state, other_state, done = states_beyond(place, mine, other, local)
    grad_queries, part_k, part_v = done
    grad_keys, grad_values = last_part(
        scale, parity, key_vectors, value_vectors, part_k, part_v, own_state, other_state
    )
    return (
        grad_stream,
        grad_queries,
        grad_keys,
        grad_values,
        grad_gate[None],
        grad_up[None],
        grad_down[None],
        router,
        gain_total[0],
    )


def solution(mesh):
    rows = P(AXES, None)
    cube = P(AXES, None, None)
    in_specs = (rows, rows, P(), rows, rows, rows, P(), rows, cube, cube, cube)
    out_specs = (rows, rows, rows, rows, cube, cube, cube, rows, P())
    return jax.shard_map(body, mesh=mesh, in_specs=in_specs, out_specs=out_specs, check_vma=False)
```

time: 213 us -> 202 us (0.948)
  blocking collectives: 34.7 us -> 0 us
  starting transfers between devices: 26.8 us -> 40.2 us
  between operations: 14.3 us -> 1.29 us
  waiting for transfers between devices: 66.4 us -> 77.3 us
  local copies, waits for them, and re-layouts: 3.34 us -> 8.96 us
  Pallas kernels: 46.4 us -> 50.3 us
  matrix products: 8.11 us -> 10.6 us
    all_to_all x1 -> x0, blocking collectives: 34.7 us -> none  [exchange(): lax.all_to_all(value, AXES, split_axis=0, concat_axis=0, tiled=True, axis...]
    ppermute x1, waiting for transfers between devices: 20.5 us -> 0.01 us  [body(): far_cot = lax.ppermute(cotangent, AXES, swap)]
    all_to_all x1 -> x2, waiting for transfers between devices: 1.78 us -> 18.9 us  [exchange(): lax.all_to_all(value, AXES, split_axis=0, concat_axis=0, tiled=True, axis...]
    ppermute x6 -> x12, waiting for transfers between devices: 5.92 us -> 21.9 us  [swap(): lax.ppermute(value.astype(BF16), 'seq', [(i, i ^ bit) for i in range(coun...]
    ppermute x6 -> x12, starting transfers between devices: 4.19 us -> 10.6 us  [swap(): lax.ppermute(value.astype(BF16), 'seq', [(i, i ^ bit) for i in range(coun...]
    all_to_all x1 -> x2, starting transfers between devices: 6.48 us -> 11.3 us  [exchange(): lax.all_to_all(value, AXES, split_axis=0, concat_axis=0, tiled=True, axis...]
    reduce_sum x2, other arithmetic: 4.49 us -> 0.86 us  [the longest x1 0.71 us: body(): jnp.sum(jnp.where(place_t, slot_router, 0.0), axis=0, keepdims=True)]
    pallas_call x4 -> x5, Pallas kernels: 28.4 us -> 31.8 us  [the longest x2 19.8 us: expert(): pl.pallas_call(expert_kernel, in_specs=[pl.BlockSpec(memory_space=pltpu.S...]
  transfers between devices with their start and end apart: 16 -> 22, of which waited for: 10 -> 11; matrix products, arithmetic and copies ran while one was open for 9% -> 13% of each run, Pallas kernels for 15% -> 13%
where the time goes in v3:
time: 202 us; the launch traced here: 201 us
  waiting for transfers between devices  77.3 us (38%)
  Pallas kernels  50.3 us (25%)
  starting transfers between devices  40.2 us (20%)
  other arithmetic  12.3 us (6%)
  matrix products  10.6 us (5%)
  local copies, waits for them, and re-layouts  8.96 us (4%)
    ppermute x5, waiting for transfers between devices, total(): lax.ppermute(value, AXES, [(i, i ^ 1 << b) for i in range(count)])  24.7 us
    ppermute x12, waiting for transfers between devices, swap(): lax.ppermute(value.astype(BF16), 'seq', [(i, i ^ bit) for i in range(coun...  21.9 us
    pallas_call x2, Pallas kernels, expert(): pl.pallas_call(expert_kernel, in_specs=[pl.BlockSpec(memory_space=pltpu.S...  19.8 us
    all_to_all x2, waiting for transfers between devices, exchange(): lax.all_to_all(value, AXES, split_axis=0, concat_axis=0, tiled=True, axis...  18.9 us
    pallas_call x3, Pallas kernels, streamed(): pl.pallas_call(kernel, in_specs=[pl.BlockSpec(memory_space=pltpu.SMEM)] +...  12 us
    ppermute x1, waiting for transfers between devices, body(): far_inputs = lax.ppermute(inputs, AXES, swap)  11.8 us
    all_to_all x2, starting transfers between devices, exchange(): lax.all_to_all(value, AXES, split_axis=0, concat_axis=0, tiled=True, axis...  11.3 us
    ppermute x12, starting transfers between devices, swap(): lax.ppermute(value.astype(BF16), 'seq', [(i, i ^ bit) for i in range(coun...  10.6 us
  transfers between devices with their start and end apart: 22, of which 11 were waited for; matrix products, arithmetic and copies ran while one was open for 13% of the time, Pallas kernels for 13%

profile of v3, /device:TPU:0, one launch (start us, length us, event | category | flops | bytes accessed | tf_op | source)
XLA Modules:
  0.0 201.0 jit_solution(17641855177368934436)
XLA Ops:
  0.7 4.9 %prepare_rows.1 = (bf16[128,2048]{1,0:T(8,128)(2,1)}, bf16[256,4096]{1,0:T(8,128)(2,1)}) custom-call(s32[1]{0:T(128)} %bitcast.1.half_ref.first_ref, s32[1]{0:T(128)} %bitcast.2.device_ref, s32[32,256]{1,0:T(8,128)} %index_ref.3, f32[1,2048]{1,0:T(1,128)} %bitcast.35, bf16[128,2048]{1,0:T(8,128)(2,1)} %cot_hbm.1, bf16[128,2048]{1,0:T(8,128)(2,1)} %stream_hbm.1), custom_call_target="tpu_custom_call" | custom-call | flops 1 | bytes 1 | tf_op jit(solution)/shard_map/prepare_rows/pallas_call | solution.py:104
  5.6 6.5 %all-to-all-start.1 = ((bf16[16,16,4096]{2,1,0:T(8,128)(2,1)}), bf16[16,16,4096]{2,1,0:T(8,128)(2,1)}, u32[]{:S(2)}, u32[]{:S(2)}) async-start(bf16[16,16,4096]{2,1,0:T(8,128)(2,1)} %bitcast.32), calls=%async_computation.1 | async-start | bytes 4194304 | tf_op jit(solution)/shard_map/all_to_all | solution.py:476
  12.1 3.3 %early_states.1 = (bf16[16,128,128]{2,1,0:T(8,128)(2,1)}, bf16[128,2048]{1,0:T(8,128)(2,1)}) custom-call(s32[1]{0:T(128)} %bitcast.refs_0_.parity_ref, bf16[128,2048]{1,0:T(8,128)(2,1)} %refs_1_.4, bf16[128,2048]{1,0:T(8,128)(2,1)} %refs_1_.5, bf16[128,2048]{1,0:T(8,128)(2,1)} %refs_2_.5), custom_call_target="tpu_custom_call" | custom-call | flops 1 | bytes 1 | tf_op jit(solution)/shard_map/early_states/pallas_call | solution.py:192
  16.8 2.6 %collective-permute-start = (bf16[128,2048]{1,0:T(8,128)(2,1)S(1)}, bf16[128,2048]{1,0:T(8,128)(2,1)}, u32[]{:S(2)}, u32[]{:S(2)}) collective-permute-start(bf16[128,2048]{1,0:T(8,128)(2,1)S(1)} %copy-done), channel_id=1, source_target_pairs={{0,16},{1,17},{2,18},{3,19},{4,20},{5,21},{6,22},{7,23},{8,24},{9,... | collective-permute-start | bytes 1572872 | tf_op jit(solution)/shard_map/ppermute | solution.py:480
  24.0 8.3 %collective-permute-done.3 = bf16[4,128,128]{2,1,0:T(8,128)(2,1)S(1)} collective-permute-done((bf16[4,128,128]{2,1,0:T(8,128)(2,1)S(1)}, bf16[4,128,128]{2,1,0:T(8,128)(2,1)S(1)}, u32[]{:S(2)}, u32[]{:S(2)}) %collective-permute-start.3) | collective-permute-done | bytes 131104 | tf_op jit(solution)/shard_map/ppermute | solution.py:417
  35.1 3.1 %pick_slots.2 = bf16[512,128]{1,0:T(8,128)(2,1)} custom-call(s32[1]{0:T(128)} %bitcast.2.device_ref, s32[32,256]{1,0:T(8,128)} %index_ref.3), custom_call_target="tpu_custom_call" | custom-call | flops 1 | bytes 1 | tf_op jit(solution)/shard_map/pick_slots/pallas_call | solution.py:61
  44.8 5.2 %collective-permute-done.6 = bf16[4,128,128]{2,1,0:T(8,128)(2,1)S(1)} collective-permute-done((bf16[4,128,128]{2,1,0:T(8,128)(2,1)}, bf16[4,128,128]{2,1,0:T(8,128)(2,1)S(1)}, u32[]{:S(2)}, u32[]{:S(2)}) %collective-permute-start.6) | collective-permute-done | bytes 131104 | tf_op jit(solution)/shard_map/ppermute | solution.py:417
  53.7 11.8 %collective-permute-done.1.x_ref = bf16[128,2048]{1,0:T(8,128)(2,1)} collective-permute-done((bf16[128,2048]{1,0:T(8,128)(2,1)}, bf16[128,2048]{1,0:T(8,128)(2,1)}, u32[]{:S(2)}, u32[]{:S(2)}) %collective-permute-start.1) | collective-permute-done | bytes 524320 | tf_op jit(solution)/shard_map/ppermute | solution.py:481
  65.5 2.9 %pack_rows.1 = bf16[256,4096]{1,0:T(8,128)(2,1)} custom-call(bf16[256,128]{1,0:T(8,128)(2,1)} %pick_slots.3.pick_ref, bf16[128,2048]{1,0:T(8,128)(2,1)} %collective-permute-done.1.x_ref, bf16[128,2048]{1,0:T(8,128)(2,1)} %collective-permute-done.cot_ref), custom_call_target="tpu_custom_call" | custom-call | flops 1 | bytes 1 | tf_op jit(solution)/shard_map/pack_rows/pallas_call | solution.py:139
  68.4 4.8 %all-to-all-start = ((bf16[16,16,4096]{2,1,0:T(8,128)(2,1)}), bf16[16,16,4096]{2,1,0:T(8,128)(2,1)}, u32[]{:S(2)}, u32[]{:S(2)}) async-start(bf16[16,16,4096]{2,1,0:T(8,128)(2,1)} %bitcast.31), calls=%async_computation | async-start | bytes 4194304 | tf_op jit(solution)/shard_map/all_to_all | solution.py:476
  73.7 9.9 %expert_rows.2 = (bf16[512,2048]{1,0:T(8,128)(2,1)}, bf16[256,768]{1,0:T(8,128)(2,1)}, bf16[256,768]{1,0:T(8,128)(2,1)}, bf16[256,768]{1,0:T(8,128)(2,1)}, f32[1,256]{1,0:T(1,128)}, /*index=5*/f32[1,2048]{1,0:T(1,128)}) custom-call(s32[1]{0:T(128)} %bitcast.1.half_ref.first_ref, f32[1,256]{1,0:T(1,128)} %get-tuple-element.119.gates_ref._, ...), custom_call_target="tpu_custom_call" | custom-call | flops 4026531840 | bytes 12582912 | tf_op jit(solution)/shard_map/expert_rows/pallas_call | solution.py:356
  83.6 18.9 %all-to-all-done = bf16[16,16,4096]{2,1,0:T(8,128)(2,1)} async-done(((bf16[16,16,4096]{2,1,0:T(8,128)(2,1)}), bf16[16,16,4096]{2,1,0:T(8,128)(2,1)}, u32[]{:S(2)}, u32[]{:S(2)}) %all-to-all-start) | async-done | bytes 2097184 | tf_op jit(solution)/shard_map/all_to_all | solution.py:476
  102.5 9.9 %expert_rows.3 = (bf16[512,2048]{1,0:T(8,128)(2,1)}, bf16[256,768]{1,0:T(8,128)(2,1)}, bf16[256,768]{1,0:T(8,128)(2,1)}, bf16[256,768]{1,0:T(8,128)(2,1)}, f32[1,256]{1,0:T(1,128)}, /*index=5*/f32[1,2048]{1,0:T(1,128)}) custom-call(s32[1]{0:T(128)S(6)} %sub.27.first_ref, f32[1,256]{1,0:T(1,128)} %get-tuple-element.120.gates_ref, ...), custom_call_target="tpu_custom_call", output_to_operand_aliasing={{0}: (6, {})} | custom-call | flops 4026531840 | bytes 12582912 | tf_op jit(solution)/shard_map/expert_rows/pallas_call | solution.py:356
  112.5 6.4 %all-to-all-start.2 = ((bf16[32,16,2048]{2,1,0:T(8,128)(2,1)}), bf16[32,16,2048]{2,1,0:T(8,128)(2,1)}, u32[]{:S(2)}, u32[]{:S(2)}) async-start(bf16[32,16,2048]{2,1,0:T(8,128)(2,1)} %bitcast.33), calls=%async_computation.2 | async-start | bytes 4194304 | tf_op jit(solution)/shard_map/all_to_all | solution.py:517
  122.8 3.5 %convolution_convert_fusion.1 = bf16[2048,768]{1,0:T(8,128)(2,1)} fusion(bf16[512,4096]{1,0:T(8,128)(2,1)S(1)} %constant_dynamic-update-slice_fusion, bf16[256,768]{1,0:T(8,128)(2,1)S(1)} %copy-done.14, bf16[256,768]{1,0:T(8,128)(2,1)S(1)} %copy-done.17), kind=kOutput, calls=%fused_computation.1 | convolution fusion | flops 1613758464 | bytes 6029312 | tf_op jit(solution)/shard_map/dot_general | solution.py:527
  128.1 3.6 %convolution_convert_fusion.2 = bf16[2048,768]{1,0:T(8,128)(2,1)} fusion(bf16[512,4096]{1,0:T(8,128)(2,1)S(1)} %constant_dynamic-update-slice_fusion, bf16[256,768]{1,0:T(8,128)(2,1)S(1)} %copy-done.13, bf16[256,768]{1,0:T(8,128)(2,1)S(1)} %copy-done.16), kind=kOutput, calls=%fused_computation.2 | convolution fusion | flops 1613758464 | bytes 6029312 | tf_op jit(solution)/shard_map/dot_general | solution.py:526
  134.5 3.5 %convolution_convert_fusion = bf16[768,2048]{1,0:T(8,128)(2,1)} fusion(bf16[512,4096]{1,0:T(8,128)(2,1)S(1)} %constant_dynamic-update-slice_fusion, bf16[256,768]{1,0:T(8,128)(2,1)S(1)} %copy-done.12, bf16[256,768]{1,0:T(8,128)(2,1)S(1)} %copy-done.15), kind=kOutput, calls=%fused_computation | convolution fusion | flops 1613758464 | bytes 6029312 | tf_op jit(solution)/shard_map/dot_general | solution.py:528
  138.7 15.2 %collective-permute-done.11 = f32[1,2048]{1,0:T(1,128)S(1)} collective-permute-done((f32[1,2048]{1,0:T(1,128)S(1)}, f32[1,2048]{1,0:T(1,128)S(1)}, u32[]{:S(2)}, u32[]{:S(2)}) %collective-permute-start.11) | collective-permute-done | bytes 8224 | tf_op jit(solution)/shard_map/ppermute | solution.py:375
  153.9 4.2 %collective-permute-start.12 = (f32[1,2048]{1,0:T(1,128)S(1)}, f32[1,2048]{1,0:T(1,128)S(1)}, u32[]{:S(2)}, u32[]{:S(2)}) collective-permute-start(f32[1,2048]{1,0:T(1,128)S(1)} %add.123), channel_id=1, source_target_pairs={{0,16},{1,17},{2,18},{3,19},{4,20},{5,21},{6,22},{7,23},{8,24},{9,... | collective-permute-start | bytes 24584 | tf_op jit(solution)/shard_map/ppermute | solution.py:375
  158.8 9.1 %collective-permute-done.12 = f32[1,2048]{1,0:T(1,128)S(1)} collective-permute-done((f32[1,2048]{1,0:T(1,128)S(1)}, f32[1,2048]{1,0:T(1,128)S(1)}, u32[]{:S(2)}, u32[]{:S(2)}) %collective-permute-start.12) | collective-permute-done | bytes 8224 | tf_op jit(solution)/shard_map/ppermute | solution.py:375
  168.5 5.3 %combine_rows.1 = (bf16[128,2048]{1,0:T(8,128)(2,1)}, bf16[8,128,128]{2,1,0:T(8,128)(2,1)}, bf16[8,128,128]{2,1,0:T(8,128)(2,1)}) custom-call(s32[1]{0:T(128)} %bitcast.refs_0_.parity_ref, bf16[128,512]{1,0:T(8,128)(2,1)} %bitcast.34, f32[1,2048]{1,0:T(1,128)} %bitcast.36, bf16[128,2048]{1,0:T(8,128)(2,1)} %stream_hbm.1, ...), custom_call_target="tpu_custom_call" | custom-call | flops 335544320 | bytes 5242880 | tf_op jit(solution)/shard_map/combine_rows/pallas_call | solution.py:272
  180.9 5.6 %local_attention.1 = (bf16[128,2048]{1,0:T(8,128)(2,1)}, bf16[128,2048]{1,0:T(8,128)(2,1)}, bf16[128,2048]{1,0:T(8,128)(2,1)}) custom-call(s32[1]{0:T(128)} %bitcast.refs_0_.parity_ref, bf16[128,2048]{1,0:T(8,128)(2,1)} %refs_1_.4, bf16[128,2048]{1,0:T(8,128)(2,1)} %refs_1_.5, bf16[128,2048]{1,0:T(8,128)(2,1)} %refs_2_.5, ...), custom_call_target="tpu_custom_call" | custom-call | flops 1 | bytes 1 | tf_op jit(solution)/shard_map/local_attention/pallas_call | solution.py:192
  188.8 3.7 %collective-permute-done.16 = bf16[4,128,128]{2,1,0:T(8,128)(2,1)S(1)} collective-permute-done((bf16[4,128,128]{2,1,0:T(8,128)(2,1)S(1)}, bf16[4,128,128]{2,1,0:T(8,128)(2,1)S(1)}, u32[]{:S(2)}, u32[]{:S(2)}) %collective-permute-start.16) | collective-permute-done | bytes 131104 | tf_op jit(solution)/shard_map/ppermute | solution.py:417
  197.6 3.2 %last_attention.1 = (bf16[128,2048]{1,0:T(8,128)(2,1)}, bf16[128,2048]{1,0:T(8,128)(2,1)}) custom-call(s32[1]{0:T(128)} %bitcast.refs_0_.parity_ref, bf16[128,2048]{1,0:T(8,128)(2,1)} %refs_1_.5, bf16[128,2048]{1,0:T(8,128)(2,1)} %refs_2_.5, bf16[128,2048]{1,0:T(8,128)(2,1)} %get-tuple-element.94.refs_3_, bf16[128,2048]{1,0:T(8,128)(2,1)} %get-tuple-element.95.refs_4_, ...), custom_call_target="tpu_custom_call" | custom-call | flops 1 | bytes 1 | tf_op jit(solution)/shard_map/last_attention/pallas_call | solution.py:192
  (103 shorter events, 44.4 us)
Async XLA Ops:
  5.6 62.8 %all-to-all-start.1 = ((bf16[16,16,4096]{2,1,0:T(8,128)(2,1)}), bf16[16,16,4096]{2,1,0:T(8,128)(2,1)}, u32[]{:S(2)}, u32[]{:S(2)}) async-start(bf16[16,16,4096]{2,1,0:T(8,128)(2,1)} %bitcast.32), calls=%async_computation.1 | async-start | bytes 4194304 | tf_op jit(solution)/shard_map/all_to_all | solution.py:476
  15.4 35.8 %copy-start.9 = (f32[1,256]{1,0:T(1,128)S(1)}, f32[1,256]{1,0:T(1,128)}, u32[]{:S(2)}) copy-start(f32[1,256]{1,0:T(1,128)} %param.18) | copy-start | bytes 3076
  16.4 3.4 %collective-permute-start.2 = (bf16[8,128,128]{2,1,0:T(8,128)(2,1)S(1)}, bf16[8,128,128]{2,1,0:T(8,128)(2,1)S(1)}, u32[]{:S(2)}, u32[]{:S(2)}) collective-permute-start(bf16[8,128,128]{2,1,0:T(8,128)(2,1)S(1)} %slice.31), channel_id=1, source_target_pairs={{0,1},{1,0},{2,3},{3,2},{4,5},{5,4},{6,7},{7,6},{8,9},{9,8},{10,11... | collective-permute-start | bytes 786440 | tf_op jit(solution)/shard_map/ppermute | solution.py:417
  16.8 48.8 %collective-permute-start = (bf16[128,2048]{1,0:T(8,128)(2,1)S(1)}, bf16[128,2048]{1,0:T(8,128)(2,1)}, u32[]{:S(2)}, u32[]{:S(2)}) collective-permute-start(bf16[128,2048]{1,0:T(8,128)(2,1)S(1)} %copy-done), channel_id=1, source_target_pairs={{0,16},{1,17},{2,18},{3,19},{4,20},{5,21},{6,22},{7,23},{8,24},{9,... | collective-permute-start | bytes 1572872 | tf_op jit(solution)/shard_map/ppermute | solution.py:480
  19.4 46.2 %collective-permute-start.1 = (bf16[128,2048]{1,0:T(8,128)(2,1)}, bf16[128,2048]{1,0:T(8,128)(2,1)}, u32[]{:S(2)}, u32[]{:S(2)}) collective-permute-start(bf16[128,2048]{1,0:T(8,128)(2,1)} %get-tuple-element.57), channel_id=1, source_target_pairs={{0,16},{1,17},{2,18},{3,19},{4,20},{5,21},{6,22},{7,23},{8,24},{9,... | collective-permute-start | bytes 1572872 | tf_op jit(solution)/shard_map/ppermute | solution.py:481
  20.8 11.6 %collective-permute-start.3 = (bf16[4,128,128]{2,1,0:T(8,128)(2,1)S(1)}, bf16[4,128,128]{2,1,0:T(8,128)(2,1)S(1)}, u32[]{:S(2)}, u32[]{:S(2)}) collective-permute-start(bf16[4,128,128]{2,1,0:T(8,128)(2,1)S(1)} %get-tuple-element.117), channel_id=1, source_target_pairs={{0,2},{1,3},{2,0},{3,1},{4,6},{5,7},{6,4},{7,5},{8,10},{9,11},{10,... | collective-permute-start | bytes 393224 | tf_op jit(solution)/shard_map/ppermute | solution.py:417
  22.5 9.8 %collective-permute-start.5 = (bf16[4,128,128]{2,1,0:T(8,128)(2,1)S(1)}, bf16[4,128,128]{2,1,0:T(8,128)(2,1)S(1)}, u32[]{:S(2)}, u32[]{:S(2)}) collective-permute-start(bf16[4,128,128]{2,1,0:T(8,128)(2,1)S(1)} %get-tuple-element.118), channel_id=1, source_target_pairs={{0,4},{1,5},{2,6},{3,7},{4,0},{5,1},{6,2},{7,3},{8,12},{9,13},{10,... | collective-permute-start | bytes 393224 | tf_op jit(solution)/shard_map/ppermute | solution.py:417
  33.2 10.6 %collective-permute-start.4 = (bf16[4,128,128]{2,1,0:T(8,128)(2,1)}, bf16[4,128,128]{2,1,0:T(8,128)(2,1)}, u32[]{:S(2)}, u32[]{:S(2)}) collective-permute-start(bf16[4,128,128]{2,1,0:T(8,128)(2,1)} %get-tuple-element.115), channel_id=1, source_target_pairs={{0,4},{1,5},{2,6},{3,7},{4,0},{5,1},{6,2},{7,3},{8,12},{9,13},{10,... | collective-permute-start | bytes 393224 | tf_op jit(solution)/shard_map/ppermute | solution.py:417
  42.4 7.6 %collective-permute-start.6 = (bf16[4,128,128]{2,1,0:T(8,128)(2,1)}, bf16[4,128,128]{2,1,0:T(8,128)(2,1)S(1)}, u32[]{:S(2)}, u32[]{:S(2)}) collective-permute-start(bf16[4,128,128]{2,1,0:T(8,128)(2,1)} %get-tuple-element.116), channel_id=1, source_target_pairs={{0,2},{1,3},{2,0},{3,1},{4,6},{5,7},{6,4},{7,5},{8,10},{9,11},{10,... | collective-permute-start | bytes 393224 | tf_op jit(solution)/shard_map/ppermute | solution.py:417
  51.1 1.6 collective-permute-start.7
  68.4 34.2 %all-to-all-start = ((bf16[16,16,4096]{2,1,0:T(8,128)(2,1)}), bf16[16,16,4096]{2,1,0:T(8,128)(2,1)}, u32[]{:S(2)}, u32[]{:S(2)}) async-start(bf16[16,16,4096]{2,1,0:T(8,128)(2,1)} %bitcast.31), calls=%async_computation | async-start | bytes 4194304 | tf_op jit(solution)/shard_map/all_to_all | solution.py:476
  112.5 56.0 %all-to-all-start.2 = ((bf16[32,16,2048]{2,1,0:T(8,128)(2,1)}), bf16[32,16,2048]{2,1,0:T(8,128)(2,1)}, u32[]{:S(2)}, u32[]{:S(2)}) async-start(bf16[32,16,2048]{2,1,0:T(8,128)(2,1)} %bitcast.33), calls=%async_computation.2 | async-start | bytes 4194304 | tf_op jit(solution)/shard_map/all_to_all | solution.py:517
  119.0 7.4 %collective-permute-start.8 = (f32[1,2048]{1,0:T(1,128)S(1)}, f32[1,2048]{1,0:T(1,128)S(1)}, u32[]{:S(2)}, u32[]{:S(2)}) collective-permute-start(f32[1,2048]{1,0:T(1,128)S(1)} %add_divide_fusion), channel_id=1, source_target_pairs={{0,1},{1,0},{2,3},{3,2},{4,5},{5,4},{6,7},{7,6},{8,9},{9,8},{10,11... | collective-permute-start | bytes 24584 | tf_op jit(solution)/shard_map/ppermute | solution.py:375
  126.4 5.7 %collective-permute-start.9 = (f32[1,2048]{1,0:T(1,128)S(1)}, f32[1,2048]{1,0:T(1,128)S(1)}, u32[]{:S(2)}, u32[]{:S(2)}) collective-permute-start(f32[1,2048]{1,0:T(1,128)S(1)} %add.120), channel_id=1, source_target_pairs={{0,2},{1,3},{2,0},{3,1},{4,6},{5,7},{6,4},{7,5},{8,10},{9,11},{10,... | collective-permute-start | bytes 24584 | tf_op jit(solution)/shard_map/ppermute | solution.py:375
  132.1 5.9 %collective-permute-start.10 = (f32[1,2048]{1,0:T(1,128)S(1)}, f32[1,2048]{1,0:T(1,128)S(1)}, u32[]{:S(2)}, u32[]{:S(2)}) collective-permute-start(f32[1,2048]{1,0:T(1,128)S(1)} %add.121), channel_id=1, source_target_pairs={{0,4},{1,5},{2,6},{3,7},{4,0},{5,1},{6,2},{7,3},{8,12},{9,13},{10,... | collective-permute-start | bytes 24584 | tf_op jit(solution)/shard_map/ppermute | solution.py:375
  138.0 15.8 %collective-permute-start.11 = (f32[1,2048]{1,0:T(1,128)S(1)}, f32[1,2048]{1,0:T(1,128)S(1)}, u32[]{:S(2)}, u32[]{:S(2)}) collective-permute-start(f32[1,2048]{1,0:T(1,128)S(1)} %add.122), channel_id=1, source_target_pairs={{0,8},{1,9},{2,10},{3,11},{4,12},{5,13},{6,14},{7,15},{8,0},{9,1},... | collective-permute-start | bytes 24584 | tf_op jit(solution)/shard_map/ppermute | solution.py:375
  153.9 14.0 %collective-permute-start.12 = (f32[1,2048]{1,0:T(1,128)S(1)}, f32[1,2048]{1,0:T(1,128)S(1)}, u32[]{:S(2)}, u32[]{:S(2)}) collective-permute-start(f32[1,2048]{1,0:T(1,128)S(1)} %add.123), channel_id=1, source_target_pairs={{0,16},{1,17},{2,18},{3,19},{4,20},{5,21},{6,22},{7,23},{8,24},{9,... | collective-permute-start | bytes 24584 | tf_op jit(solution)/shard_map/ppermute | solution.py:375
  173.8 1.8 collective-permute-start.13
  177.3 16.2 %copy-start.1 = (bf16[8,128,128]{2,1,0:T(8,128)(2,1)S(1)}, bf16[8,128,128]{2,1,0:T(8,128)(2,1)}, u32[]{:S(2)}) copy-start(bf16[8,128,128]{2,1,0:T(8,128)(2,1)} %get-tuple-element.86) | copy-start | bytes 786436
  178.1 8.3 %collective-permute-start.14 = (bf16[4,128,128]{2,1,0:T(8,128)(2,1)}, bf16[4,128,128]{2,1,0:T(8,128)(2,1)}, u32[]{:S(2)}, u32[]{:S(2)}) collective-permute-start(bf16[4,128,128]{2,1,0:T(8,128)(2,1)} %get-tuple-element.114), channel_id=1, source_target_pairs={{0,2},{1,3},{2,0},{3,1},{4,6},{5,7},{6,4},{7,5},{8,10},{9,11},{10,... | collective-permute-start | bytes 393224 | tf_op jit(solution)/shard_map/ppermute | solution.py:417
  179.5 7.0 %collective-permute-start.15 = (bf16[4,128,128]{2,1,0:T(8,128)(2,1)}, bf16[4,128,128]{2,1,0:T(8,128)(2,1)S(1)}, u32[]{:S(2)}, u32[]{:S(2)}) collective-permute-start(bf16[4,128,128]{2,1,0:T(8,128)(2,1)} %get-tuple-element.113), channel_id=1, source_target_pairs={{0,4},{1,5},{2,6},{3,7},{4,0},{5,1},{6,2},{7,3},{8,12},{9,13},{10,... | collective-permute-start | bytes 393224 | tf_op jit(solution)/shard_map/ppermute | solution.py:417
  187.4 5.0 %collective-permute-start.16 = (bf16[4,128,128]{2,1,0:T(8,128)(2,1)S(1)}, bf16[4,128,128]{2,1,0:T(8,128)(2,1)S(1)}, u32[]{:S(2)}, u32[]{:S(2)}) collective-permute-start(bf16[4,128,128]{2,1,0:T(8,128)(2,1)S(1)} %get-tuple-element.111), channel_id=1, source_target_pairs={{0,4},{1,5},{2,6},{3,7},{4,0},{5,1},{6,2},{7,3},{8,12},{9,13},{10,... | collective-permute-start | bytes 393224 | tf_op jit(solution)/shard_map/ppermute | solution.py:417
  188.1 5.3 %collective-permute-start.17 = (bf16[4,128,128]{2,1,0:T(8,128)(2,1)S(1)}, bf16[4,128,128]{2,1,0:T(8,128)(2,1)S(1)}, u32[]{:S(2)}, u32[]{:S(2)}) collective-permute-start(bf16[4,128,128]{2,1,0:T(8,128)(2,1)S(1)} %get-tuple-element.112), channel_id=1, source_target_pairs={{0,2},{1,3},{2,0},{3,1},{4,6},{5,7},{6,4},{7,5},{8,10},{9,11},{10,... | collective-permute-start | bytes 393224 | tf_op jit(solution)/shard_map/ppermute | solution.py:417
  195.3 1.5 collective-permute-start.18
  (16 other events, 82.5 us)

commit v4 on v3

--- a/solution.py
+++ b/solution.py
@@ -83,15 +83,32 @@
 
 
 def prepare_kernel(
-    most, half_ref, device_ref, index_ref, gain_ref, cot_ref, stream_ref, x_ref, out_hbm, out_ref, pick_ref, member_ref, sems
+    most, half_ref, device_ref, index_hbm, gain_hbm, cot_hbm, stream_hbm, x_hbm, out_hbm,
+    index_ref, gain_ref, cot_ref, stream_ref, x_ref, out_ref, pick_ref, member_ref, sems, edge_sems,
 ):
-    del half_ref
+    half = index_ref.shape[0]
+    first = pl.ds(pl.multiple_of(half_ref[0] * half, half), half)
+    index_in = pltpu.make_async_copy(index_hbm.at[first, :], index_ref, edge_sems.at[3])
+    gain_in = pltpu.make_async_copy(gain_hbm, gain_ref, edge_sems.at[4])
+    index_in.start()
+    gain_in.start()
+    cot_in = pltpu.make_async_copy(cot_hbm, cot_ref, edge_sems.at[0])
+    stream_in = pltpu.make_async_copy(stream_hbm, stream_ref, edge_sems.at[1])
+    cot_in.start()
+    stream_in.start()
+    index_in.wait()
     index = index_ref[...].astype(F32).T
     pick_ref[...] = one_hot_slots(most, device_ref[0], index, member_ref, *pick_ref.shape)
+    stream_in.wait()
     wide = stream_ref[...].astype(F32)
     inv = lax.rsqrt(jnp.mean(wide * wide, axis=1, keepdims=True) + EPS)
+    gain_in.wait()
     x_ref[...] = (wide * inv * gain_ref[...]).astype(BF16)
-    for part in send_rows(pick_ref, (x_ref, cot_ref), out_hbm, out_ref, sems):
+    cot_in.wait()
+    copies = send_rows(pick_ref, (x_ref, cot_ref), out_hbm, out_ref, sems)
+    x_out = pltpu.make_async_copy(x_ref, x_hbm, edge_sems.at[2])
+    x_out.start()
+    for part in copies + [x_out]:
         part.wait()
 
 
@@ -100,27 +117,20 @@
     experts, cap = index.shape
     experts = experts // 2
     rows = experts * most
-    whole = lambda *shape: pl.BlockSpec(shape, lambda j, side: (0, 0))
+    hbm = pl.BlockSpec(memory_space=pl.ANY)
     return pl.pallas_call(
         functools.partial(prepare_kernel, most),
-        grid_spec=pltpu.PrefetchScalarGridSpec(
-            num_scalar_prefetch=1,
-            grid=(1,),
-            in_specs=[
-                pl.BlockSpec(memory_space=pltpu.SMEM),
-                pl.BlockSpec((experts, cap), lambda j, side: (side[0], 0)),
-                whole(1, width),
-                whole(tok, width),
-                whole(tok, width),
-            ],
-            out_specs=[whole(tok, width), pl.BlockSpec(memory_space=pl.ANY)],
-            scratch_shapes=[
-                pltpu.VMEM((rows, 2 * width), BF16),
-                pltpu.VMEM((rows, tok), BF16),
-                pltpu.VMEM((experts, tok), F32),
-                pltpu.SemaphoreType.DMA((width // CHUNK,)),
-            ],
-        ),
+        in_specs=[pl.BlockSpec(memory_space=pltpu.SMEM)] * 2 + [hbm] * 4,
+        out_specs=[hbm] * 2,
+        scratch_shapes=[pltpu.VMEM((experts, cap), jnp.int32), pltpu.VMEM((1, width), F32)]
+        + [pltpu.VMEM((tok, width), BF16)] * 3
+        + [
+            pltpu.VMEM((rows, 2 * width), BF16),
+            pltpu.VMEM((rows, tok), BF16),
+            pltpu.VMEM((experts, tok), F32),
+            pltpu.SemaphoreType.DMA((width // CHUNK,)),
+            pltpu.SemaphoreType.DMA((5,)),
+        ],
         out_shape=[jax.ShapeDtypeStruct((tok, width), BF16), jax.ShapeDtypeStruct((rows, 2 * width), BF16)],
         compiler_params=params(),
         cost_estimate=cost(1, 1),
@@ -128,24 +138,48 @@
     )(side, device, index, gain, cotangent, stream)
 
 
-def pack_kernel(pick_ref, x_ref, cot_ref, out_hbm, out_ref, sems):
-    for part in send_rows(pick_ref, (x_ref, cot_ref), out_hbm, out_ref, sems):
-        part.wait()
-
-
-def pack(pick, inputs, cotangent):
-    width = inputs.shape[1]
-    shape = (pick.shape[0], 2 * width)
+def pack(pick, source, which, out=None):
+    rows, width = pick.shape[0], source.shape[1]
+    step = 2 * CHUNK
+
+    def kernel(pick_hbm, source_hbm, _, out_hbm, pick_ref, source_ref, out_ref, sems):
+        steps = width // step
+        pick_in = pltpu.make_async_copy(pick_hbm, pick_ref, sems.at[2 * steps])
+        pick_in.start()
+        loads = []
+        for j in range(0, width, step):
+            at = slice(j, j + step)
+            loads.append(pltpu.make_async_copy(source_hbm.at[:, at], source_ref.at[:, at], sems.at[steps + len(loads)]))
+            loads[-1].start()
+        pick_in.wait()
+        copies = []
+        for j in range(0, width, step):
+            at = slice(j, j + step)
+            loads[len(copies)].wait()
+            out_ref[:, at] = mm(pick_ref[...], source_ref[:, at]).astype(BF16)
+            there = out_hbm.at[:, which * width + j : which * width + j + step]
+            copies.append(pltpu.make_async_copy(out_ref.at[:, at], there, sems.at[len(copies)]))
+            copies[-1].start()
+        for part in copies:
+            part.wait()
+
+    hbm = pl.BlockSpec(memory_space=pl.ANY)
     return pl.pallas_call(
-        pack_kernel,
-        in_specs=[pl.BlockSpec(memory_space=pltpu.VMEM)] * 3,
-        out_specs=pl.BlockSpec(memory_space=pl.ANY),
-        out_shape=jax.ShapeDtypeStruct(shape, BF16),
-        scratch_shapes=[pltpu.VMEM(shape, BF16), pltpu.SemaphoreType.DMA((width // CHUNK,))],
+        kernel,
+        in_specs=[hbm] * 3,
+        out_specs=hbm,
+        out_shape=jax.ShapeDtypeStruct((rows, 2 * width), BF16),
+        scratch_shapes=[
+            pltpu.VMEM(pick.shape, BF16),
+            pltpu.VMEM(source.shape, BF16),
+            pltpu.VMEM((rows, width), BF16),
+            pltpu.SemaphoreType.DMA((2 * width // step + 1,)),
+        ],
+        input_output_aliases={} if out is None else {2: 0},
         compiler_params=params(),
         cost_estimate=cost(1, 1),
         name="pack_rows",
-    )(pick, inputs, cotangent)
+    )(pick, source, source if out is None else out)
 
 
 def streamed(work, name, scalar, ins, outs):
@@ -224,8 +258,8 @@
 
 
 def combine_kernel(
-    parity_ref, pick_ref, gain_ref, stream_hbm, back_hbm, cot_hbm, q_hbm, grad_hbm, mine_ref, other_ref,
-    stream_ref, back_ref, cot_ref, q_ref, grad_ref, normed_ref, sum_ref, sems,
+    parity_ref, pick_hbm, gain_hbm, stream_hbm, back_hbm, cot_hbm, q_hbm, grad_hbm, mine_hbm, other_hbm,
+    stream_ref, back_ref, cot_ref, q_ref, grad_ref, normed_ref, sum_ref, pick_ref, gain_ref, mine_ref, other_ref, sems,
 ):
     width = stream_ref.shape[1]
     count = iter(range(sems.shape[0]))
@@ -237,6 +271,7 @@
         return made
 
     stream_in = copy(stream_hbm, stream_ref)
+    small_in = [copy(pick_hbm, pick_ref), copy(gain_hbm, gain_ref)]
     back_in = [copy(back_hbm.at[:, at], back_ref.at[:, at]) for at in pieces]
     cot_in = copy(cot_hbm, cot_ref)
     q_in = copy(q_hbm, q_ref)
@@ -244,6 +279,8 @@
     wide = stream_ref[...].astype(F32)
     inv = lax.rsqrt(jnp.mean(wide * wide, axis=1, keepdims=True) + EPS)
     normed_ref[...] = wide * inv
+    for part in small_in:
+        part.wait()
     total = 0.0
     for part, at in zip(back_in, pieces):
         part.wait()
@@ -255,30 +292,34 @@
     for at in pieces:
         grad = cot_ref[:, at].astype(F32) + inv * (sum_ref[:, at] - normed_ref[:, at] * mean)
         grad_ref[:, at] = grad.astype(BF16)
-    grad_out = copy(grad_ref, grad_hbm)
+    out = [copy(grad_ref, grad_hbm)]
     q_in.wait()
     half = mine_ref.shape[0]
-    for state_ref, first in ((other_ref, (1 - parity_ref[0]) * half), (mine_ref, parity_ref[0] * half)):
+    sides = ((other_ref, other_hbm, (1 - parity_ref[0]) * half), (mine_ref, mine_hbm, parity_ref[0] * half))
+    for state_ref, state_hbm, first in sides:
         for h in range(half):
             at = pl.ds(pl.multiple_of((first + h) * HEAD, HEAD), HEAD)
             state_ref[h] = mm(q_ref[:, at], grad_ref[:, at], TN).astype(BF16)
-    grad_out.wait()
+        out += [copy(state_ref, state_hbm)]
+    for part in out:
+        part.wait()
 
 
 def combine(parity, pick_t, gain, stream, back, cotangent, queries):
     tok, width = stream.shape
-    vmem = pl.BlockSpec(memory_space=pltpu.VMEM)
     hbm = pl.BlockSpec(memory_space=pl.ANY)
     return pl.pallas_call(
         combine_kernel,
-        in_specs=[pl.BlockSpec(memory_space=pltpu.SMEM)] + [vmem] * 2 + [hbm] * 4,
-        out_specs=[hbm] + [vmem] * 2,
+        in_specs=[pl.BlockSpec(memory_space=pltpu.SMEM)] + [hbm] * 6,
+        out_specs=[hbm] * 3,
         out_shape=[jax.ShapeDtypeStruct((tok, width), BF16)]
         + [jax.ShapeDtypeStruct((width // HEAD // 2, HEAD, HEAD), BF16)] * 2,
         scratch_shapes=[pltpu.VMEM((tok, width), BF16), pltpu.VMEM(back.shape, BF16)]
         + [pltpu.VMEM((tok, width), BF16)] * 3
         + [pltpu.VMEM((tok, width), F32)] * 2
-        + [pltpu.SemaphoreType.DMA((width // CHUNK + 4,))],
+        + [pltpu.VMEM(pick_t.shape, BF16), pltpu.VMEM((1, width), F32)]
+        + [pltpu.VMEM((width // HEAD // 2, HEAD, HEAD), BF16)] * 2
+        + [pltpu.SemaphoreType.DMA((width // CHUNK + 8,))],
         compiler_params=params(),
         cost_estimate=cost(2 * tok * width * (back.shape[0] + HEAD), 2 * width * (back.shape[0] + 6 * tok)),
         name="combine_rows",
@@ -286,9 +327,9 @@
 
 
 def expert_kernel(
-    first_ref, gates_ref, in_hbm, wg_hbm, wu_hbm, wd_hbm, _,
-    back_hbm, ggp_hbm, gup_hbm, hid_hbm, router_ref, gain_ref,
-    in_ref, wg_ref, wu_ref, wd_ref, back_ref, ggp_ref, gup_ref, hid_ref, sems,
+    first_ref, gates_hbm, in_hbm, wg_hbm, wu_hbm, wd_hbm, _,
+    back_hbm, ggp_hbm, gup_hbm, hid_hbm, router_hbm, gain_hbm,
+    in_ref, wg_ref, wu_ref, wd_ref, back_ref, ggp_ref, gup_ref, hid_ref, gates_ref, router_ref, gain_ref, sems,
 ):
     width = wg_ref.shape[0]
     slots = in_ref.shape[0]
@@ -307,6 +348,7 @@
         loads += [copy(wu_hbm.at[at, :], wu_ref.at[at, :])]
     for at, there in zip(pieces, shifted):
         loads += [copy(in_hbm.at[:, there], in_ref.at[:, there]), copy(wd_hbm.at[:, at], wd_ref.at[:, at])]
+    gates_in = copy(gates_hbm, gates_ref)
     loads = iter(loads)
     gate_pre = up_pre = raw_hidden = 0.0
     for at in pieces:
@@ -319,6 +361,7 @@
             next(loads).wait()
         raw_hidden += mm(in_ref[:, there], wd_ref[:, at], NT)
     same = lax.broadcasted_iota(jnp.int32, (slots, slots), 0) == lax.broadcasted_iota(jnp.int32, (slots, slots), 1)
+    gates_in.wait()
     gates = jnp.sum(jnp.where(same, gates_ref[...], 0.0), axis=1, keepdims=True)
     sigmoid = 1.0 / (1.0 + jnp.exp(-gate_pre))
     silu = gate_pre * sigmoid
@@ -331,14 +374,14 @@
     hid_ref[...] = (hidden * gates).astype(BF16)
     router = jnp.sum(hidden.astype(BF16).astype(F32) * raw_hidden, axis=1, keepdims=True)
     router_ref[...] = jnp.sum(jnp.where(same, router, 0.0), axis=0, keepdims=True)
-    out += [copy(hid_ref, hid_hbm)]
+    out += [copy(hid_ref, hid_hbm), copy(router_ref, router_hbm)]
     first = pl.ds(pl.multiple_of(first_ref[0] * slots, slots), slots)
     for at in pieces:
         grad = mm(ggp_ref[...], wg_ref[at, :], NT) + mm(gup_ref[...], wu_ref[at, :], NT)
         back_ref[:, at] = grad.astype(BF16)
         out += [copy(back_ref.at[:, at], back_hbm.at[first, at])]
-    for at in pieces:
         gain_ref[:, at] = jnp.sum(back_ref[:, at].astype(F32) * in_ref[:, at].astype(F32), axis=0, keepdims=True)
+    out += [copy(gain_ref, gain_hbm)]
     for part in out:
         part.wait()
 
@@ -346,7 +389,6 @@
 def expert(first, gates, incoming, w_gate, w_up, w_down, back=None):
     slots = incoming.shape[0]
     width, inner = w_gate.shape
-    vmem = pl.BlockSpec(memory_space=pltpu.VMEM)
     hbm = pl.BlockSpec(memory_space=pl.ANY)
     small = [(slots, inner)] * 3
     held = [incoming.shape, w_gate.shape, w_up.shape, w_down.shape, (slots, width)] + small
@@ -355,11 +397,13 @@
         back = gates
     return pl.pallas_call(
         expert_kernel,
-        in_specs=[pl.BlockSpec(memory_space=pltpu.SMEM), vmem] + [hbm] * 5,
-        out_specs=[hbm] * 4 + [vmem] * 2,
+        in_specs=[pl.BlockSpec(memory_space=pltpu.SMEM)] + [hbm] * 6,
+        out_specs=[hbm] * 6,
         out_shape=[jax.ShapeDtypeStruct(shape, BF16) for shape in [(2 * slots, width)] + small]
         + [jax.ShapeDtypeStruct((1, slots), F32), jax.ShapeDtypeStruct((1, width), F32)],
-        scratch_shapes=[pltpu.VMEM(shape, BF16) for shape in held] + [pltpu.SemaphoreType.DMA((6 * width // CHUNK + 3,))],
+        scratch_shapes=[pltpu.VMEM(shape, BF16) for shape in held]
+        + [pltpu.VMEM((1, size), F32) for size in (slots, slots, width)]
+        + [pltpu.SemaphoreType.DMA((6 * width // CHUNK + 6,))],
         input_output_aliases=alias,
         compiler_params=params(),
         cost_estimate=cost(10 * slots * width * inner, 6 * width * (inner + slots)),
@@ -367,31 +411,38 @@
     )(first, gates, incoming, w_gate, w_up, w_down, back)
 
 
-def total(value):
+def add_across(value, bit):
     count = lax.axis_size("grp") * lax.axis_size("seq")
-    if count & (count - 1):
-        return lax.psum(value, AXES)
-    for b in range(count.bit_length() - 1):
-        value = value + lax.ppermute(value, AXES, [(i, i ^ (1 << b)) for i in range(count)])
-    return value
-
-
-def local_part(scale, parity, queries, keys, values, grad, mix, prior):
+    return value + lax.ppermute(value, AXES, [(i, i ^ bit) for i in range(count)])
+
+
+def query_part(scale, parity, keys, values, grad, prior):
+    tok, width = keys.shape
+
+    def work(_, h, at, ins, outs):
+        k_ref, v_ref, g_ref, prior_ref = ins
+        row, col = triangle(tok)
+        g = g_ref[:, at]
+        mix_a = jnp.where(row >= col, mm(g, v_ref[:, at], NT), 0.0).astype(BF16)
+        outs[0][:, at] = (scale * (mm(mix_a, k_ref[:, at]) + mm(g, prior_ref[h], NT))).astype(BF16)
+
+    outs = [jax.ShapeDtypeStruct((tok, width), BF16)]
+    return streamed(work, "query_attention", parity, [keys, values, grad, prior], outs)
+
+
+def local_part(parity, queries, values, grad, mix):
     tok, width = queries.shape
 
     def work(_, h, at, ins, outs):
-        q_ref, k_ref, v_ref, g_ref, mix_ref, prior_ref = ins
-        gq_ref, pk_ref, pv_ref = outs
+        q_ref, v_ref, g_ref, mix_ref = ins
         row, col = triangle(tok)
-        k, v, g = k_ref[:, at], v_ref[:, at], g_ref[:, at]
-        mix_a = jnp.where(row >= col, mm(g, v, NT), 0.0).astype(BF16)
-        mix_t = jnp.where(row <= col, mm(v, g, NT), 0.0).astype(BF16)
-        gq_ref[:, at] = (scale * (mm(mix_a, k) + mm(g, prior_ref[h], NT))).astype(BF16)
-        pk_ref[:, at] = mm(mix_t, q_ref[:, at]).astype(BF16)
-        pv_ref[:, at] = mm(mix_ref[:, at], g).astype(BF16)
-
-    outs = [jax.ShapeDtypeStruct((tok, width), BF16)] * 3
-    return streamed(work, "local_attention", parity, [queries, keys, values, grad, mix, prior], outs)
+        g = g_ref[:, at]
+        mix_t = jnp.where(row <= col, mm(v_ref[:, at], g, NT), 0.0).astype(BF16)
+        outs[0][:, at] = mm(mix_t, q_ref[:, at]).astype(BF16)
+        outs[1][:, at] = mm(mix_ref[:, at], g).astype(BF16)
+
+    outs = [jax.ShapeDtypeStruct((tok, width), BF16)] * 2
+    return streamed(work, "local_attention", parity, [queries, values, grad, mix], outs)
 
 
 def last_part(scale, parity, keys, values, pk, pv, own, other):
@@ -424,12 +475,13 @@
     rising_sum, falling_base = both[:quarter], both[quarter:]
     rising = jnp.zeros_like(rising_sum)
     falling = jnp.zeros_like(falling_base)
-    beside_out = None
+    beside_out = []
     for up, down in zip(bits, reversed(bits)):
         got_up = swap(rising_sum, up)
         got_down = swap(falling + jnp.where((place & down) == 0, 0.0, falling_base), down)
-        if beside is not None and beside_out is None:
-            got_up, got_down, beside_out = lax.optimization_barrier((got_up, got_down, beside()))
+        if beside:
+            got_up, got_down, done = lax.optimization_barrier((got_up, got_down, beside.pop(0)(rising_sum)))
+            beside_out.append(done)
         got_up, got_down = got_up.astype(F32), got_down.astype(F32)
         rising = rising + jnp.where((place & up) == 0, got_up, 0.0)
         rising_sum = rising_sum + got_up
@@ -437,7 +489,7 @@
     own = jnp.concatenate([rising, falling])
     theirs = swap(own + jnp.where(parity == 1, mine, 0.0), 1)
     own = (own + jnp.where(parity == 0, partner, 0.0)).astype(BF16)
-    return own, theirs, beside_out
+    return own, theirs, beside_out + [work(rising_sum) for work in beside]
 
 
 def body(
@@ -480,16 +532,6 @@
     far_cot = lax.ppermute(cotangent, AXES, swap)
     far_inputs = lax.ppermute(inputs, AXES, swap)
 
-    key_states, mix_b = early(parity, queries, key_vectors, value_vectors)
-    heads = width // HEAD
-    place = lax.axis_index("seq")
-    own_prior, other_prior, _ = states_beyond(
-        seq_count - 1 - place, key_states[: heads // 2], key_states[heads // 2 :], None
-    )
-    is_low = parity[0] == 0
-    prior = jnp.concatenate(
-        [jnp.where(is_low, own_prior, other_prior), jnp.where(is_low, other_prior, own_prior)]
-    )
     pick_t = picks(most, tok, here_array, expert_index).T
     half_index = lax.dynamic_slice_in_dim(expert_index, side * (experts // 2), experts // 2, 0)
     far_pick = picks(most, tok, there_array, half_index)
@@ -500,25 +542,40 @@
     arrival = jnp.where(source // halves == side, source % halves, halves + source % halves) * most + before
     place_t = arrival[None, :] == jnp.arange(dev_count * most)[:, None]
     slot_gates = jnp.sum(jnp.where(place_t, router_gates, 0.0), axis=1).reshape(2, 1, halves * most)
-    far_cot, far_inputs, mix_b, pick_t, far_pick, slot_gates, prior = lax.optimization_barrier(
-        (far_cot, far_inputs, mix_b, pick_t, far_pick, slot_gates, prior)
-    )
-    far_out = pack(far_pick, far_inputs, far_cot)
+    far_out = pack(far_pick, far_cot, 1)
+    far_inputs, far_out, pick_t, slot_gates = lax.optimization_barrier((far_inputs, far_out, pick_t, slot_gates))
+    far_out = pack(far_pick, far_inputs, 0, far_out)
     far = exchange(far_out)
 
-    own, far_out = lax.optimization_barrier((own, far_out))
+    own, far_out, q_early, k_early, v_early = lax.optimization_barrier(
+        (own, far_out, queries, key_vectors, value_vectors)
+    )
+    key_states, mix_b = early(parity, q_early, k_early, v_early)
     back, own_ggp, own_gup, own_hidden, own_router, own_gain = expert(
         side_array, slot_gates[0], own, w_gate, w_up, w_down
     )
-    far, back = lax.optimization_barrier((far, back))
+    far, back, key_states, mix_b = lax.optimization_barrier((far, back, key_states, mix_b))
     back, far_ggp, far_gup, far_hidden, far_router, far_gain = expert(
         1 - side_array, slot_gates[1], far, w_gate, w_up, w_down, back
     )
     returned = lax.all_to_all(back, AXES, split_axis=0, concat_axis=0, tiled=True)
 
-    gain_total = total((own_gain + far_gain) / gain)
+    heads = width // HEAD
+    place = lax.axis_index("seq")
+    own_prior, other_prior, _ = states_beyond(
+        seq_count - 1 - place, key_states[: heads // 2], key_states[heads // 2 :], []
+    )
+    is_low = parity[0] == 0
+    prior = jnp.concatenate(
+        [jnp.where(is_low, own_prior, other_prior), jnp.where(is_low, other_prior, own_prior)]
+    )
     own, far, far_ggp, back = lax.optimization_barrier((own, far, far_ggp, back))
     arrived = jnp.concatenate([own, far])
+    arrived, own_gain, far_gain = lax.optimization_barrier((arrived, own_gain, far_gain))
+    gain_total = (own_gain + far_gain) / gain
+    bits = [1 << b for b in range(dev_count.bit_length() - 1)]
+    for bit in bits[:-2]:
+        gain_total = add_across(gain_total, bit)
     rows, dy_rows = arrived[:, :width], arrived[:, width:]
     grad_gate_pre = jnp.concatenate([own_ggp, far_ggp])
     grad_up_pre = jnp.concatenate([own_gup, far_gup])
@@ -528,14 +585,27 @@
     grad_down = lax.dot_general(hidden, dy_rows, TN, preferred_element_type=F32).astype(BF16)
     slot_router = jnp.concatenate([own_router, far_router], axis=1).reshape(dev_count * most, 1)
     router = jnp.sum(jnp.where(place_t, slot_router, 0.0), axis=0, keepdims=True)
-    returned, grad_gate, grad_up, grad_down, router, gain_total = lax.optimization_barrier(
-        (returned, grad_gate, grad_up, grad_down, router, gain_total)
+    returned, grad_gate, grad_up, grad_down, router, gain_total, prior, mix_b = lax.optimization_barrier(
+        (returned, grad_gate, grad_up, grad_down, router, gain_total, prior, mix_b)
     )
 
     grad_stream, mine, other = combine(parity, pick_t, gain, stream, returned, cotangent, queries)
-    local = lambda: local_part(scale, parity, queries, key_vectors, value_vectors, grad_stream, mix_b, prior)
-    own_state, other_state, done = states_beyond(place, mine, other, local)
-    grad_queries, part_k, part_v = done
+
+    gain_across = [(i, i ^ bits[-1]) for i in range(dev_count)]
+    gain_sums = [gain_total]
+
+    def first(_):
+        gain_sums.append(add_across(gain_total, bits[-2]))
+        return local_part(parity, queries, value_vectors, grad_stream, mix_b), gain_sums[-1]
+
+    def second(after):
+        grad, _ = lax.optimization_barrier((grad_stream, after))
+        done = query_part(scale, parity, key_vectors, value_vectors, grad, prior)
+        return done, lax.ppermute(gain_sums[-1], AXES, gain_across)
+
+    own_state, other_state, done = states_beyond(place, mine, other, [first, second])
+    ((part_k, part_v), gain_total), ((grad_queries,), gain_other) = done
+    gain_total += gain_other
     grad_keys, grad_values = last_part(
         scale, parity, key_vectors, value_vectors, part_k, part_v, own_state, other_state
     )

time: 202 us -> 195 us (0.965)
  local copies, waits for them, and re-layouts: 8.96 us -> 5.18 us
  starting transfers between devices: 40.2 us -> 37.8 us
    ppermute x1, waiting for transfers between devices: 0.01 us -> 26.2 us  [body(): far_cot = lax.ppermute(cotangent, AXES, swap)]
    ppermute x5, waiting for transfers between devices: 24.7 us -> 4.99 us  [the longest x4 4.99 us: add_across(): lax.ppermute(value, AXES, [(i, i ^ bit) for i in range(count)])]
    ppermute x5, starting transfers between devices: 9.01 us -> 3.54 us  [the longest x4 2.05 us: add_across(): lax.ppermute(value, AXES, [(i, i ^ bit) for i in range(count)])]
    all_to_all x1, waiting for transfers between devices: 0.01 us -> 5.4 us  [body(): lax.all_to_all(back, AXES, split_axis=0, concat_axis=0, tiled=True)]
    all_to_all x2, starting transfers between devices: 11.3 us -> 16.1 us  [exchange(): lax.all_to_all(value, AXES, split_axis=0, concat_axis=0, tiled=True, axis...]
    ppermute x12, waiting for transfers between devices: 21.9 us -> 17.2 us  [swap(): lax.ppermute(value.astype(BF16), 'seq', [(i, i ^ bit) for i in range(coun...]
    ppermute x1, waiting for transfers between devices: 11.8 us -> 7.86 us  [body(): far_inputs = lax.ppermute(inputs, AXES, swap)]
    convert_element_type x5, other arithmetic: 5.42 us -> 2.44 us  [swap(): value.astype(BF16)]
  transfers between devices with their start and end apart: 22 -> 22, of which waited for: 11 -> 12; matrix products, arithmetic and copies ran while one was open for 13% -> 10% of each run, Pallas kernels for 13% -> 20%
where the time goes in v4:
time: 195 us
  waiting for transfers between devices  78.3 us (40%)
  Pallas kernels  49.7 us (25%)
  starting transfers between devices  37.8 us (19%)
  other arithmetic  11.9 us (6%)
  matrix products  10.5 us (5%)
  local copies, waits for them, and re-layouts  5.18 us (3%)
    ppermute x1, waiting for transfers between devices, body(): far_cot = lax.ppermute(cotangent, AXES, swap)  26.2 us
    pallas_call x2, Pallas kernels, expert(): pl.pallas_call(expert_kernel, in_specs=[pl.BlockSpec(memory_space=pltpu.S...  17.6 us
    ppermute x12, waiting for transfers between devices, swap(): lax.ppermute(value.astype(BF16), 'seq', [(i, i ^ bit) for i in range(coun...  17.2 us
    all_to_all x2, waiting for transfers between devices, exchange(): lax.all_to_all(value, AXES, split_axis=0, concat_axis=0, tiled=True, axis...  16.7 us
    all_to_all x2, starting transfers between devices, exchange(): lax.all_to_all(value, AXES, split_axis=0, concat_axis=0, tiled=True, axis...  16.1 us
    pallas_call x4, Pallas kernels, streamed(): pl.pallas_call(kernel, in_specs=[pl.BlockSpec(memory_space=pltpu.SMEM)] +...  14.1 us
    ppermute x12, starting transfers between devices, swap(): lax.ppermute(value.astype(BF16), 'seq', [(i, i ^ bit) for i in range(coun...  11.1 us
    ppermute x1, waiting for transfers between devices, body(): far_inputs = lax.ppermute(inputs, AXES, swap)  7.86 us
  transfers between devices with their start and end apart: 22, of which 12 were waited for; matrix products, arithmetic and copies ran while one was open for 10% of the time, Pallas kernels for 20%

profile of v4, /device:TPU:0, one launch (start us, length us, event | category | flops | bytes accessed | tf_op | source)
XLA Modules:
  0.0 194.7 jit_solution(7336574276714518614)
XLA Ops:
  0.7 3.8 %prepare_rows.1 = (bf16[128,2048]{1,0:T(8,128)(2,1)}, bf16[256,4096]{1,0:T(8,128)(2,1)}) custom-call(s32[1]{0:T(128)} %bitcast.1.half_ref.first_ref, s32[1]{0:T(128)} %bitcast.2.device_ref, s32[32,256]{1,0:T(8,128)} %index_ref.1, f32[1,2048]{1,0:T(1,128)} %bitcast.35, bf16[128,2048]{1,0:T(8,128)(2,1)} %cot_hbm.3, bf16[128,2048]{1,0:T(8,128)(2,1)} %stream_hbm.3), custom_call_target="tpu_custom_call" | custom-call | flops 1 | bytes 1 | tf_op jit(solution)/shard_map/prepare_rows/pallas_call | solution.py:121
  4.5 6.3 %all-to-all-start.1 = ((bf16[16,16,4096]{2,1,0:T(8,128)(2,1)}), bf16[16,16,4096]{2,1,0:T(8,128)(2,1)}, u32[]{:S(2)}, u32[]{:S(2)}) async-start(bf16[16,16,4096]{2,1,0:T(8,128)(2,1)} %bitcast.32), calls=%async_computation.1 | async-start | bytes 4194304 | tf_op jit(solution)/shard_map/all_to_all | solution.py:528
  10.8 2.7 %collective-permute-start.1 = (bf16[128,2048]{1,0:T(8,128)(2,1)}, bf16[128,2048]{1,0:T(8,128)(2,1)S(1)}, u32[]{:S(2)}, u32[]{:S(2)}) collective-permute-start(bf16[128,2048]{1,0:T(8,128)(2,1)} %cot_hbm.3), channel_id=1, source_target_pairs={{0,16},{1,17},{2,18},{3,19},{4,20},{5,21},{6,22},{7,23},{8,24},{9,... | collective-permute-start | bytes 1572872 | tf_op jit(solution)/shard_map/ppermute | solution.py:532
  14.5 3.1 %pick_slots.3 = bf16[512,128]{1,0:T(8,128)(2,1)} custom-call(s32[1]{0:T(128)} %bitcast.2.device_ref, s32[32,256]{1,0:T(8,128)} %index_ref.1), custom_call_target="tpu_custom_call" | custom-call | flops 1 | bytes 1 | tf_op jit(solution)/shard_map/pick_slots/pallas_call | solution.py:61
  22.0 26.2 %collective-permute-done.1.source_hbm._ = bf16[128,2048]{1,0:T(8,128)(2,1)S(1)} collective-permute-done((bf16[128,2048]{1,0:T(8,128)(2,1)}, bf16[128,2048]{1,0:T(8,128)(2,1)S(1)}, u32[]{:S(2)}, u32[]{:S(2)}) %collective-permute-start.1) | collective-permute-done | bytes 524320 | tf_op jit(solution)/shard_map/ppermute | solution.py:532
  51.3 7.9 %collective-permute-done.source_hbm = bf16[128,2048]{1,0:T(8,128)(2,1)} collective-permute-done((bf16[128,2048]{1,0:T(8,128)(2,1)}, bf16[128,2048]{1,0:T(8,128)(2,1)}, u32[]{:S(2)}, u32[]{:S(2)}) %collective-permute-start) | collective-permute-done | bytes 524320 | tf_op jit(solution)/shard_map/ppermute | solution.py:533
  61.6 9.7 %all-to-all-start = ((bf16[16,16,4096]{2,1,0:T(8,128)(2,1)}), bf16[16,16,4096]{2,1,0:T(8,128)(2,1)}, u32[]{:S(2)}, u32[]{:S(2)}) async-start(bf16[16,16,4096]{2,1,0:T(8,128)(2,1)} %bitcast.31), calls=%async_computation | async-start | bytes 4194304 | tf_op jit(solution)/shard_map/all_to_all | solution.py:528
  71.9 3.3 %early_states.1 = (bf16[16,128,128]{2,1,0:T(8,128)(2,1)}, bf16[128,2048]{1,0:T(8,128)(2,1)}) custom-call(s32[1]{0:T(128)} %bitcast.refs_0_.parity_ref, bf16[128,2048]{1,0:T(8,128)(2,1)} %refs_1_.4, bf16[128,2048]{1,0:T(8,128)(2,1)} %refs_1_.6, bf16[128,2048]{1,0:T(8,128)(2,1)} %refs_2_.6), custom_call_target="tpu_custom_call" | custom-call | flops 1 | bytes 1 | tf_op jit(solution)/shard_map/early_states/pallas_call | solution.py:226
  75.2 8.8 %expert_rows.2 = (bf16[512,2048]{1,0:T(8,128)(2,1)}, bf16[256,768]{1,0:T(8,128)(2,1)}, bf16[256,768]{1,0:T(8,128)(2,1)}, bf16[256,768]{1,0:T(8,128)(2,1)}, f32[1,256]{1,0:T(1,128)}, /*index=5*/f32[1,2048]{1,0:T(1,128)}) custom-call(s32[1]{0:T(128)} %bitcast.1.half_ref.first_ref, f32[1,256]{1,0:T(1,128)} %get-tuple-element.139.gates_hbm._, ...), custom_call_target="tpu_custom_call" | custom-call | flops 4026531840 | bytes 12582912 | tf_op jit(solution)/shard_map/expert_rows/pallas_call | solution.py:398
  84.0 16.7 %all-to-all-done = bf16[16,16,4096]{2,1,0:T(8,128)(2,1)} async-done(((bf16[16,16,4096]{2,1,0:T(8,128)(2,1)}), bf16[16,16,4096]{2,1,0:T(8,128)(2,1)}, u32[]{:S(2)}, u32[]{:S(2)}) %all-to-all-start) | async-done | bytes 2097184 | tf_op jit(solution)/shard_map/all_to_all | solution.py:528
  101.4 8.8 %expert_rows.3 = (bf16[512,2048]{1,0:T(8,128)(2,1)}, bf16[256,768]{1,0:T(8,128)(2,1)}, bf16[256,768]{1,0:T(8,128)(2,1)}, bf16[256,768]{1,0:T(8,128)(2,1)}, f32[1,256]{1,0:T(1,128)}, /*index=5*/f32[1,2048]{1,0:T(1,128)}) custom-call(s32[1]{0:T(128)S(6)} %sub.26.first_ref, f32[1,256]{1,0:T(1,128)} %get-tuple-element.140.gates_hbm, ...), custom_call_target="tpu_custom_call", output_to_operand_aliasing={{0}: (6, {})} | custom-call | flops 4026531840 | bytes 12582912 | tf_op jit(solution)/shard_map/expert_rows/pallas_call | solution.py:398
  110.2 4.1 %all-to-all-start.2 = ((bf16[32,16,2048]{2,1,0:T(8,128)(2,1)}), bf16[32,16,2048]{2,1,0:T(8,128)(2,1)}, u32[]{:S(2)}, u32[]{:S(2)}) async-start(bf16[32,16,2048]{2,1,0:T(8,128)(2,1)} %bitcast.33), calls=%async_computation.2 | async-start | bytes 4194304 | tf_op jit(solution)/shard_map/all_to_all | solution.py:561
  114.4 2.8 %pad_maximum_fusion = bf16[512,4096]{1,0:T(8,128)(2,1)S(1)} fusion(bf16[256,4096]{1,0:T(8,128)(2,1)} %bitcast.14.in_hbm, bf16[256,4096]{1,0:T(8,128)(2,1)} %bitcast.17.in_hbm), kind=kLoop, calls=%fused_computation | loop fusion | flops 8388608 | bytes 8388608 | tf_op jit(solution)/shard_map/concatenate | solution.py:573
  120.9 3.5 %convolution_convert_fusion.1 = bf16[2048,768]{1,0:T(8,128)(2,1)} fusion(bf16[512,4096]{1,0:T(8,128)(2,1)S(1)} %pad_maximum_fusion, bf16[256,768]{1,0:T(8,128)(2,1)S(1)} %copy-done.15, bf16[256,768]{1,0:T(8,128)(2,1)S(1)} %copy-done.18), kind=kOutput, calls=%fused_computation.2 | convolution fusion | flops 1613758464 | bytes 6029312 | tf_op jit(solution)/shard_map/dot_general | solution.py:584
  124.4 8.5 %collective-permute-done.6 = bf16[4,128,128]{2,1,0:T(8,128)(2,1)S(1)} collective-permute-done((bf16[4,128,128]{2,1,0:T(8,128)(2,1)S(1)}, bf16[4,128,128]{2,1,0:T(8,128)(2,1)S(1)}, u32[]{:S(2)}, u32[]{:S(2)}) %collective-permute-start.6) | collective-permute-done | bytes 131104 | tf_op jit(solution)/shard_map/ppermute | solution.py:468
  133.7 3.5 %convolution_convert_fusion.2 = bf16[2048,768]{1,0:T(8,128)(2,1)} fusion(bf16[512,4096]{1,0:T(8,128)(2,1)S(1)} %pad_maximum_fusion, bf16[256,768]{1,0:T(8,128)(2,1)S(1)} %copy-done.14, bf16[256,768]{1,0:T(8,128)(2,1)S(1)} %copy-done.17), kind=kOutput, calls=%fused_computation.3 | convolution fusion | flops 1613758464 | bytes 6029312 | tf_op jit(solution)/shard_map/dot_general | solution.py:583
  141.6 3.8 %collective-permute-done.9 = bf16[4,128,128]{2,1,0:T(8,128)(2,1)S(1)} collective-permute-done((bf16[4,128,128]{2,1,0:T(8,128)(2,1)S(1)}, bf16[4,128,128]{2,1,0:T(8,128)(2,1)S(1)}, u32[]{:S(2)}, u32[]{:S(2)}) %collective-permute-start.9) | collective-permute-done | bytes 131104 | tf_op jit(solution)/shard_map/ppermute | solution.py:468
  145.6 3.5 %convolution_convert_fusion = bf16[768,2048]{1,0:T(8,128)(2,1)} fusion(bf16[512,4096]{1,0:T(8,128)(2,1)S(1)} %pad_maximum_fusion, bf16[256,768]{1,0:T(8,128)(2,1)S(1)} %copy-done.13, bf16[256,768]{1,0:T(8,128)(2,1)S(1)} %copy-done.16), kind=kOutput, calls=%fused_computation.1 | convolution fusion | flops 1613758464 | bytes 6029312 | tf_op jit(solution)/shard_map/dot_general | solution.py:585
  150.2 2.7 %collective-permute-done.3 = f32[1,2048]{1,0:T(1,128)S(1)} collective-permute-done((f32[1,2048]{1,0:T(1,128)S(1)}, f32[1,2048]{1,0:T(1,128)S(1)}, u32[]{:S(2)}, u32[]{:S(2)}) %collective-permute-start.3) | collective-permute-done | bytes 8224 | tf_op jit(solution)/shard_map/ppermute | solution.py:416
  157.7 5.4 %all-to-all-done.2 = bf16[32,16,2048]{2,1,0:T(8,128)(2,1)} async-done(((bf16[32,16,2048]{2,1,0:T(8,128)(2,1)}), bf16[32,16,2048]{2,1,0:T(8,128)(2,1)}, u32[]{:S(2)}, u32[]{:S(2)}) %all-to-all-start.2) | async-done | bytes 2097184 | tf_op jit(solution)/shard_map/all_to_all | solution.py:561
  163.1 4.0 %combine_rows.1 = (bf16[128,2048]{1,0:T(8,128)(2,1)}, bf16[8,128,128]{2,1,0:T(8,128)(2,1)}, bf16[8,128,128]{2,1,0:T(8,128)(2,1)}) custom-call(s32[1]{0:T(128)} %bitcast.refs_0_.parity_ref, bf16[128,512]{1,0:T(8,128)(2,1)} %bitcast.34, f32[1,2048]{1,0:T(1,128)} %bitcast.36, bf16[128,2048]{1,0:T(8,128)(2,1)} %stream_hbm.3, ...), custom_call_target="tpu_custom_call" | custom-call | flops 335544320 | bytes 5242880 | tf_op jit(solution)/shard_map/combine_rows/pallas_call | solution.py:311
  173.5 3.7 %local_attention.1 = (bf16[128,2048]{1,0:T(8,128)(2,1)}, bf16[128,2048]{1,0:T(8,128)(2,1)}) custom-call(s32[1]{0:T(128)} %bitcast.refs_0_.parity_ref, bf16[128,2048]{1,0:T(8,128)(2,1)} %refs_1_.4, bf16[128,2048]{1,0:T(8,128)(2,1)} %refs_2_.6, bf16[128,2048]{1,0:T(8,128)(2,1)} %get-tuple-element.112.refs_3_, bf16[128,2048]{1,0:T(8,128)(2,1)} %get-tuple-element.106.refs_4_), custom_call_target="tpu_custom_call" | custom-call | flops 1 | bytes 1 | tf_op jit(solution)/shard_map/local_attention/pallas_call | solution.py:226
  183.2 3.9 %query_attention.1 = bf16[128,2048]{1,0:T(8,128)(2,1)} custom-call(s32[1]{0:T(128)} %bitcast.refs_0_.parity_ref, bf16[128,2048]{1,0:T(8,128)(2,1)} %refs_1_.6, bf16[128,2048]{1,0:T(8,128)(2,1)} %refs_2_.6, bf16[128,2048]{1,0:T(8,128)(2,1)} %get-tuple-element.112.refs_3_, bf16[16,128,128]{2,1,0:T(8,128)(2,1)} %pad_maximum_fusion.2.refs_4_), custom_call_target="tpu_custom_call" | custom-call | flops 1 | bytes 1 | tf_op jit(solution)/shard_map/query_attention/pallas_call | solution.py:226
  191.3 3.2 %last_attention.1 = (bf16[128,2048]{1,0:T(8,128)(2,1)}, bf16[128,2048]{1,0:T(8,128)(2,1)}) custom-call(s32[1]{0:T(128)} %bitcast.refs_0_.parity_ref, bf16[128,2048]{1,0:T(8,128)(2,1)} %refs_1_.6, bf16[128,2048]{1,0:T(8,128)(2,1)} %refs_2_.6, bf16[128,2048]{1,0:T(8,128)(2,1)} %get-tuple-element.115.refs_3_, bf16[128,2048]{1,0:T(8,128)(2,1)} %get-tuple-element.116.refs_4_, ...), custom_call_target="tpu_custom_call" | custom-call | flops 1 | bytes 1 | tf_op jit(solution)/shard_map/last_attention/pallas_call | solution.py:226
  (106 shorter events, 43.6 us)
Async XLA Ops:
  0.7 21.2 %copy-start.10 = (f32[1,256]{1,0:T(1,128)S(1)}, f32[1,256]{1,0:T(1,128)}, u32[]{:S(2)}) copy-start(f32[1,256]{1,0:T(1,128)} %param.18) | copy-start | bytes 3076
  4.5 57.1 %all-to-all-start.1 = ((bf16[16,16,4096]{2,1,0:T(8,128)(2,1)}), bf16[16,16,4096]{2,1,0:T(8,128)(2,1)}, u32[]{:S(2)}, u32[]{:S(2)}) async-start(bf16[16,16,4096]{2,1,0:T(8,128)(2,1)} %bitcast.32), calls=%async_computation.1 | async-start | bytes 4194304 | tf_op jit(solution)/shard_map/all_to_all | solution.py:528
  10.8 37.3 %collective-permute-start.1 = (bf16[128,2048]{1,0:T(8,128)(2,1)}, bf16[128,2048]{1,0:T(8,128)(2,1)S(1)}, u32[]{:S(2)}, u32[]{:S(2)}) collective-permute-start(bf16[128,2048]{1,0:T(8,128)(2,1)} %cot_hbm.3), channel_id=1, source_target_pairs={{0,16},{1,17},{2,18},{3,19},{4,20},{5,21},{6,22},{7,23},{8,24},{9,... | collective-permute-start | bytes 1572872 | tf_op jit(solution)/shard_map/ppermute | solution.py:532
  13.5 45.7 %collective-permute-start = (bf16[128,2048]{1,0:T(8,128)(2,1)}, bf16[128,2048]{1,0:T(8,128)(2,1)}, u32[]{:S(2)}, u32[]{:S(2)}) collective-permute-start(bf16[128,2048]{1,0:T(8,128)(2,1)} %get-tuple-element.68), channel_id=1, source_target_pairs={{0,16},{1,17},{2,18},{3,19},{4,20},{5,21},{6,22},{7,23},{8,24},{9,... | collective-permute-start | bytes 1572872 | tf_op jit(solution)/shard_map/ppermute | solution.py:533
  61.6 39.1 %all-to-all-start = ((bf16[16,16,4096]{2,1,0:T(8,128)(2,1)}), bf16[16,16,4096]{2,1,0:T(8,128)(2,1)}, u32[]{:S(2)}, u32[]{:S(2)}) async-start(bf16[16,16,4096]{2,1,0:T(8,128)(2,1)} %bitcast.31), calls=%async_computation | async-start | bytes 4194304 | tf_op jit(solution)/shard_map/all_to_all | solution.py:528
  75.2 25.5 %copy-start.1 = (bf16[16,128,128]{2,1,0:T(8,128)(2,1)S(1)}, bf16[16,128,128]{2,1,0:T(8,128)(2,1)}, u32[]{:S(2)}) copy-start(bf16[16,128,128]{2,1,0:T(8,128)(2,1)} %get-tuple-element.100) | copy-start | bytes 1572868
  101.4 16.1 %collective-permute-start.5 = (bf16[8,128,128]{2,1,0:T(8,128)(2,1)}, bf16[8,128,128]{2,1,0:T(8,128)(2,1)S(1)}, u32[]{:S(2)}, u32[]{:S(2)}) collective-permute-start(bf16[8,128,128]{2,1,0:T(8,128)(2,1)} %slice.35), channel_id=1, source_target_pairs={{0,1},{1,0},{2,3},{3,2},{4,5},{5,4},{6,7},{7,6},{8,9},{9,8},{10,11... | collective-permute-start | bytes 786440 | tf_op jit(solution)/shard_map/ppermute | solution.py:468
  110.2 52.9 %all-to-all-start.2 = ((bf16[32,16,2048]{2,1,0:T(8,128)(2,1)}), bf16[32,16,2048]{2,1,0:T(8,128)(2,1)}, u32[]{:S(2)}, u32[]{:S(2)}) async-start(bf16[32,16,2048]{2,1,0:T(8,128)(2,1)} %bitcast.33), calls=%async_computation.2 | async-start | bytes 4194304 | tf_op jit(solution)/shard_map/all_to_all | solution.py:561
  117.2 31.9 %collective-permute-start.2 = (f32[1,2048]{1,0:T(1,128)S(1)}, f32[1,2048]{1,0:T(1,128)S(1)}, u32[]{:S(2)}, u32[]{:S(2)}) collective-permute-start(f32[1,2048]{1,0:T(1,128)S(1)} %add_divide_fusion), channel_id=1, source_target_pairs={{0,1},{1,0},{2,3},{3,2},{4,5},{5,4},{6,7},{7,6},{8,9},{9,8},{10,11... | collective-permute-start | bytes 24584 | tf_op jit(solution)/shard_map/ppermute | solution.py:416
  117.6 15.3 %collective-permute-start.6 = (bf16[4,128,128]{2,1,0:T(8,128)(2,1)S(1)}, bf16[4,128,128]{2,1,0:T(8,128)(2,1)S(1)}, u32[]{:S(2)}, u32[]{:S(2)}) collective-permute-start(bf16[4,128,128]{2,1,0:T(8,128)(2,1)S(1)} %get-tuple-element.137), channel_id=1, source_target_pairs={{0,2},{1,3},{2,0},{3,1},{4,6},{5,7},{6,4},{7,5},{8,10},{9,11},{10,... | collective-permute-start | bytes 393224 | tf_op jit(solution)/shard_map/ppermute | solution.py:468
  119.3 13.5 %collective-permute-start.8 = (bf16[4,128,128]{2,1,0:T(8,128)(2,1)S(1)}, bf16[4,128,128]{2,1,0:T(8,128)(2,1)S(1)}, u32[]{:S(2)}, u32[]{:S(2)}) collective-permute-start(bf16[4,128,128]{2,1,0:T(8,128)(2,1)S(1)} %get-tuple-element.138), channel_id=1, source_target_pairs={{0,4},{1,5},{2,6},{3,7},{4,0},{5,1},{6,2},{7,3},{8,12},{9,13},{10,... | collective-permute-start | bytes 393224 | tf_op jit(solution)/shard_map/ppermute | solution.py:468
  132.9 8.6 %collective-permute-start.7 = (bf16[4,128,128]{2,1,0:T(8,128)(2,1)S(1)}, bf16[4,128,128]{2,1,0:T(8,128)(2,1)S(1)}, u32[]{:S(2)}, u32[]{:S(2)}) collective-permute-start(bf16[4,128,128]{2,1,0:T(8,128)(2,1)S(1)} %get-tuple-element.135), channel_id=1, source_target_pairs={{0,4},{1,5},{2,6},{3,7},{4,0},{5,1},{6,2},{7,3},{8,12},{9,13},{10,... | collective-permute-start | bytes 393224 | tf_op jit(solution)/shard_map/ppermute | solution.py:468
  137.2 8.1 %collective-permute-start.9 = (bf16[4,128,128]{2,1,0:T(8,128)(2,1)S(1)}, bf16[4,128,128]{2,1,0:T(8,128)(2,1)S(1)}, u32[]{:S(2)}, u32[]{:S(2)}) collective-permute-start(bf16[4,128,128]{2,1,0:T(8,128)(2,1)S(1)} %get-tuple-element.136), channel_id=1, source_target_pairs={{0,2},{1,3},{2,0},{3,1},{4,6},{5,7},{6,4},{7,5},{8,10},{9,11},{10,... | collective-permute-start | bytes 393224 | tf_op jit(solution)/shard_map/ppermute | solution.py:468
  145.5 11.2 %collective-permute-start.10 = (bf16[8,128,128]{2,1,0:T(8,128)(2,1)S(1)}, bf16[8,128,128]{2,1,0:T(8,128)(2,1)S(1)}, u32[]{:S(2)}, u32[]{:S(2)}) collective-permute-start(bf16[8,128,128]{2,1,0:T(8,128)(2,1)S(1)} %fusion.13), channel_id=1, source_target_pairs={{0,1},{1,0},{2,3},{3,2},{4,5},{5,4},{6,7},{7,6},{8,9},{9,8},{10,11... | collective-permute-start | bytes 786440 | tf_op jit(solution)/shard_map/ppermute | solution.py:468
  149.1 3.7 %collective-permute-start.3 = (f32[1,2048]{1,0:T(1,128)S(1)}, f32[1,2048]{1,0:T(1,128)S(1)}, u32[]{:S(2)}, u32[]{:S(2)}) collective-permute-start(f32[1,2048]{1,0:T(1,128)S(1)} %add.113), channel_id=1, source_target_pairs={{0,2},{1,3},{2,0},{3,1},{4,6},{5,7},{6,4},{7,5},{8,10},{9,11},{10,... | collective-permute-start | bytes 24584 | tf_op jit(solution)/shard_map/ppermute | solution.py:416
  152.9 3.8 %collective-permute-start.4 = (f32[1,2048]{1,0:T(1,128)S(1)}, f32[1,2048]{1,0:T(1,128)S(1)}, u32[]{:S(2)}, u32[]{:S(2)}) collective-permute-start(f32[1,2048]{1,0:T(1,128)S(1)} %add.114), channel_id=1, source_target_pairs={{0,4},{1,5},{2,6},{3,7},{4,0},{5,1},{6,2},{7,3},{8,12},{9,13},{10,... | collective-permute-start | bytes 24584 | tf_op jit(solution)/shard_map/ppermute | solution.py:416
  167.1 1.8 collective-permute-start.11
  170.8 6.5 %collective-permute-start.12 = (bf16[4,128,128]{2,1,0:T(8,128)(2,1)}, bf16[4,128,128]{2,1,0:T(8,128)(2,1)}, u32[]{:S(2)}, u32[]{:S(2)}) collective-permute-start(bf16[4,128,128]{2,1,0:T(8,128)(2,1)} %get-tuple-element.134), channel_id=1, source_target_pairs={{0,2},{1,3},{2,0},{3,1},{4,6},{5,7},{6,4},{7,5},{8,10},{9,11},{10,... | collective-permute-start | bytes 393224 | tf_op jit(solution)/shard_map/ppermute | solution.py:468
  172.1 5.5 %collective-permute-start.13 = (bf16[4,128,128]{2,1,0:T(8,128)(2,1)}, bf16[4,128,128]{2,1,0:T(8,128)(2,1)S(1)}, u32[]{:S(2)}, u32[]{:S(2)}) collective-permute-start(bf16[4,128,128]{2,1,0:T(8,128)(2,1)} %get-tuple-element.133), channel_id=1, source_target_pairs={{0,4},{1,5},{2,6},{3,7},{4,0},{5,1},{6,2},{7,3},{8,12},{9,13},{10,... | collective-permute-start | bytes 393224 | tf_op jit(solution)/shard_map/ppermute | solution.py:468
  173.5 3.8 %collective-permute-start.14 = (f32[1,2048]{1,0:T(1,128)S(1)}, f32[1,2048]{1,0:T(1,128)S(1)}, u32[]{:S(2)}, u32[]{:S(2)}) collective-permute-start(f32[1,2048]{1,0:T(1,128)S(1)} %add.115), channel_id=1, source_target_pairs={{0,8},{1,9},{2,10},{3,11},{4,12},{5,13},{6,14},{7,15},{8,0},{9,1},... | collective-permute-start | bytes 24584 | tf_op jit(solution)/shard_map/ppermute | solution.py:416
  179.9 7.3 %collective-permute-start.16 = (bf16[4,128,128]{2,1,0:T(8,128)(2,1)}, bf16[4,128,128]{2,1,0:T(8,128)(2,1)S(1)}, u32[]{:S(2)}, u32[]{:S(2)}) collective-permute-start(bf16[4,128,128]{2,1,0:T(8,128)(2,1)} %fusion.24), channel_id=1, source_target_pairs={{0,2},{1,3},{2,0},{3,1},{4,6},{5,7},{6,4},{7,5},{8,10},{9,11},{10,... | collective-permute-start | bytes 393224 | tf_op jit(solution)/shard_map/ppermute | solution.py:468
  180.6 6.6 %collective-permute-start.15 = (bf16[4,128,128]{2,1,0:T(8,128)(2,1)}, bf16[4,128,128]{2,1,0:T(8,128)(2,1)S(1)}, u32[]{:S(2)}, u32[]{:S(2)}) collective-permute-start(bf16[4,128,128]{2,1,0:T(8,128)(2,1)} %convert_add_fusion.4), channel_id=1, source_target_pairs={{0,4},{1,5},{2,6},{3,7},{4,0},{5,1},{6,2},{7,3},{8,12},{9,13},{10,... | collective-permute-start | bytes 393224 | tf_op jit(solution)/shard_map/ppermute | solution.py:468
  181.7 5.4 %collective-permute-start.17 = (f32[1,2048]{1,0:T(1,128)S(1)}, f32[1,2048]{1,0:T(1,128)S(1)}, u32[]{:S(2)}, u32[]{:S(2)}) collective-permute-start(f32[1,2048]{1,0:T(1,128)S(1)} %add.124), channel_id=1, source_target_pairs={{0,16},{1,17},{2,18},{3,19},{4,20},{5,21},{6,22},{7,23},{8,24},{9,... | collective-permute-start | bytes 24584 | tf_op jit(solution)/shard_map/ppermute | solution.py:604
  189.0 1.5 collective-permute-start.18
  (17 other events, 122.3 us)

commit v5 on v4

--- a/solution.py
+++ b/solution.py
@@ -15,6 +15,7 @@
 AXES = ("grp", "seq")
 VMEM_LIMIT = 63 * 1024 * 1024
 CHUNK = 512
+WIDE = 1024
 
 NN = (((1,), (0,)), ((), ()))
 NT = (((1,), (1,)), ((), ()))
@@ -140,7 +141,7 @@
 
 def pack(pick, source, which, out=None):
     rows, width = pick.shape[0], source.shape[1]
-    step = 2 * CHUNK
+    step = WIDE
 
     def kernel(pick_hbm, source_hbm, _, out_hbm, pick_ref, source_ref, out_ref, sems):
         steps = width // step
@@ -184,12 +185,12 @@
 
 def streamed(work, name, scalar, ins, outs):
     width = max(x.shape[-1] for x in ins)
-    steps = width // CHUNK
-    group = CHUNK // HEAD
+    steps = width // WIDE
+    group = WIDE // HEAD
 
     def part(ref, j):
         if len(ref.shape) == 2:
-            return ref.at[:, j * CHUNK : (j + 1) * CHUNK]
+            return ref.at[:, j * WIDE : (j + 1) * WIDE]
         return ref.at[j * group : (j + 1) * group]
 
     def kernel(*refs):
@@ -240,21 +241,50 @@
     return lax.broadcasted_iota(jnp.int32, (tok, tok), 0), lax.broadcasted_iota(jnp.int32, (tok, tok), 1)
 
 
+def early_kernel(
+    parity_ref, q_hbm, k_hbm, v_hbm, mine_hbm, other_hbm, mix_hbm, q_ref, k_ref, v_ref, mine_ref, other_ref, mix_ref, sems
+):
+    pairs = [(k_hbm, k_ref), (v_hbm, v_ref), (q_hbm, q_ref)]
+    loads = [pltpu.make_async_copy(a, b, sems.at[i]) for i, (a, b) in enumerate(pairs)]
+    for load in loads:
+        load.start()
+    loads[0].wait()
+    loads[1].wait()
+    half = mine_ref.shape[0]
+    stores = []
+    sides = ((other_ref, other_hbm, (1 - parity_ref[0]) * half), (mine_ref, mine_hbm, parity_ref[0] * half))
+    for state_ref, state_hbm, first in sides:
+        for h in range(half):
+            at = pl.ds(pl.multiple_of((first + h) * HEAD, HEAD), HEAD)
+            state_ref[h] = mm(k_ref[:, at], v_ref[:, at], TN).astype(BF16)
+        stores.append(pltpu.make_async_copy(state_ref, state_hbm, sems.at[3 + len(stores)]))
+        stores[-1].start()
+    loads[2].wait()
+    row, col = triangle(q_ref.shape[0])
+    for h in range(2 * half):
+        at = slice(h * HEAD, (h + 1) * HEAD)
+        mix_ref[:, at] = jnp.where(row <= col, mm(k_ref[:, at], q_ref[:, at], NT), 0.0).astype(BF16)
+    stores.append(pltpu.make_async_copy(mix_ref, mix_hbm, sems.at[5]))
+    stores[-1].start()
+    for store in stores:
+        store.wait()
+
+
 def early(parity, queries, keys, values):
     tok, width = queries.shape
-    heads = width // HEAD
-
-    def work(parity_ref, h, at, ins, outs):
-        q_ref, k_ref, v_ref = ins
-        state_ref, mix_ref = outs
-        row, col = triangle(tok)
-        k = k_ref[:, at]
-        state_ref[lax.rem(h + parity_ref[0] * (heads // 2), heads)] = mm(k, v_ref[:, at], TN).astype(BF16)
-        mix_ref[:, at] = jnp.where(row <= col, mm(k, q_ref[:, at], NT), 0.0).astype(BF16)
-
-    states = jax.ShapeDtypeStruct((heads, HEAD, HEAD), BF16)
-    outs = [states, jax.ShapeDtypeStruct((tok, width), BF16)]
-    return streamed(work, "early_states", parity, [queries, keys, values], outs)
+    hbm = pl.BlockSpec(memory_space=pl.ANY)
+    shapes = [(width // HEAD // 2, HEAD, HEAD)] * 2 + [(tok, width)]
+    return pl.pallas_call(
+        early_kernel,
+        in_specs=[pl.BlockSpec(memory_space=pltpu.SMEM)] + [hbm] * 3,
+        out_specs=[hbm] * 3,
+        out_shape=[jax.ShapeDtypeStruct(shape, BF16) for shape in shapes],
+        scratch_shapes=[pltpu.VMEM(shape, BF16) for shape in [(tok, width)] * 3 + shapes]
+        + [pltpu.SemaphoreType.DMA((6,))],
+        compiler_params=params(),
+        cost_estimate=cost(1, 1),
+        name="early_states",
+    )(parity, queries, keys, values)
 
 
 def combine_kernel(
@@ -263,7 +293,7 @@
 ):
     width = stream_ref.shape[1]
     count = iter(range(sems.shape[0]))
-    pieces = [slice(j, j + CHUNK) for j in range(0, width, CHUNK)]
+    pieces = [slice(j, j + WIDE) for j in range(0, width, WIDE)]
 
     def copy(source, target):
         made = pltpu.make_async_copy(source, target, sems.at[next(count)])
@@ -319,7 +349,7 @@
         + [pltpu.VMEM((tok, width), F32)] * 2
         + [pltpu.VMEM(pick_t.shape, BF16), pltpu.VMEM((1, width), F32)]
         + [pltpu.VMEM((width // HEAD // 2, HEAD, HEAD), BF16)] * 2
-        + [pltpu.SemaphoreType.DMA((width // CHUNK + 8,))],
+        + [pltpu.SemaphoreType.DMA((width // WIDE + 8,))],
         compiler_params=params(),
         cost_estimate=cost(2 * tok * width * (back.shape[0] + HEAD), 2 * width * (back.shape[0] + 6 * tok)),
         name="combine_rows",
@@ -550,21 +580,18 @@
     own, far_out, q_early, k_early, v_early = lax.optimization_barrier(
         (own, far_out, queries, key_vectors, value_vectors)
     )
-    key_states, mix_b = early(parity, q_early, k_early, v_early)
+    key_mine, key_other, mix_b = early(parity, q_early, k_early, v_early)
     back, own_ggp, own_gup, own_hidden, own_router, own_gain = expert(
         side_array, slot_gates[0], own, w_gate, w_up, w_down
     )
-    far, back, key_states, mix_b = lax.optimization_barrier((far, back, key_states, mix_b))
+    far, back, key_mine, key_other, mix_b = lax.optimization_barrier((far, back, key_mine, key_other, mix_b))
     back, far_ggp, far_gup, far_hidden, far_router, far_gain = expert(
         1 - side_array, slot_gates[1], far, w_gate, w_up, w_down, back
     )
     returned = lax.all_to_all(back, AXES, split_axis=0, concat_axis=0, tiled=True)
 
-    heads = width // HEAD
     place = lax.axis_index("seq")
-    own_prior, other_prior, _ = states_beyond(
-        seq_count - 1 - place, key_states[: heads // 2], key_states[heads // 2 :], []
-    )
+    own_prior, other_prior, _ = states_beyond(seq_count - 1 - place, key_mine, key_other, [])
     is_low = parity[0] == 0
     prior = jnp.concatenate(
         [jnp.where(is_low, own_prior, other_prior), jnp.where(is_low, other_prior, own_prior)]

time: 195 us -> 193 us (0.990)
    pallas_call x4 -> x3, Pallas kernels: 14.1 us -> 9.98 us  [streamed(): pl.pallas_call(kernel, in_specs=[pl.BlockSpec(memory_space=pltpu.SMEM)] +...]
    pallas_call x0 -> x1, Pallas kernels: none -> 2.99 us  [early(): pl.pallas_call(early_kernel, in_specs=[pl.BlockSpec(memory_space=pltpu.SM...]
  transfers between devices with their start and end apart: 22 -> 22, of which waited for: 12 -> 13; matrix products, arithmetic and copies ran while one was open for 10% -> 10% of each run, Pallas kernels for 20% -> 20%
where the time goes in v5:
time: 193 us
  waiting for transfers between devices  79 us (41%)
  Pallas kernels  48.3 us (25%)
  starting transfers between devices  37.3 us (19%)
  other arithmetic  11.9 us (6%)
  matrix products  10.5 us (5%)
  local copies, waits for them, and re-layouts  4.47 us (2%)
    ppermute x1, waiting for transfers between devices, body(): far_cot = lax.ppermute(cotangent, AXES, swap)  26.2 us
    pallas_call x2, Pallas kernels, expert(): pl.pallas_call(expert_kernel, in_specs=[pl.BlockSpec(memory_space=pltpu.S...  17.6 us
    ppermute x12, waiting for transfers between devices, swap(): lax.ppermute(value.astype(BF16), 'seq', [(i, i ^ bit) for i in range(coun...  17.3 us
    all_to_all x2, waiting for transfers between devices, exchange(): lax.all_to_all(value, AXES, split_axis=0, concat_axis=0, tiled=True, axis...  16.9 us
    all_to_all x2, starting transfers between devices, exchange(): lax.all_to_all(value, AXES, split_axis=0, concat_axis=0, tiled=True, axis...  16.1 us
    ppermute x12, starting transfers between devices, swap(): lax.ppermute(value.astype(BF16), 'seq', [(i, i ^ bit) for i in range(coun...  11 us
    pallas_call x3, Pallas kernels, streamed(): pl.pallas_call(kernel, in_specs=[pl.BlockSpec(memory_space=pltpu.SMEM)] +...  9.98 us
    ppermute x1, waiting for transfers between devices, body(): far_inputs = lax.ppermute(inputs, AXES, swap)  7.86 us
  transfers between devices with their start and end apart: 22, of which 13 were waited for; matrix products, arithmetic and copies ran while one was open for 10% of the time, Pallas kernels for 20%

profile of v5, /device:TPU:0, one launch (start us, length us, event | category | flops | bytes accessed | tf_op | source)
XLA Modules:
  0.0 192.8 jit_solution(5714049150212175643)
XLA Ops:
  0.7 3.8 %prepare_rows.1 = (bf16[128,2048]{1,0:T(8,128)(2,1)}, bf16[256,4096]{1,0:T(8,128)(2,1)}) custom-call(s32[1]{0:T(128)} %bitcast.1.half_ref.first_ref, s32[1]{0:T(128)} %bitcast.2.device_ref, s32[32,256]{1,0:T(8,128)} %index_ref.1, f32[1,2048]{1,0:T(1,128)} %bitcast.35, bf16[128,2048]{1,0:T(8,128)(2,1)} %cot_hbm.3, bf16[128,2048]{1,0:T(8,128)(2,1)} %stream_hbm.3), custom_call_target="tpu_custom_call" | custom-call | flops 1 | bytes 1 | tf_op jit(solution)/shard_map/prepare_rows/pallas_call | solution.py:122
  4.5 6.3 %all-to-all-start.1 = ((bf16[16,16,4096]{2,1,0:T(8,128)(2,1)}), bf16[16,16,4096]{2,1,0:T(8,128)(2,1)}, u32[]{:S(2)}, u32[]{:S(2)}) async-start(bf16[16,16,4096]{2,1,0:T(8,128)(2,1)} %bitcast.32), calls=%async_computation.1 | async-start | bytes 4194304 | tf_op jit(solution)/shard_map/all_to_all | solution.py:558
  10.8 2.7 %collective-permute-start.1 = (bf16[128,2048]{1,0:T(8,128)(2,1)}, bf16[128,2048]{1,0:T(8,128)(2,1)S(1)}, u32[]{:S(2)}, u32[]{:S(2)}) collective-permute-start(bf16[128,2048]{1,0:T(8,128)(2,1)} %cot_hbm.3), channel_id=1, source_target_pairs={{0,16},{1,17},{2,18},{3,19},{4,20},{5,21},{6,22},{7,23},{8,24},{9,... | collective-permute-start | bytes 1572872 | tf_op jit(solution)/shard_map/ppermute | solution.py:562
  14.5 3.1 %pick_slots.3 = bf16[512,128]{1,0:T(8,128)(2,1)} custom-call(s32[1]{0:T(128)} %bitcast.2.device_ref, s32[32,256]{1,0:T(8,128)} %index_ref.1), custom_call_target="tpu_custom_call" | custom-call | flops 1 | bytes 1 | tf_op jit(solution)/shard_map/pick_slots/pallas_call | solution.py:62
  22.0 26.2 %collective-permute-done.1.source_hbm._ = bf16[128,2048]{1,0:T(8,128)(2,1)S(1)} collective-permute-done((bf16[128,2048]{1,0:T(8,128)(2,1)}, bf16[128,2048]{1,0:T(8,128)(2,1)S(1)}, u32[]{:S(2)}, u32[]{:S(2)}) %collective-permute-start.1) | collective-permute-done | bytes 524320 | tf_op jit(solution)/shard_map/ppermute | solution.py:562
  51.3 7.9 %collective-permute-done.source_hbm = bf16[128,2048]{1,0:T(8,128)(2,1)} collective-permute-done((bf16[128,2048]{1,0:T(8,128)(2,1)}, bf16[128,2048]{1,0:T(8,128)(2,1)}, u32[]{:S(2)}, u32[]{:S(2)}) %collective-permute-start) | collective-permute-done | bytes 524320 | tf_op jit(solution)/shard_map/ppermute | solution.py:563
  61.6 9.7 %all-to-all-start = ((bf16[16,16,4096]{2,1,0:T(8,128)(2,1)}), bf16[16,16,4096]{2,1,0:T(8,128)(2,1)}, u32[]{:S(2)}, u32[]{:S(2)}) async-start(bf16[16,16,4096]{2,1,0:T(8,128)(2,1)} %bitcast.31), calls=%async_computation | async-start | bytes 4194304 | tf_op jit(solution)/shard_map/all_to_all | solution.py:558
  71.9 3.0 %early_states.1 = (bf16[8,128,128]{2,1,0:T(8,128)(2,1)}, bf16[8,128,128]{2,1,0:T(8,128)(2,1)}, bf16[128,2048]{1,0:T(8,128)(2,1)}) custom-call(s32[1]{0:T(128)} %bitcast.parity_ref.refs_0_, bf16[128,2048]{1,0:T(8,128)(2,1)} %refs_1_.3, bf16[128,2048]{1,0:T(8,128)(2,1)} %refs_1_.5, bf16[128,2048]{1,0:T(8,128)(2,1)} %refs_2_.5), custom_call_target="tpu_custom_call" | custom-call | flops 1 | bytes 1 | tf_op jit(solution)/shard_map/early_states/pallas_call | solution.py:277
  75.0 8.8 %expert_rows.2 = (bf16[512,2048]{1,0:T(8,128)(2,1)}, bf16[256,768]{1,0:T(8,128)(2,1)}, bf16[256,768]{1,0:T(8,128)(2,1)}, bf16[256,768]{1,0:T(8,128)(2,1)}, f32[1,256]{1,0:T(1,128)}, /*index=5*/f32[1,2048]{1,0:T(1,128)}) custom-call(s32[1]{0:T(128)} %bitcast.1.half_ref.first_ref, f32[1,256]{1,0:T(1,128)} %get-tuple-element.143.gates_hbm._, ...), custom_call_target="tpu_custom_call" | custom-call | flops 4026531840 | bytes 12582912 | tf_op jit(solution)/shard_map/expert_rows/pallas_call | solution.py:428
  83.8 16.9 %all-to-all-done = bf16[16,16,4096]{2,1,0:T(8,128)(2,1)} async-done(((bf16[16,16,4096]{2,1,0:T(8,128)(2,1)}), bf16[16,16,4096]{2,1,0:T(8,128)(2,1)}, u32[]{:S(2)}, u32[]{:S(2)}) %all-to-all-start) | async-done | bytes 2097184 | tf_op jit(solution)/shard_map/all_to_all | solution.py:558
  100.7 8.8 %expert_rows.3 = (bf16[512,2048]{1,0:T(8,128)(2,1)}, bf16[256,768]{1,0:T(8,128)(2,1)}, bf16[256,768]{1,0:T(8,128)(2,1)}, bf16[256,768]{1,0:T(8,128)(2,1)}, f32[1,256]{1,0:T(1,128)}, /*index=5*/f32[1,2048]{1,0:T(1,128)}) custom-call(s32[1]{0:T(128)S(6)} %sub.26.first_ref, f32[1,256]{1,0:T(1,128)} %get-tuple-element.144.gates_hbm, ...), custom_call_target="tpu_custom_call", output_to_operand_aliasing={{0}: (6, {})} | custom-call | flops 4026531840 | bytes 12582912 | tf_op jit(solution)/shard_map/expert_rows/pallas_call | solution.py:428
  109.5 4.1 %all-to-all-start.2 = ((bf16[32,16,2048]{2,1,0:T(8,128)(2,1)}), bf16[32,16,2048]{2,1,0:T(8,128)(2,1)}, u32[]{:S(2)}, u32[]{:S(2)}) async-start(bf16[32,16,2048]{2,1,0:T(8,128)(2,1)} %bitcast.33), calls=%async_computation.2 | async-start | bytes 4194304 | tf_op jit(solution)/shard_map/all_to_all | solution.py:591
  113.7 2.8 %pad_maximum_fusion = bf16[512,4096]{1,0:T(8,128)(2,1)S(1)} fusion(bf16[256,4096]{1,0:T(8,128)(2,1)} %bitcast.14.in_hbm, bf16[256,4096]{1,0:T(8,128)(2,1)} %bitcast.17.in_hbm), kind=kLoop, calls=%fused_computation | loop fusion | flops 8388608 | bytes 8388608 | tf_op jit(solution)/shard_map/concatenate | solution.py:600
  120.2 3.5 %convolution_convert_fusion.1 = bf16[2048,768]{1,0:T(8,128)(2,1)} fusion(bf16[512,4096]{1,0:T(8,128)(2,1)S(1)} %pad_maximum_fusion, bf16[256,768]{1,0:T(8,128)(2,1)S(1)} %copy-done.16, bf16[256,768]{1,0:T(8,128)(2,1)S(1)} %copy-done.19), kind=kOutput, calls=%fused_computation.2 | convolution fusion | flops 1613758464 | bytes 6029312 | tf_op jit(solution)/shard_map/dot_general | solution.py:611
  123.7 8.5 %collective-permute-done.6 = bf16[4,128,128]{2,1,0:T(8,128)(2,1)S(1)} collective-permute-done((bf16[4,128,128]{2,1,0:T(8,128)(2,1)S(1)}, bf16[4,128,128]{2,1,0:T(8,128)(2,1)S(1)}, u32[]{:S(2)}, u32[]{:S(2)}) %collective-permute-start.6) | collective-permute-done | bytes 131104 | tf_op jit(solution)/shard_map/ppermute | solution.py:498
  133.0 3.5 %convolution_convert_fusion.2 = bf16[2048,768]{1,0:T(8,128)(2,1)} fusion(bf16[512,4096]{1,0:T(8,128)(2,1)S(1)} %pad_maximum_fusion, bf16[256,768]{1,0:T(8,128)(2,1)S(1)} %copy-done.15, bf16[256,768]{1,0:T(8,128)(2,1)S(1)} %copy-done.18), kind=kOutput, calls=%fused_computation.3 | convolution fusion | flops 1613758464 | bytes 6029312 | tf_op jit(solution)/shard_map/dot_general | solution.py:610
  140.9 3.8 %collective-permute-done.9 = bf16[4,128,128]{2,1,0:T(8,128)(2,1)S(1)} collective-permute-done((bf16[4,128,128]{2,1,0:T(8,128)(2,1)S(1)}, bf16[4,128,128]{2,1,0:T(8,128)(2,1)S(1)}, u32[]{:S(2)}, u32[]{:S(2)}) %collective-permute-start.9) | collective-permute-done | bytes 131104 | tf_op jit(solution)/shard_map/ppermute | solution.py:498
  144.9 3.5 %convolution_convert_fusion = bf16[768,2048]{1,0:T(8,128)(2,1)} fusion(bf16[512,4096]{1,0:T(8,128)(2,1)S(1)} %pad_maximum_fusion, bf16[256,768]{1,0:T(8,128)(2,1)S(1)} %copy-done.14, bf16[256,768]{1,0:T(8,128)(2,1)S(1)} %copy-done.17), kind=kOutput, calls=%fused_computation.1 | convolution fusion | flops 1613758464 | bytes 6029312 | tf_op jit(solution)/shard_map/dot_general | solution.py:612
  149.5 2.7 %collective-permute-done.3 = f32[1,2048]{1,0:T(1,128)S(1)} collective-permute-done((f32[1,2048]{1,0:T(1,128)S(1)}, f32[1,2048]{1,0:T(1,128)S(1)}, u32[]{:S(2)}, u32[]{:S(2)}) %collective-permute-start.3) | collective-permute-done | bytes 8224 | tf_op jit(solution)/shard_map/ppermute | solution.py:446
  157.0 5.4 %all-to-all-done.2 = bf16[32,16,2048]{2,1,0:T(8,128)(2,1)} async-done(((bf16[32,16,2048]{2,1,0:T(8,128)(2,1)}), bf16[32,16,2048]{2,1,0:T(8,128)(2,1)}, u32[]{:S(2)}, u32[]{:S(2)}) %all-to-all-start.2) | async-done | bytes 2097184 | tf_op jit(solution)/shard_map/all_to_all | solution.py:591
  162.4 3.7 %combine_rows.1 = (bf16[128,2048]{1,0:T(8,128)(2,1)}, bf16[8,128,128]{2,1,0:T(8,128)(2,1)}, bf16[8,128,128]{2,1,0:T(8,128)(2,1)}) custom-call(s32[1]{0:T(128)} %bitcast.parity_ref.refs_0_, bf16[128,512]{1,0:T(8,128)(2,1)} %bitcast.34, f32[1,2048]{1,0:T(1,128)} %bitcast.36, bf16[128,2048]{1,0:T(8,128)(2,1)} %stream_hbm.3, ...), custom_call_target="tpu_custom_call" | custom-call | flops 335544320 | bytes 5242880 | tf_op jit(solution)/shard_map/combine_rows/pallas_call | solution.py:341
  172.5 3.3 %local_attention.1 = (bf16[128,2048]{1,0:T(8,128)(2,1)}, bf16[128,2048]{1,0:T(8,128)(2,1)}) custom-call(s32[1]{0:T(128)} %bitcast.parity_ref.refs_0_, bf16[128,2048]{1,0:T(8,128)(2,1)} %refs_1_.3, bf16[128,2048]{1,0:T(8,128)(2,1)} %refs_2_.5, bf16[128,2048]{1,0:T(8,128)(2,1)} %get-tuple-element.116.refs_3_, bf16[128,2048]{1,0:T(8,128)(2,1)} %get-tuple-element.110.refs_4_), custom_call_target="tpu_custom_call" | custom-call | flops 1 | bytes 1 | tf_op jit(solution)/shard_map/local_attention/pallas_call | solution.py:227
  181.8 3.7 %query_attention.1 = bf16[128,2048]{1,0:T(8,128)(2,1)} custom-call(s32[1]{0:T(128)} %bitcast.parity_ref.refs_0_, bf16[128,2048]{1,0:T(8,128)(2,1)} %refs_1_.5, bf16[128,2048]{1,0:T(8,128)(2,1)} %refs_2_.5, bf16[128,2048]{1,0:T(8,128)(2,1)} %get-tuple-element.116.refs_3_, bf16[16,128,128]{2,1,0:T(8,128)(2,1)} %pad_maximum_fusion.2.refs_4_), custom_call_target="tpu_custom_call" | custom-call | flops 1 | bytes 1 | tf_op jit(solution)/shard_map/query_attention/pallas_call | solution.py:227
  189.6 3.0 %last_attention.1 = (bf16[128,2048]{1,0:T(8,128)(2,1)}, bf16[128,2048]{1,0:T(8,128)(2,1)}) custom-call(s32[1]{0:T(128)} %bitcast.parity_ref.refs_0_, bf16[128,2048]{1,0:T(8,128)(2,1)} %refs_1_.5, bf16[128,2048]{1,0:T(8,128)(2,1)} %refs_2_.5, bf16[128,2048]{1,0:T(8,128)(2,1)} %get-tuple-element.119.refs_3_, bf16[128,2048]{1,0:T(8,128)(2,1)} %get-tuple-element.120.refs_4_, ...), custom_call_target="tpu_custom_call" | custom-call | flops 1 | bytes 1 | tf_op jit(solution)/shard_map/last_attention/pallas_call | solution.py:227
  (107 shorter events, 42.8 us)
Async XLA Ops:
  0.7 21.2 %copy-start.10 = (f32[1,256]{1,0:T(1,128)S(1)}, f32[1,256]{1,0:T(1,128)}, u32[]{:S(2)}) copy-start(f32[1,256]{1,0:T(1,128)} %param.18) | copy-start | bytes 3076
  4.5 57.1 %all-to-all-start.1 = ((bf16[16,16,4096]{2,1,0:T(8,128)(2,1)}), bf16[16,16,4096]{2,1,0:T(8,128)(2,1)}, u32[]{:S(2)}, u32[]{:S(2)}) async-start(bf16[16,16,4096]{2,1,0:T(8,128)(2,1)} %bitcast.32), calls=%async_computation.1 | async-start | bytes 4194304 | tf_op jit(solution)/shard_map/all_to_all | solution.py:558
  10.8 37.3 %collective-permute-start.1 = (bf16[128,2048]{1,0:T(8,128)(2,1)}, bf16[128,2048]{1,0:T(8,128)(2,1)S(1)}, u32[]{:S(2)}, u32[]{:S(2)}) collective-permute-start(bf16[128,2048]{1,0:T(8,128)(2,1)} %cot_hbm.3), channel_id=1, source_target_pairs={{0,16},{1,17},{2,18},{3,19},{4,20},{5,21},{6,22},{7,23},{8,24},{9,... | collective-permute-start | bytes 1572872 | tf_op jit(solution)/shard_map/ppermute | solution.py:562
  13.5 45.7 %collective-permute-start = (bf16[128,2048]{1,0:T(8,128)(2,1)}, bf16[128,2048]{1,0:T(8,128)(2,1)}, u32[]{:S(2)}, u32[]{:S(2)}) collective-permute-start(bf16[128,2048]{1,0:T(8,128)(2,1)} %get-tuple-element.70), channel_id=1, source_target_pairs={{0,16},{1,17},{2,18},{3,19},{4,20},{5,21},{6,22},{7,23},{8,24},{9,... | collective-permute-start | bytes 1572872 | tf_op jit(solution)/shard_map/ppermute | solution.py:563
  61.6 39.1 %all-to-all-start = ((bf16[16,16,4096]{2,1,0:T(8,128)(2,1)}), bf16[16,16,4096]{2,1,0:T(8,128)(2,1)}, u32[]{:S(2)}, u32[]{:S(2)}) async-start(bf16[16,16,4096]{2,1,0:T(8,128)(2,1)} %bitcast.31), calls=%async_computation | async-start | bytes 4194304 | tf_op jit(solution)/shard_map/all_to_all | solution.py:558
  74.9 25.8 %copy-start.13 = (bf16[8,128,128]{2,1,0:T(8,128)(2,1)S(1)}, bf16[8,128,128]{2,1,0:T(8,128)(2,1)}, u32[]{:S(2)}) copy-start(bf16[8,128,128]{2,1,0:T(8,128)(2,1)} %get-tuple-element.104) | copy-start | bytes 786436
  100.7 16.1 %collective-permute-start.5 = (bf16[8,128,128]{2,1,0:T(8,128)(2,1)S(1)}, bf16[8,128,128]{2,1,0:T(8,128)(2,1)S(1)}, u32[]{:S(2)}, u32[]{:S(2)}) collective-permute-start(bf16[8,128,128]{2,1,0:T(8,128)(2,1)S(1)} %copy-done.13), channel_id=1, source_target_pairs={{0,1},{1,0},{2,3},{3,2},{4,5},{5,4},{6,7},{7,6},{8,9},{9,8},{10,11... | collective-permute-start | bytes 786440 | tf_op jit(solution)/shard_map/ppermute | solution.py:498
  109.5 52.9 %all-to-all-start.2 = ((bf16[32,16,2048]{2,1,0:T(8,128)(2,1)}), bf16[32,16,2048]{2,1,0:T(8,128)(2,1)}, u32[]{:S(2)}, u32[]{:S(2)}) async-start(bf16[32,16,2048]{2,1,0:T(8,128)(2,1)} %bitcast.33), calls=%async_computation.2 | async-start | bytes 4194304 | tf_op jit(solution)/shard_map/all_to_all | solution.py:591
  116.6 31.9 %collective-permute-start.2 = (f32[1,2048]{1,0:T(1,128)S(1)}, f32[1,2048]{1,0:T(1,128)S(1)}, u32[]{:S(2)}, u32[]{:S(2)}) collective-permute-start(f32[1,2048]{1,0:T(1,128)S(1)} %add_divide_fusion), channel_id=1, source_target_pairs={{0,1},{1,0},{2,3},{3,2},{4,5},{5,4},{6,7},{7,6},{8,9},{9,8},{10,11... | collective-permute-start | bytes 24584 | tf_op jit(solution)/shard_map/ppermute | solution.py:446
  117.0 15.2 %collective-permute-start.6 = (bf16[4,128,128]{2,1,0:T(8,128)(2,1)S(1)}, bf16[4,128,128]{2,1,0:T(8,128)(2,1)S(1)}, u32[]{:S(2)}, u32[]{:S(2)}) collective-permute-start(bf16[4,128,128]{2,1,0:T(8,128)(2,1)S(1)} %get-tuple-element.141), channel_id=1, source_target_pairs={{0,2},{1,3},{2,0},{3,1},{4,6},{5,7},{6,4},{7,5},{8,10},{9,11},{10,... | collective-permute-start | bytes 393224 | tf_op jit(solution)/shard_map/ppermute | solution.py:498
  118.7 13.5 %collective-permute-start.8 = (bf16[4,128,128]{2,1,0:T(8,128)(2,1)S(1)}, bf16[4,128,128]{2,1,0:T(8,128)(2,1)S(1)}, u32[]{:S(2)}, u32[]{:S(2)}) collective-permute-start(bf16[4,128,128]{2,1,0:T(8,128)(2,1)S(1)} %get-tuple-element.142), channel_id=1, source_target_pairs={{0,4},{1,5},{2,6},{3,7},{4,0},{5,1},{6,2},{7,3},{8,12},{9,13},{10,... | collective-permute-start | bytes 393224 | tf_op jit(solution)/shard_map/ppermute | solution.py:498
  132.3 8.6 %collective-permute-start.7 = (bf16[4,128,128]{2,1,0:T(8,128)(2,1)S(1)}, bf16[4,128,128]{2,1,0:T(8,128)(2,1)S(1)}, u32[]{:S(2)}, u32[]{:S(2)}) collective-permute-start(bf16[4,128,128]{2,1,0:T(8,128)(2,1)S(1)} %get-tuple-element.139), channel_id=1, source_target_pairs={{0,4},{1,5},{2,6},{3,7},{4,0},{5,1},{6,2},{7,3},{8,12},{9,13},{10,... | collective-permute-start | bytes 393224 | tf_op jit(solution)/shard_map/ppermute | solution.py:498
  136.6 8.1 %collective-permute-start.9 = (bf16[4,128,128]{2,1,0:T(8,128)(2,1)S(1)}, bf16[4,128,128]{2,1,0:T(8,128)(2,1)S(1)}, u32[]{:S(2)}, u32[]{:S(2)}) collective-permute-start(bf16[4,128,128]{2,1,0:T(8,128)(2,1)S(1)} %get-tuple-element.140), channel_id=1, source_target_pairs={{0,2},{1,3},{2,0},{3,1},{4,6},{5,7},{6,4},{7,5},{8,10},{9,11},{10,... | collective-permute-start | bytes 393224 | tf_op jit(solution)/shard_map/ppermute | solution.py:498
  144.8 11.2 %collective-permute-start.10 = (bf16[8,128,128]{2,1,0:T(8,128)(2,1)S(1)}, bf16[8,128,128]{2,1,0:T(8,128)(2,1)S(1)}, u32[]{:S(2)}, u32[]{:S(2)}) collective-permute-start(bf16[8,128,128]{2,1,0:T(8,128)(2,1)S(1)} %fusion.13), channel_id=1, source_target_pairs={{0,1},{1,0},{2,3},{3,2},{4,5},{5,4},{6,7},{7,6},{8,9},{9,8},{10,11... | collective-permute-start | bytes 786440 | tf_op jit(solution)/shard_map/ppermute | solution.py:498
  148.5 3.7 %collective-permute-start.3 = (f32[1,2048]{1,0:T(1,128)S(1)}, f32[1,2048]{1,0:T(1,128)S(1)}, u32[]{:S(2)}, u32[]{:S(2)}) collective-permute-start(f32[1,2048]{1,0:T(1,128)S(1)} %add.113), channel_id=1, source_target_pairs={{0,2},{1,3},{2,0},{3,1},{4,6},{5,7},{6,4},{7,5},{8,10},{9,11},{10,... | collective-permute-start | bytes 24584 | tf_op jit(solution)/shard_map/ppermute | solution.py:446
  152.2 3.8 %collective-permute-start.4 = (f32[1,2048]{1,0:T(1,128)S(1)}, f32[1,2048]{1,0:T(1,128)S(1)}, u32[]{:S(2)}, u32[]{:S(2)}) collective-permute-start(f32[1,2048]{1,0:T(1,128)S(1)} %add.114), channel_id=1, source_target_pairs={{0,4},{1,5},{2,6},{3,7},{4,0},{5,1},{6,2},{7,3},{8,12},{9,13},{10,... | collective-permute-start | bytes 24584 | tf_op jit(solution)/shard_map/ppermute | solution.py:446
  166.2 1.8 collective-permute-start.11
  169.8 6.4 %collective-permute-start.12 = (bf16[4,128,128]{2,1,0:T(8,128)(2,1)}, bf16[4,128,128]{2,1,0:T(8,128)(2,1)}, u32[]{:S(2)}, u32[]{:S(2)}) collective-permute-start(bf16[4,128,128]{2,1,0:T(8,128)(2,1)} %get-tuple-element.138), channel_id=1, source_target_pairs={{0,2},{1,3},{2,0},{3,1},{4,6},{5,7},{6,4},{7,5},{8,10},{9,11},{10,... | collective-permute-start | bytes 393224 | tf_op jit(solution)/shard_map/ppermute | solution.py:498
  171.1 5.5 %collective-permute-start.13 = (bf16[4,128,128]{2,1,0:T(8,128)(2,1)}, bf16[4,128,128]{2,1,0:T(8,128)(2,1)S(1)}, u32[]{:S(2)}, u32[]{:S(2)}) collective-permute-start(bf16[4,128,128]{2,1,0:T(8,128)(2,1)} %get-tuple-element.137), channel_id=1, source_target_pairs={{0,4},{1,5},{2,6},{3,7},{4,0},{5,1},{6,2},{7,3},{8,12},{9,13},{10,... | collective-permute-start | bytes 393224 | tf_op jit(solution)/shard_map/ppermute | solution.py:498
  172.5 3.7 %collective-permute-start.14 = (f32[1,2048]{1,0:T(1,128)S(1)}, f32[1,2048]{1,0:T(1,128)S(1)}, u32[]{:S(2)}, u32[]{:S(2)}) collective-permute-start(f32[1,2048]{1,0:T(1,128)S(1)} %add.115), channel_id=1, source_target_pairs={{0,8},{1,9},{2,10},{3,11},{4,12},{5,13},{6,14},{7,15},{8,0},{9,1},... | collective-permute-start | bytes 24584 | tf_op jit(solution)/shard_map/ppermute | solution.py:446
  178.9 6.6 %collective-permute-start.16 = (bf16[4,128,128]{2,1,0:T(8,128)(2,1)}, bf16[4,128,128]{2,1,0:T(8,128)(2,1)S(1)}, u32[]{:S(2)}, u32[]{:S(2)}) collective-permute-start(bf16[4,128,128]{2,1,0:T(8,128)(2,1)} %fusion.24), channel_id=1, source_target_pairs={{0,2},{1,3},{2,0},{3,1},{4,6},{5,7},{6,4},{7,5},{8,10},{9,11},{10,... | collective-permute-start | bytes 393224 | tf_op jit(solution)/shard_map/ppermute | solution.py:498
  179.6 5.9 %collective-permute-start.15 = (bf16[4,128,128]{2,1,0:T(8,128)(2,1)}, bf16[4,128,128]{2,1,0:T(8,128)(2,1)S(1)}, u32[]{:S(2)}, u32[]{:S(2)}) collective-permute-start(bf16[4,128,128]{2,1,0:T(8,128)(2,1)} %convert_add_fusion.4), channel_id=1, source_target_pairs={{0,4},{1,5},{2,6},{3,7},{4,0},{5,1},{6,2},{7,3},{8,12},{9,13},{10,... | collective-permute-start | bytes 393224 | tf_op jit(solution)/shard_map/ppermute | solution.py:498
  180.7 4.7 %collective-permute-start.17 = (f32[1,2048]{1,0:T(1,128)S(1)}, f32[1,2048]{1,0:T(1,128)S(1)}, u32[]{:S(2)}, u32[]{:S(2)}) collective-permute-start(f32[1,2048]{1,0:T(1,128)S(1)} %add.124), channel_id=1, source_target_pairs={{0,16},{1,17},{2,18},{3,19},{4,20},{5,21},{6,22},{7,23},{8,24},{9,... | collective-permute-start | bytes 24584 | tf_op jit(solution)/shard_map/ppermute | solution.py:631
  187.4 1.5 collective-permute-start.18
  (18 other events, 124.1 us)

commit v6 on v5

--- a/solution.py
+++ b/solution.py
@@ -71,15 +71,14 @@
     )(device, index)
 
 
-def send_rows(pick_ref, sources, out_hbm, out_ref, sems):
+def send_rows(pick_ref, source, first, out_hbm, out_ref, sems):
     copies = []
-    width = sources[0].shape[1]
-    for i, source in enumerate(sources):
-        for j in range(0, width, 2 * CHUNK):
-            at = slice(i * width + j, i * width + j + 2 * CHUNK)
-            out_ref[:, at] = mm(pick_ref[...], source[:, j : j + 2 * CHUNK]).astype(BF16)
-            copies.append(pltpu.make_async_copy(out_ref.at[:, at], out_hbm.at[:, at], sems.at[len(copies)]))
-            copies[-1].start()
+    width = source.shape[1]
+    for j in range(0, width, WIDE):
+        at = slice(first + j, first + j + WIDE)
+        out_ref[:, at] = mm(pick_ref[...], source[:, j : j + WIDE]).astype(BF16)
+        copies.append(pltpu.make_async_copy(out_ref.at[:, at], out_hbm.at[:, at], sems.at[(first + j) // WIDE]))
+        copies[-1].start()
     return copies
 
 
@@ -100,15 +99,16 @@
     index_in.wait()
     index = index_ref[...].astype(F32).T
     pick_ref[...] = one_hot_slots(most, device_ref[0], index, member_ref, *pick_ref.shape)
+    cot_in.wait()
+    copies = send_rows(pick_ref, cot_ref, cot_ref.shape[1], out_hbm, out_ref, sems)
     stream_in.wait()
     wide = stream_ref[...].astype(F32)
     inv = lax.rsqrt(jnp.mean(wide * wide, axis=1, keepdims=True) + EPS)
     gain_in.wait()
     x_ref[...] = (wide * inv * gain_ref[...]).astype(BF16)
-    cot_in.wait()
-    copies = send_rows(pick_ref, (x_ref, cot_ref), out_hbm, out_ref, sems)
     x_out = pltpu.make_async_copy(x_ref, x_hbm, edge_sems.at[2])
     x_out.start()
+    copies += send_rows(pick_ref, x_ref, 0, out_hbm, out_ref, sems)
     for part in copies + [x_out]:
         part.wait()
 

time: 193 us -> 194 us (level)
  no operation moved by 1% of the time
where the time goes in v6:
time: 194 us; the launch traced here: 193 us
  waiting for transfers between devices  79 us (41%)
  Pallas kernels  48.4 us (25%)
  starting transfers between devices  37.3 us (19%)
  other arithmetic  11.9 us (6%)
  matrix products  10.5 us (5%)
  local copies, waits for them, and re-layouts  4.47 us (2%)
    ppermute x1, waiting for transfers between devices, body(): far_cot = lax.ppermute(cotangent, AXES, swap)  26.2 us
    pallas_call x2, Pallas kernels, expert(): pl.pallas_call(expert_kernel, in_specs=[pl.BlockSpec(memory_space=pltpu.S...  17.6 us
    ppermute x12, waiting for transfers between devices, swap(): lax.ppermute(value.astype(BF16), 'seq', [(i, i ^ bit) for i in range(coun...  17.3 us
    all_to_all x2, waiting for transfers between devices, exchange(): lax.all_to_all(value, AXES, split_axis=0, concat_axis=0, tiled=True, axis...  16.9 us
    all_to_all x2, starting transfers between devices, exchange(): lax.all_to_all(value, AXES, split_axis=0, concat_axis=0, tiled=True, axis...  16 us
    ppermute x12, starting transfers between devices, swap(): lax.ppermute(value.astype(BF16), 'seq', [(i, i ^ bit) for i in range(coun...  11 us
    pallas_call x3, Pallas kernels, streamed(): pl.pallas_call(kernel, in_specs=[pl.BlockSpec(memory_space=pltpu.SMEM)] +...  9.98 us
    ppermute x1, waiting for transfers between devices, body(): far_inputs = lax.ppermute(inputs, AXES, swap)  7.86 us
  transfers between devices with their start and end apart: 22, of which 13 were waited for; matrix products, arithmetic and copies ran while one was open for 10% of the time, Pallas kernels for 20%

profile of v6, /device:TPU:0, one launch (start us, length us, event | category | flops | bytes accessed | tf_op | source)
XLA Modules:
  0.0 192.9 jit_solution(680777190349003715)
XLA Ops:
  0.7 3.8 %prepare_rows.1 = (bf16[128,2048]{1,0:T(8,128)(2,1)}, bf16[256,4096]{1,0:T(8,128)(2,1)}) custom-call(s32[1]{0:T(128)} %bitcast.1.half_ref.first_ref, s32[1]{0:T(128)} %bitcast.2.device_ref, s32[32,256]{1,0:T(8,128)} %index_ref.1, f32[1,2048]{1,0:T(1,128)} %bitcast.35, bf16[128,2048]{1,0:T(8,128)(2,1)} %cot_hbm.3, bf16[128,2048]{1,0:T(8,128)(2,1)} %stream_hbm.3), custom_call_target="tpu_custom_call" | custom-call | flops 1 | bytes 1 | tf_op jit(solution)/shard_map/prepare_rows/pallas_call | solution.py:122
  4.5 6.3 %all-to-all-start.1 = ((bf16[16,16,4096]{2,1,0:T(8,128)(2,1)}), bf16[16,16,4096]{2,1,0:T(8,128)(2,1)}, u32[]{:S(2)}, u32[]{:S(2)}) async-start(bf16[16,16,4096]{2,1,0:T(8,128)(2,1)} %bitcast.32), calls=%async_computation.1 | async-start | bytes 4194304 | tf_op jit(solution)/shard_map/all_to_all | solution.py:558
  10.9 2.7 %collective-permute-start.1 = (bf16[128,2048]{1,0:T(8,128)(2,1)}, bf16[128,2048]{1,0:T(8,128)(2,1)S(1)}, u32[]{:S(2)}, u32[]{:S(2)}) collective-permute-start(bf16[128,2048]{1,0:T(8,128)(2,1)} %cot_hbm.3), channel_id=1, source_target_pairs={{0,16},{1,17},{2,18},{3,19},{4,20},{5,21},{6,22},{7,23},{8,24},{9,... | collective-permute-start | bytes 1572872 | tf_op jit(solution)/shard_map/ppermute | solution.py:562
  14.5 3.1 %pick_slots.3 = bf16[512,128]{1,0:T(8,128)(2,1)} custom-call(s32[1]{0:T(128)} %bitcast.2.device_ref, s32[32,256]{1,0:T(8,128)} %index_ref.1), custom_call_target="tpu_custom_call" | custom-call | flops 1 | bytes 1 | tf_op jit(solution)/shard_map/pick_slots/pallas_call | solution.py:62
  22.1 26.2 %collective-permute-done.1.source_hbm._ = bf16[128,2048]{1,0:T(8,128)(2,1)S(1)} collective-permute-done((bf16[128,2048]{1,0:T(8,128)(2,1)}, bf16[128,2048]{1,0:T(8,128)(2,1)S(1)}, u32[]{:S(2)}, u32[]{:S(2)}) %collective-permute-start.1) | collective-permute-done | bytes 524320 | tf_op jit(solution)/shard_map/ppermute | solution.py:562
  51.4 7.9 %collective-permute-done.source_hbm = bf16[128,2048]{1,0:T(8,128)(2,1)} collective-permute-done((bf16[128,2048]{1,0:T(8,128)(2,1)}, bf16[128,2048]{1,0:T(8,128)(2,1)}, u32[]{:S(2)}, u32[]{:S(2)}) %collective-permute-start) | collective-permute-done | bytes 524320 | tf_op jit(solution)/shard_map/ppermute | solution.py:563
  61.7 9.7 %all-to-all-start = ((bf16[16,16,4096]{2,1,0:T(8,128)(2,1)}), bf16[16,16,4096]{2,1,0:T(8,128)(2,1)}, u32[]{:S(2)}, u32[]{:S(2)}) async-start(bf16[16,16,4096]{2,1,0:T(8,128)(2,1)} %bitcast.31), calls=%async_computation | async-start | bytes 4194304 | tf_op jit(solution)/shard_map/all_to_all | solution.py:558
  72.0 3.0 %early_states.1 = (bf16[8,128,128]{2,1,0:T(8,128)(2,1)}, bf16[8,128,128]{2,1,0:T(8,128)(2,1)}, bf16[128,2048]{1,0:T(8,128)(2,1)}) custom-call(s32[1]{0:T(128)} %bitcast.parity_ref.refs_0_, bf16[128,2048]{1,0:T(8,128)(2,1)} %refs_1_.3, bf16[128,2048]{1,0:T(8,128)(2,1)} %refs_1_.5, bf16[128,2048]{1,0:T(8,128)(2,1)} %refs_2_.5), custom_call_target="tpu_custom_call" | custom-call | flops 1 | bytes 1 | tf_op jit(solution)/shard_map/early_states/pallas_call | solution.py:277
  75.0 8.8 %expert_rows.2 = (bf16[512,2048]{1,0:T(8,128)(2,1)}, bf16[256,768]{1,0:T(8,128)(2,1)}, bf16[256,768]{1,0:T(8,128)(2,1)}, bf16[256,768]{1,0:T(8,128)(2,1)}, f32[1,256]{1,0:T(1,128)}, /*index=5*/f32[1,2048]{1,0:T(1,128)}) custom-call(s32[1]{0:T(128)} %bitcast.1.half_ref.first_ref, f32[1,256]{1,0:T(1,128)} %get-tuple-element.143.gates_hbm._, ...), custom_call_target="tpu_custom_call" | custom-call | flops 4026531840 | bytes 12582912 | tf_op jit(solution)/shard_map/expert_rows/pallas_call | solution.py:428
  83.8 16.9 %all-to-all-done = bf16[16,16,4096]{2,1,0:T(8,128)(2,1)} async-done(((bf16[16,16,4096]{2,1,0:T(8,128)(2,1)}), bf16[16,16,4096]{2,1,0:T(8,128)(2,1)}, u32[]{:S(2)}, u32[]{:S(2)}) %all-to-all-start) | async-done | bytes 2097184 | tf_op jit(solution)/shard_map/all_to_all | solution.py:558
  100.8 8.8 %expert_rows.3 = (bf16[512,2048]{1,0:T(8,128)(2,1)}, bf16[256,768]{1,0:T(8,128)(2,1)}, bf16[256,768]{1,0:T(8,128)(2,1)}, bf16[256,768]{1,0:T(8,128)(2,1)}, f32[1,256]{1,0:T(1,128)}, /*index=5*/f32[1,2048]{1,0:T(1,128)}) custom-call(s32[1]{0:T(128)S(6)} %sub.26.first_ref, f32[1,256]{1,0:T(1,128)} %get-tuple-element.144.gates_hbm, ...), custom_call_target="tpu_custom_call", output_to_operand_aliasing={{0}: (6, {})} | custom-call | flops 4026531840 | bytes 12582912 | tf_op jit(solution)/shard_map/expert_rows/pallas_call | solution.py:428
  109.6 4.1 %all-to-all-start.2 = ((bf16[32,16,2048]{2,1,0:T(8,128)(2,1)}), bf16[32,16,2048]{2,1,0:T(8,128)(2,1)}, u32[]{:S(2)}, u32[]{:S(2)}) async-start(bf16[32,16,2048]{2,1,0:T(8,128)(2,1)} %bitcast.33), calls=%async_computation.2 | async-start | bytes 4194304 | tf_op jit(solution)/shard_map/all_to_all | solution.py:591
  113.8 2.8 %pad_maximum_fusion = bf16[512,4096]{1,0:T(8,128)(2,1)S(1)} fusion(bf16[256,4096]{1,0:T(8,128)(2,1)} %bitcast.14.in_hbm, bf16[256,4096]{1,0:T(8,128)(2,1)} %bitcast.17.in_hbm), kind=kLoop, calls=%fused_computation | loop fusion | flops 8388608 | bytes 8388608 | tf_op jit(solution)/shard_map/concatenate | solution.py:600
  120.2 3.5 %convolution_convert_fusion.1 = bf16[2048,768]{1,0:T(8,128)(2,1)} fusion(bf16[512,4096]{1,0:T(8,128)(2,1)S(1)} %pad_maximum_fusion, bf16[256,768]{1,0:T(8,128)(2,1)S(1)} %copy-done.16, bf16[256,768]{1,0:T(8,128)(2,1)S(1)} %copy-done.19), kind=kOutput, calls=%fused_computation.2 | convolution fusion | flops 1613758464 | bytes 6029312 | tf_op jit(solution)/shard_map/dot_general | solution.py:611
  123.8 8.5 %collective-permute-done.6 = bf16[4,128,128]{2,1,0:T(8,128)(2,1)S(1)} collective-permute-done((bf16[4,128,128]{2,1,0:T(8,128)(2,1)S(1)}, bf16[4,128,128]{2,1,0:T(8,128)(2,1)S(1)}, u32[]{:S(2)}, u32[]{:S(2)}) %collective-permute-start.6) | collective-permute-done | bytes 131104 | tf_op jit(solution)/shard_map/ppermute | solution.py:498
  133.1 3.5 %convolution_convert_fusion.2 = bf16[2048,768]{1,0:T(8,128)(2,1)} fusion(bf16[512,4096]{1,0:T(8,128)(2,1)S(1)} %pad_maximum_fusion, bf16[256,768]{1,0:T(8,128)(2,1)S(1)} %copy-done.15, bf16[256,768]{1,0:T(8,128)(2,1)S(1)} %copy-done.18), kind=kOutput, calls=%fused_computation.3 | convolution fusion | flops 1613758464 | bytes 6029312 | tf_op jit(solution)/shard_map/dot_general | solution.py:610
  141.0 3.8 %collective-permute-done.9 = bf16[4,128,128]{2,1,0:T(8,128)(2,1)S(1)} collective-permute-done((bf16[4,128,128]{2,1,0:T(8,128)(2,1)S(1)}, bf16[4,128,128]{2,1,0:T(8,128)(2,1)S(1)}, u32[]{:S(2)}, u32[]{:S(2)}) %collective-permute-start.9) | collective-permute-done | bytes 131104 | tf_op jit(solution)/shard_map/ppermute | solution.py:498
  145.0 3.5 %convolution_convert_fusion = bf16[768,2048]{1,0:T(8,128)(2,1)} fusion(bf16[512,4096]{1,0:T(8,128)(2,1)S(1)} %pad_maximum_fusion, bf16[256,768]{1,0:T(8,128)(2,1)S(1)} %copy-done.14, bf16[256,768]{1,0:T(8,128)(2,1)S(1)} %copy-done.17), kind=kOutput, calls=%fused_computation.1 | convolution fusion | flops 1613758464 | bytes 6029312 | tf_op jit(solution)/shard_map/dot_general | solution.py:612
  149.6 2.7 %collective-permute-done.3 = f32[1,2048]{1,0:T(1,128)S(1)} collective-permute-done((f32[1,2048]{1,0:T(1,128)S(1)}, f32[1,2048]{1,0:T(1,128)S(1)}, u32[]{:S(2)}, u32[]{:S(2)}) %collective-permute-start.3) | collective-permute-done | bytes 8224 | tf_op jit(solution)/shard_map/ppermute | solution.py:446
  157.1 5.4 %all-to-all-done.2 = bf16[32,16,2048]{2,1,0:T(8,128)(2,1)} async-done(((bf16[32,16,2048]{2,1,0:T(8,128)(2,1)}), bf16[32,16,2048]{2,1,0:T(8,128)(2,1)}, u32[]{:S(2)}, u32[]{:S(2)}) %all-to-all-start.2) | async-done | bytes 2097184 | tf_op jit(solution)/shard_map/all_to_all | solution.py:591
  162.5 3.7 %combine_rows.1 = (bf16[128,2048]{1,0:T(8,128)(2,1)}, bf16[8,128,128]{2,1,0:T(8,128)(2,1)}, bf16[8,128,128]{2,1,0:T(8,128)(2,1)}) custom-call(s32[1]{0:T(128)} %bitcast.parity_ref.refs_0_, bf16[128,512]{1,0:T(8,128)(2,1)} %bitcast.34, f32[1,2048]{1,0:T(1,128)} %bitcast.36, bf16[128,2048]{1,0:T(8,128)(2,1)} %stream_hbm.3, ...), custom_call_target="tpu_custom_call" | custom-call | flops 335544320 | bytes 5242880 | tf_op jit(solution)/shard_map/combine_rows/pallas_call | solution.py:341
  172.6 3.3 %local_attention.1 = (bf16[128,2048]{1,0:T(8,128)(2,1)}, bf16[128,2048]{1,0:T(8,128)(2,1)}) custom-call(s32[1]{0:T(128)} %bitcast.parity_ref.refs_0_, bf16[128,2048]{1,0:T(8,128)(2,1)} %refs_1_.3, bf16[128,2048]{1,0:T(8,128)(2,1)} %refs_2_.5, bf16[128,2048]{1,0:T(8,128)(2,1)} %get-tuple-element.116.refs_3_, bf16[128,2048]{1,0:T(8,128)(2,1)} %get-tuple-element.110.refs_4_), custom_call_target="tpu_custom_call" | custom-call | flops 1 | bytes 1 | tf_op jit(solution)/shard_map/local_attention/pallas_call | solution.py:227
  181.9 3.7 %query_attention.1 = bf16[128,2048]{1,0:T(8,128)(2,1)} custom-call(s32[1]{0:T(128)} %bitcast.parity_ref.refs_0_, bf16[128,2048]{1,0:T(8,128)(2,1)} %refs_1_.5, bf16[128,2048]{1,0:T(8,128)(2,1)} %refs_2_.5, bf16[128,2048]{1,0:T(8,128)(2,1)} %get-tuple-element.116.refs_3_, bf16[16,128,128]{2,1,0:T(8,128)(2,1)} %pad_maximum_fusion.2.refs_4_), custom_call_target="tpu_custom_call" | custom-call | flops 1 | bytes 1 | tf_op jit(solution)/shard_map/query_attention/pallas_call | solution.py:227
  189.7 3.0 %last_attention.1 = (bf16[128,2048]{1,0:T(8,128)(2,1)}, bf16[128,2048]{1,0:T(8,128)(2,1)}) custom-call(s32[1]{0:T(128)} %bitcast.parity_ref.refs_0_, bf16[128,2048]{1,0:T(8,128)(2,1)} %refs_1_.5, bf16[128,2048]{1,0:T(8,128)(2,1)} %refs_2_.5, bf16[128,2048]{1,0:T(8,128)(2,1)} %get-tuple-element.119.refs_3_, bf16[128,2048]{1,0:T(8,128)(2,1)} %get-tuple-element.120.refs_4_, ...), custom_call_target="tpu_custom_call" | custom-call | flops 1 | bytes 1 | tf_op jit(solution)/shard_map/last_attention/pallas_call | solution.py:227
  (107 shorter events, 42.8 us)
Async XLA Ops:
  0.7 21.2 %copy-start.10 = (f32[1,256]{1,0:T(1,128)S(1)}, f32[1,256]{1,0:T(1,128)}, u32[]{:S(2)}) copy-start(f32[1,256]{1,0:T(1,128)} %param.18) | copy-start | bytes 3076
  4.5 57.1 %all-to-all-start.1 = ((bf16[16,16,4096]{2,1,0:T(8,128)(2,1)}), bf16[16,16,4096]{2,1,0:T(8,128)(2,1)}, u32[]{:S(2)}, u32[]{:S(2)}) async-start(bf16[16,16,4096]{2,1,0:T(8,128)(2,1)} %bitcast.32), calls=%async_computation.1 | async-start | bytes 4194304 | tf_op jit(solution)/shard_map/all_to_all | solution.py:558
  10.9 37.3 %collective-permute-start.1 = (bf16[128,2048]{1,0:T(8,128)(2,1)}, bf16[128,2048]{1,0:T(8,128)(2,1)S(1)}, u32[]{:S(2)}, u32[]{:S(2)}) collective-permute-start(bf16[128,2048]{1,0:T(8,128)(2,1)} %cot_hbm.3), channel_id=1, source_target_pairs={{0,16},{1,17},{2,18},{3,19},{4,20},{5,21},{6,22},{7,23},{8,24},{9,... | collective-permute-start | bytes 1572872 | tf_op jit(solution)/shard_map/ppermute | solution.py:562
  13.6 45.7 %collective-permute-start = (bf16[128,2048]{1,0:T(8,128)(2,1)}, bf16[128,2048]{1,0:T(8,128)(2,1)}, u32[]{:S(2)}, u32[]{:S(2)}) collective-permute-start(bf16[128,2048]{1,0:T(8,128)(2,1)} %get-tuple-element.70), channel_id=1, source_target_pairs={{0,16},{1,17},{2,18},{3,19},{4,20},{5,21},{6,22},{7,23},{8,24},{9,... | collective-permute-start | bytes 1572872 | tf_op jit(solution)/shard_map/ppermute | solution.py:563
  61.7 39.1 %all-to-all-start = ((bf16[16,16,4096]{2,1,0:T(8,128)(2,1)}), bf16[16,16,4096]{2,1,0:T(8,128)(2,1)}, u32[]{:S(2)}, u32[]{:S(2)}) async-start(bf16[16,16,4096]{2,1,0:T(8,128)(2,1)} %bitcast.31), calls=%async_computation | async-start | bytes 4194304 | tf_op jit(solution)/shard_map/all_to_all | solution.py:558
  75.0 25.8 %copy-start.13 = (bf16[8,128,128]{2,1,0:T(8,128)(2,1)S(1)}, bf16[8,128,128]{2,1,0:T(8,128)(2,1)}, u32[]{:S(2)}) copy-start(bf16[8,128,128]{2,1,0:T(8,128)(2,1)} %get-tuple-element.104) | copy-start | bytes 786436
  100.8 16.1 %collective-permute-start.5 = (bf16[8,128,128]{2,1,0:T(8,128)(2,1)S(1)}, bf16[8,128,128]{2,1,0:T(8,128)(2,1)S(1)}, u32[]{:S(2)}, u32[]{:S(2)}) collective-permute-start(bf16[8,128,128]{2,1,0:T(8,128)(2,1)S(1)} %copy-done.13), channel_id=1, source_target_pairs={{0,1},{1,0},{2,3},{3,2},{4,5},{5,4},{6,7},{7,6},{8,9},{9,8},{10,11... | collective-permute-start | bytes 786440 | tf_op jit(solution)/shard_map/ppermute | solution.py:498
  109.6 52.9 %all-to-all-start.2 = ((bf16[32,16,2048]{2,1,0:T(8,128)(2,1)}), bf16[32,16,2048]{2,1,0:T(8,128)(2,1)}, u32[]{:S(2)}, u32[]{:S(2)}) async-start(bf16[32,16,2048]{2,1,0:T(8,128)(2,1)} %bitcast.33), calls=%async_computation.2 | async-start | bytes 4194304 | tf_op jit(solution)/shard_map/all_to_all | solution.py:591
  116.7 31.9 %collective-permute-start.2 = (f32[1,2048]{1,0:T(1,128)S(1)}, f32[1,2048]{1,0:T(1,128)S(1)}, u32[]{:S(2)}, u32[]{:S(2)}) collective-permute-start(f32[1,2048]{1,0:T(1,128)S(1)} %add_divide_fusion), channel_id=1, source_target_pairs={{0,1},{1,0},{2,3},{3,2},{4,5},{5,4},{6,7},{7,6},{8,9},{9,8},{10,11... | collective-permute-start | bytes 24584 | tf_op jit(solution)/shard_map/ppermute | solution.py:446
  117.0 15.2 %collective-permute-start.6 = (bf16[4,128,128]{2,1,0:T(8,128)(2,1)S(1)}, bf16[4,128,128]{2,1,0:T(8,128)(2,1)S(1)}, u32[]{:S(2)}, u32[]{:S(2)}) collective-permute-start(bf16[4,128,128]{2,1,0:T(8,128)(2,1)S(1)} %get-tuple-element.141), channel_id=1, source_target_pairs={{0,2},{1,3},{2,0},{3,1},{4,6},{5,7},{6,4},{7,5},{8,10},{9,11},{10,... | collective-permute-start | bytes 393224 | tf_op jit(solution)/shard_map/ppermute | solution.py:498
  118.8 13.5 %collective-permute-start.8 = (bf16[4,128,128]{2,1,0:T(8,128)(2,1)S(1)}, bf16[4,128,128]{2,1,0:T(8,128)(2,1)S(1)}, u32[]{:S(2)}, u32[]{:S(2)}) collective-permute-start(bf16[4,128,128]{2,1,0:T(8,128)(2,1)S(1)} %get-tuple-element.142), channel_id=1, source_target_pairs={{0,4},{1,5},{2,6},{3,7},{4,0},{5,1},{6,2},{7,3},{8,12},{9,13},{10,... | collective-permute-start | bytes 393224 | tf_op jit(solution)/shard_map/ppermute | solution.py:498
  132.3 8.6 %collective-permute-start.7 = (bf16[4,128,128]{2,1,0:T(8,128)(2,1)S(1)}, bf16[4,128,128]{2,1,0:T(8,128)(2,1)S(1)}, u32[]{:S(2)}, u32[]{:S(2)}) collective-permute-start(bf16[4,128,128]{2,1,0:T(8,128)(2,1)S(1)} %get-tuple-element.139), channel_id=1, source_target_pairs={{0,4},{1,5},{2,6},{3,7},{4,0},{5,1},{6,2},{7,3},{8,12},{9,13},{10,... | collective-permute-start | bytes 393224 | tf_op jit(solution)/shard_map/ppermute | solution.py:498
  136.6 8.1 %collective-permute-start.9 = (bf16[4,128,128]{2,1,0:T(8,128)(2,1)S(1)}, bf16[4,128,128]{2,1,0:T(8,128)(2,1)S(1)}, u32[]{:S(2)}, u32[]{:S(2)}) collective-permute-start(bf16[4,128,128]{2,1,0:T(8,128)(2,1)S(1)} %get-tuple-element.140), channel_id=1, source_target_pairs={{0,2},{1,3},{2,0},{3,1},{4,6},{5,7},{6,4},{7,5},{8,10},{9,11},{10,... | collective-permute-start | bytes 393224 | tf_op jit(solution)/shard_map/ppermute | solution.py:498
  144.9 11.2 %collective-permute-start.10 = (bf16[8,128,128]{2,1,0:T(8,128)(2,1)S(1)}, bf16[8,128,128]{2,1,0:T(8,128)(2,1)S(1)}, u32[]{:S(2)}, u32[]{:S(2)}) collective-permute-start(bf16[8,128,128]{2,1,0:T(8,128)(2,1)S(1)} %fusion.13), channel_id=1, source_target_pairs={{0,1},{1,0},{2,3},{3,2},{4,5},{5,4},{6,7},{7,6},{8,9},{9,8},{10,11... | collective-permute-start | bytes 786440 | tf_op jit(solution)/shard_map/ppermute | solution.py:498
  148.5 3.7 %collective-permute-start.3 = (f32[1,2048]{1,0:T(1,128)S(1)}, f32[1,2048]{1,0:T(1,128)S(1)}, u32[]{:S(2)}, u32[]{:S(2)}) collective-permute-start(f32[1,2048]{1,0:T(1,128)S(1)} %add.113), channel_id=1, source_target_pairs={{0,2},{1,3},{2,0},{3,1},{4,6},{5,7},{6,4},{7,5},{8,10},{9,11},{10,... | collective-permute-start | bytes 24584 | tf_op jit(solution)/shard_map/ppermute | solution.py:446
  152.3 3.8 %collective-permute-start.4 = (f32[1,2048]{1,0:T(1,128)S(1)}, f32[1,2048]{1,0:T(1,128)S(1)}, u32[]{:S(2)}, u32[]{:S(2)}) collective-permute-start(f32[1,2048]{1,0:T(1,128)S(1)} %add.114), channel_id=1, source_target_pairs={{0,4},{1,5},{2,6},{3,7},{4,0},{5,1},{6,2},{7,3},{8,12},{9,13},{10,... | collective-permute-start | bytes 24584 | tf_op jit(solution)/shard_map/ppermute | solution.py:446
  166.2 1.8 collective-permute-start.11
  169.9 6.4 %collective-permute-start.12 = (bf16[4,128,128]{2,1,0:T(8,128)(2,1)}, bf16[4,128,128]{2,1,0:T(8,128)(2,1)}, u32[]{:S(2)}, u32[]{:S(2)}) collective-permute-start(bf16[4,128,128]{2,1,0:T(8,128)(2,1)} %get-tuple-element.138), channel_id=1, source_target_pairs={{0,2},{1,3},{2,0},{3,1},{4,6},{5,7},{6,4},{7,5},{8,10},{9,11},{10,... | collective-permute-start | bytes 393224 | tf_op jit(solution)/shard_map/ppermute | solution.py:498
  171.2 5.5 %collective-permute-start.13 = (bf16[4,128,128]{2,1,0:T(8,128)(2,1)}, bf16[4,128,128]{2,1,0:T(8,128)(2,1)S(1)}, u32[]{:S(2)}, u32[]{:S(2)}) collective-permute-start(bf16[4,128,128]{2,1,0:T(8,128)(2,1)} %get-tuple-element.137), channel_id=1, source_target_pairs={{0,4},{1,5},{2,6},{3,7},{4,0},{5,1},{6,2},{7,3},{8,12},{9,13},{10,... | collective-permute-start | bytes 393224 | tf_op jit(solution)/shard_map/ppermute | solution.py:498
  172.6 3.7 %collective-permute-start.14 = (f32[1,2048]{1,0:T(1,128)S(1)}, f32[1,2048]{1,0:T(1,128)S(1)}, u32[]{:S(2)}, u32[]{:S(2)}) collective-permute-start(f32[1,2048]{1,0:T(1,128)S(1)} %add.115), channel_id=1, source_target_pairs={{0,8},{1,9},{2,10},{3,11},{4,12},{5,13},{6,14},{7,15},{8,0},{9,1},... | collective-permute-start | bytes 24584 | tf_op jit(solution)/shard_map/ppermute | solution.py:446
  178.9 6.6 %collective-permute-start.16 = (bf16[4,128,128]{2,1,0:T(8,128)(2,1)}, bf16[4,128,128]{2,1,0:T(8,128)(2,1)S(1)}, u32[]{:S(2)}, u32[]{:S(2)}) collective-permute-start(bf16[4,128,128]{2,1,0:T(8,128)(2,1)} %fusion.24), channel_id=1, source_target_pairs={{0,2},{1,3},{2,0},{3,1},{4,6},{5,7},{6,4},{7,5},{8,10},{9,11},{10,... | collective-permute-start | bytes 393224 | tf_op jit(solution)/shard_map/ppermute | solution.py:498
  179.7 5.9 %collective-permute-start.15 = (bf16[4,128,128]{2,1,0:T(8,128)(2,1)}, bf16[4,128,128]{2,1,0:T(8,128)(2,1)S(1)}, u32[]{:S(2)}, u32[]{:S(2)}) collective-permute-start(bf16[4,128,128]{2,1,0:T(8,128)(2,1)} %convert_add_fusion.4), channel_id=1, source_target_pairs={{0,4},{1,5},{2,6},{3,7},{4,0},{5,1},{6,2},{7,3},{8,12},{9,13},{10,... | collective-permute-start | bytes 393224 | tf_op jit(solution)/shard_map/ppermute | solution.py:498
  180.8 4.7 %collective-permute-start.17 = (f32[1,2048]{1,0:T(1,128)S(1)}, f32[1,2048]{1,0:T(1,128)S(1)}, u32[]{:S(2)}, u32[]{:S(2)}) collective-permute-start(f32[1,2048]{1,0:T(1,128)S(1)} %add.124), channel_id=1, source_target_pairs={{0,16},{1,17},{2,18},{3,19},{4,20},{5,21},{6,22},{7,23},{8,24},{9,... | collective-permute-start | bytes 24584 | tf_op jit(solution)/shard_map/ppermute | solution.py:631
  187.5 1.5 collective-permute-start.18
  (18 other events, 124.2 us)
